TPU v7x, 32 devices: a whole 2x2x4 slice. The times are simulated.
32 devices in a mesh: seq: 8 (over z, x), sub: 4 (over y, core).
Axes of the slice: x: 2, y: 2, z: 4, core: 2. Of those that a mesh axis runs over, the one named last changes fastest.
Arguments:
- features: bfloat16 [32768, 768], P(('seq', 'sub')), may hold values from -6 to 6
- kernel: bfloat16 [3, 768, 384], replicated, may hold values from -0.125 to 0.125
- offsets: float32 [384], replicated, may hold values from -3 to 3
- mixer: bfloat16 [384, 768], replicated, may hold values from -0.3125 to 0.3125
- biases: float32 [768], replicated, may hold values from -3 to 3
- cotangent: bfloat16 [32768, 768], P(('seq', 'sub')), may hold values from -6 to 6
Outputs:
- layer_output: bfloat16 [32768, 768], P(('seq', 'sub'))
- input_grad: bfloat16 [32768, 768], P(('seq', 'sub'))
- kernel_grad: float32 [3, 768, 384], replicated
- offset_grad: float32 [384], replicated
- mixer_grad: float32 [384, 768], replicated
- biases_grad: float32 [768], replicated
All inputs are finite; a program needn't handle non-finite values.
Results may differ from a plain program's by a relative error of at most 0.0075.
Values may be sent and summed in bfloat16 or wider, within the bound.
No kernel may reach another device: no remote copies, remote signals or barrier semaphores. Data moves between devices by JAX's collectives and lax.ppermute only.
A program may use at most 64 MiB of HBM per device.

v0:
```python
import math

import jax
import jax.numpy as jnp
from jax import lax
from jax.sharding import PartitionSpec as P

DILATION_STEP = 8192


def from_behind(value, axis, steps):
    count = lax.axis_size(axis)
    pairs = [(source, (source + steps) % count) for source in range(count)]
    return lax.ppermute(value, axis, pairs)


def gelu_exact(values):
    return jax.nn.gelu(values, approximate=False)


def gelu_slope(values):
    normal_cdf = 0.5 * (1.0 + jax.scipy.special.erf(values / math.sqrt(2.0)))
    return normal_cdf + values * jnp.exp(-0.5 * values * values) / math.sqrt(2.0 * math.pi)


def contract_rows(left, right):
    return lax.dot_general(
        left, right, (((0,), (0,)), ((), ())), preferred_element_type=jnp.float32
    )


def times_transposed(left, right):
    return lax.dot_general(
        left, right, (((1,), (1,)), ((), ())), preferred_element_type=jnp.float32
    )


def local(features, kernel, offsets, mixer, biases, cotangent):
    partition_rows = features.shape[0]
    offset_distance = DILATION_STEP // (partition_rows * lax.axis_size("sub"))
    factor = 1.0 / math.sqrt(partition_rows * lax.axis_size("seq") * lax.axis_size("sub"))
    inputs = features.astype(jnp.float32)
    activated_output = gelu_exact(inputs).astype(jnp.bfloat16)
    behind_neighbor = from_behind(activated_output, "seq", offset_distance)
    ahead_neighbor = from_behind(activated_output, "seq", -offset_distance)
    tap_early = jnp.dot(behind_neighbor, kernel[0], preferred_element_type=jnp.float32).astype(
        jnp.bfloat16
    )
    tap_late = jnp.dot(ahead_neighbor, kernel[2], preferred_element_type=jnp.float32).astype(
        jnp.bfloat16
    )
    preact = (
        jnp.dot(activated_output, kernel[1], preferred_element_type=jnp.float32)
        + tap_early.astype(jnp.float32)
        + tap_late.astype(jnp.float32)
        + offsets
    )
    hidden = gelu_exact(preact).astype(jnp.bfloat16)
    layer_output = (
        inputs + jnp.dot(hidden, mixer, preferred_element_type=jnp.float32) + biases
    ).astype(jnp.bfloat16)
    cot_float = cotangent.astype(jnp.float32)
    mixer_part = contract_rows(hidden, cotangent) * factor
    biases_part = jnp.sum(cot_float, axis=0) * factor
    hidden_grad = times_transposed(cotangent, mixer)
    preactivation_grad = (hidden_grad * gelu_slope(preact)).astype(jnp.bfloat16)
    grad_later = from_behind(preactivation_grad, "seq", -offset_distance)
    grad_earlier = from_behind(preactivation_grad, "seq", offset_distance)
    kernel_part = (
        jnp.stack(
            [
                contract_rows(behind_neighbor, preactivation_grad),
                contract_rows(activated_output, preactivation_grad),
                contract_rows(ahead_neighbor, preactivation_grad),
            ]
        )
        * factor
    )
    offset_part = jnp.sum(preactivation_grad.astype(jnp.float32), axis=0) * factor
    activated_output_grad = (
        times_transposed(preactivation_grad, kernel[1])
        + times_transposed(grad_later, kernel[0])
        + times_transposed(grad_earlier, kernel[2])
    )
    input_grad = (cot_float + activated_output_grad * gelu_slope(inputs)).astype(jnp.bfloat16)
    kernel_grad, offset_grad, mixer_grad, biases_grad = lax.psum(
        (kernel_part, offset_part, mixer_part, biases_part), ("seq", "sub")
    )
    return (layer_output, input_grad, kernel_grad, offset_grad, mixer_grad, biases_grad)


def solution(mesh):
    placed = (P(("seq", "sub"), None), P(), P(), P(), P(), P(("seq", "sub"), None))
    return jax.shard_map(
        local,
        mesh=mesh,
        in_specs=placed,
        out_specs=(P(("seq", "sub"), None), P(("seq", "sub"), None), P(), P(), P(), P()),
        check_vma=False,
    )
```

profile of v0, /device:TPU:0, one launch (start us, length us, event | category | flops | bytes accessed | tf_op | source)
XLA Modules:
  0.0 288.0 jit_solution(8757086449695751668)
XLA Ops:
  7.2 0.0 copy-start
  7.2 0.0 all-reduce.4.cloned.1.call-start
  7.2 0.0 copy-start.5
  7.2 8.0 %fusion.3 = bf16[1024,768]{1,0:T(8,128)(2,1)S(1)} fusion(bf16[1024,768]{1,0:T(8,128)(2,1)} %param.6), kind=kLoop, calls=%fused_computation.14 | loop fusion | flops 51904512 | bytes 3145728 | tf_op jit(solution)/shard_map/convert_element_type | solution.py:43
  15.3 3.1 %collective-permute-start = (bf16[1024,768]{1,0:T(8,128)(2,1)S(1)}, bf16[1024,768]{1,0:T(8,128)(2,1)S(1)}, u32[]{:S(2)}, u32[]{:S(2)}) collective-permute-start(bf16[1024,768]{1,0:T(8,128)(2,1)S(1)} %fusion.3), channel_id=1, source_target_pairs={{0,8},{4,12},{8,16},{12,20},{16,24},{20,28},{24,0},{28,4},{1,9},{5... | collective-permute-start | bytes 4718600 | tf_op jit(solution)/shard_map/ppermute | solution.py:14
  18.4 2.1 collective-permute-start.1
  20.5 0.0 copy-done.5
  20.5 1.0 fusion.64
  21.4 0.0 copy-start.8
  21.4 34.2 %collective-permute-done = bf16[1024,768]{1,0:T(8,128)(2,1)S(1)} collective-permute-done((bf16[1024,768]{1,0:T(8,128)(2,1)S(1)}, bf16[1024,768]{1,0:T(8,128)(2,1)S(1)}, u32[]{:S(2)}, u32[]{:S(2)}) %collective-permute-start) | collective-permute-done | bytes 1572896 | tf_op jit(solution)/shard_map/ppermute | solution.py:14
  55.7 1.0 convolution_convert_fusion.1
  56.6 0.0 copy-start.1
  56.6 31.3 %collective-permute-done.1 = bf16[1024,768]{1,0:T(8,128)(2,1)S(1)} collective-permute-done((bf16[1024,768]{1,0:T(8,128)(2,1)S(1)}, bf16[1024,768]{1,0:T(8,128)(2,1)S(1)}, u32[]{:S(2)}, u32[]{:S(2)}) %collective-permute-start.1) | collective-permute-done | bytes 1572896 | tf_op jit(solution)/shard_map/ppermute | solution.py:14
  87.9 0.0 copy-done.8
  87.9 4.3 %fusion.43 = (bf16[1024,384]{1,0:T(8,128)(2,1)S(1)}, f32[1024,384]{1,0:T(8,128)S(1)}) fusion(f32[384]{0:T(512)S(1)} %copy-done.8, bf16[1024,768]{1,0:T(8,128)(2,1)S(1)} %collective-permute-done.1, bf16[3,768,384]{2,1,0:T(8,128)(2,1)S(1)} %copy-done.5, f32[1024,384]{1,0:T(8,128)S(1)} %fusion.64, bf16[1024,384]{1,0:T(8,128)(2,1)S(1)} %convolution_convert_fusion.1), kind=kOutput, calls=%fused_computation.56 | convolution fusion | flops 631898112 | bytes 6883328 | tf_op jit(solution)/shard_map/dot_general | solution.py:49
  92.2 0.0 copy-done
  92.2 0.0 copy-done.1
  92.2 2.2 convert_reduce_fusion.1
  94.4 2.1 convolution_bitcast_fusion.1
  96.6 1.8 convolution_multiply_fusion
  98.4 2.1 convolution_bitcast_fusion
  100.6 2.1 convolution_bitcast_fusion.2
  102.7 2.1 maximum_multiply_fusion
  104.8 0.0 all-reduce.4.cloned.1.call-update
  104.8 0.3 convert_reduce_fusion
  105.1 0.0 copy-start.7
  105.1 3.4 %collective-permute-start.2 = (bf16[1024,384]{1,0:T(8,128)(2,1)}, bf16[1024,384]{1,0:T(8,128)(2,1)}, u32[]{:S(2)}, u32[]{:S(2)}) collective-permute-start(bf16[1024,384]{1,0:T(8,128)(2,1)} %get-tuple-element.13), channel_id=1, source_target_pairs={{0,24},{4,28},{8,0},{12,4},{16,8},{20,12},{24,16},{28,20},{1,25},{... | collective-permute-start | bytes 2359304 | tf_op jit(solution)/shard_map/ppermute | solution.py:14
  108.5 0.0 collective-permute-start.3
  108.5 4.0 %fusion.62 = f32[1024,768]{1,0:T(8,128)} fusion(bf16[1024,384]{1,0:T(8,128)(2,1)} %get-tuple-element.13, bf16[3,768,384]{2,1,0:T(8,128)(2,1)} %param.7), kind=kOutput, calls=%fused_computation.91 | convolution fusion | flops 603979776 | bytes 4521984 | tf_op jit(solution)/shard_map/dot_general | solution.py:33
  112.5 69.3 %all-reduce = (f32[384]{0:T(512)}, f32[768]{0:T(1024)}) all-reduce(f32[384]{0:T(512)S(1)} %broadcast_multiply_fusion.1, f32[768]{0:T(1024)S(1)} %broadcast_multiply_fusion), channel_id=1, replica_groups=mesh['seq'=8,'sub'=4] {'seq','sub'}, use_global_device_ids=true, to_apply=%region_2.0 | all-reduce | flops 1152 | bytes 9216 | tf_op jit(solution)/shard_map/psum | solution.py:86
  181.8 0.0 copy-done.7
  181.8 0.0 copy-start.6
  181.8 0.0 copy-start.3
  181.8 3.7 %fusion.33 = bf16[1024,768]{1,0:T(8,128)(2,1)} fusion(bf16[1024,768]{1,0:T(8,128)(2,1)} %param.6, bf16[1024,384]{1,0:T(8,128)(2,1)S(1)} %get-tuple-element.10, bf16[384,768]{1,0:T(8,128)(2,1)S(1)} %copy-done, f32[768]{0:T(1024)S(1)} %copy-done.7), kind=kOutput, calls=%fused_computation.44 | convolution fusion | flops 607125504 | bytes 4525056 | tf_op jit(solution)/shard_map/dot_general | solution.py:60
  185.5 0.0 copy-start.2
  185.5 0.0 collective-permute-done.2
  185.5 0.0 copy-done.6
  185.5 2.3 fusion.59
  187.8 0.0 collective-permute-done.3
  187.8 0.0 copy-done.3
  187.8 0.0 copy-done.2
  187.8 4.6 %fusion = bf16[1024,768]{1,0:T(8,128)(2,1)} fusion(bf16[1024,768]{1,0:T(8,128)(2,1)S(1)} %copy-done.1, bf16[1024,768]{1,0:T(8,128)(2,1)S(1)} %copy-done.3, f32[1024,768]{1,0:T(8,128)S(1)} %copy-done.2, f32[1024,768]{1,0:T(8,128)S(1)} %fusion.59, bf16[1024,384]{1,0:T(8,128)(2,1)} %collective-permute-done.3, bf16[3,768,384]{2,1,0:T(8,128)(2,1)S(1)} %copy-done.6), kind=kOutput, calls=%fused_computation.11 | convolution fusion | flops 615776256 | bytes 12386304 | tf_op jit(solution)/shard_map/dot_general | solution.py:33
  192.4 83.6 %all-reduce.4.cloned.1.call-done = (f32[3,768,384]{2,1,0:T(8,128)}, f32[384,768]{1,0:T(8,128)}) async-done(((f32[3,768,384]{2,1,0:T(8,128)}, f32[384,768]{1,0:T(8,128)}), (f32[3,768,384]{2,1,0:T(8,128)}, f32[384,768]{1,0:T(8,128)})) %all-reduce.4.cloned.1.call-update) | async-done | bytes 4718608 | tf_op jit(solution)/shard_map/psum | solution.py:86
  276.0 0.0 copy-start.4
  276.0 4.1 %copy.14 = f32[3,768,384]{2,1,0:T(8,128)} copy(f32[3,768,384]{2,1,0:T(8,128)} %get-tuple-element.16) | data formatting | bytes 7077888
  280.2 0.0 copy-done.4
  280.2 1.0 copy.15
  (2 shorter events, 0.0 us)
Async XLA Ops:
  7.2 85.0 %copy-start = (bf16[384,768]{1,0:T(8,128)(2,1)S(1)}, bf16[384,768]{1,0:T(8,128)(2,1)}, u32[]{:S(2)}) copy-start(bf16[384,768]{1,0:T(8,128)(2,1)} %param.9) | copy-start | bytes 1769476
  7.2 268.9 %all-reduce.4.cloned.1.call-start = ((), (), s32[]{:S(2)}) async-start(), calls=%async_computation | async-start | bytes 9437184 | tf_op jit(solution)/shard_map/psum | solution.py:86
  7.2 13.2 %copy-start.5 = (bf16[3,768,384]{2,1,0:T(8,128)(2,1)S(1)}, bf16[3,768,384]{2,1,0:T(8,128)(2,1)}, u32[]{:S(2)}) copy-start(bf16[3,768,384]{2,1,0:T(8,128)(2,1)} %param.7) | copy-start | bytes 5308420
  15.3 40.4 %collective-permute-start = (bf16[1024,768]{1,0:T(8,128)(2,1)S(1)}, bf16[1024,768]{1,0:T(8,128)(2,1)S(1)}, u32[]{:S(2)}, u32[]{:S(2)}) collective-permute-start(bf16[1024,768]{1,0:T(8,128)(2,1)S(1)} %fusion.3), channel_id=1, source_target_pairs={{0,8},{4,12},{8,16},{12,20},{16,24},{20,28},{24,0},{28,4},{1,9},{5... | collective-permute-start | bytes 4718600 | tf_op jit(solution)/shard_map/ppermute | solution.py:14
  18.4 69.6 %collective-permute-start.1 = (bf16[1024,768]{1,0:T(8,128)(2,1)S(1)}, bf16[1024,768]{1,0:T(8,128)(2,1)S(1)}, u32[]{:S(2)}, u32[]{:S(2)}) collective-permute-start(bf16[1024,768]{1,0:T(8,128)(2,1)S(1)} %fusion.3), channel_id=1, source_target_pairs={{0,24},{4,28},{8,0},{12,4},{16,8},{20,12},{24,16},{28,20},{1,25},{... | collective-permute-start | bytes 4718600 | tf_op jit(solution)/shard_map/ppermute | solution.py:14
  21.4 66.5 %copy-start.8 = (f32[384]{0:T(512)S(1)}, f32[384]{0:T(512)}, u32[]{:S(2)}) copy-start(f32[384]{0:T(512)} %param.8) | copy-start | bytes 4612
  56.6 35.6 %copy-start.1 = (bf16[1024,768]{1,0:T(8,128)(2,1)S(1)}, bf16[1024,768]{1,0:T(8,128)(2,1)}, u32[]{:S(2)}) copy-start(bf16[1024,768]{1,0:T(8,128)(2,1)} %param.11) | copy-start | bytes 4718596
  105.1 76.7 %copy-start.7 = (f32[768]{0:T(1024)S(1)}, f32[768]{0:T(1024)}, u32[]{:S(2)}) copy-start(f32[768]{0:T(1024)} %param.10) | copy-start | bytes 9220
  105.1 80.4 %collective-permute-start.2 = (bf16[1024,384]{1,0:T(8,128)(2,1)}, bf16[1024,384]{1,0:T(8,128)(2,1)}, u32[]{:S(2)}, u32[]{:S(2)}) collective-permute-start(bf16[1024,384]{1,0:T(8,128)(2,1)} %get-tuple-element.13), channel_id=1, source_target_pairs={{0,24},{4,28},{8,0},{12,4},{16,8},{20,12},{24,16},{28,20},{1,25},{... | collective-permute-start | bytes 2359304 | tf_op jit(solution)/shard_map/ppermute | solution.py:14
  108.5 79.3 %collective-permute-start.3 = (bf16[1024,384]{1,0:T(8,128)(2,1)}, bf16[1024,384]{1,0:T(8,128)(2,1)}, u32[]{:S(2)}, u32[]{:S(2)}) collective-permute-start(bf16[1024,384]{1,0:T(8,128)(2,1)} %get-tuple-element.13), channel_id=1, source_target_pairs={{0,8},{4,12},{8,16},{12,20},{16,24},{20,28},{24,0},{28,4},{1,9},{5... | collective-permute-start | bytes 2359304 | tf_op jit(solution)/shard_map/ppermute | solution.py:14
  181.8 3.7 %copy-start.6 = (bf16[3,768,384]{2,1,0:T(8,128)(2,1)S(1)}, bf16[3,768,384]{2,1,0:T(8,128)(2,1)}, u32[]{:S(2)}) copy-start(bf16[3,768,384]{2,1,0:T(8,128)(2,1)} %param.7) | copy-start | bytes 5308420
  181.8 6.0 %copy-start.3 = (bf16[1024,768]{1,0:T(8,128)(2,1)S(1)}, bf16[1024,768]{1,0:T(8,128)(2,1)}, u32[]{:S(2)}) copy-start(bf16[1024,768]{1,0:T(8,128)(2,1)} %param.6) | copy-start | bytes 4718596
  185.5 2.3 copy-start.2
  276.0 4.1 %copy-start.4 = (f32[384,768]{1,0:T(8,128)S(1)}, f32[384,768]{1,0:T(8,128)}, u32[]{:S(2)}) copy-start(f32[384,768]{1,0:T(8,128)} %get-tuple-element.18) | copy-start | bytes 3538948
Sparse Core Ops, SparseCore 0:
  104.9 171.0 all-reduce.3
where the time goes:
time: 288 us
  waiting for transfers between devices  149 us (52%)
  blocking collectives  69.3 us (24%)
  matrix products  31.2 us (11%)
  between operations  14.2 us (5%)
  other arithmetic  10.4 us (4%)
  starting transfers between devices  8.58 us (3%)
  local copies, waits for them, and re-layouts  5.18 us (2%)
    psum x1, waiting for transfers between devices, local(): lax.psum((kernel_part, offset_part, mixer_part, biases_part), ('seq', 'su...  83.6 us
    psum x1, blocking collectives, local(): lax.psum((kernel_part, offset_part, mixer_part, biases_part), ('seq', 'su...  69.3 us
    ppermute x4, waiting for transfers between devices, from_behind(): return lax.ppermute(value, axis, pairs)  65.5 us
    dot_general x4, matrix products, times_transposed(): lax.dot_general(left, right, (((1,), (1,)), ((), ())), preferred_element_...  13.1 us
    ppermute x4, starting transfers between devices, from_behind(): return lax.ppermute(value, axis, pairs)  8.54 us
    dot_general x4, matrix products, contract_rows(): lax.dot_general(left, right, (((0,), (0,)), ((), ())), preferred_element_...  8.25 us
    convert_element_type x1, other arithmetic, local(): activated_output = gelu_exact(inputs).astype(jnp.bfloat16)  8.04 us
  transfers between devices with their start and end apart: 5, of which 3 were waited for; matrix products, arithmetic and copies ran while one was open for 6% of the time, Pallas kernels for 0%

commit v1 on v0

v1 whole, which is shorter than its diff:
```python
import math

import jax
import jax.numpy as jnp
from jax import lax
from jax.sharding import PartitionSpec as P

DILATION_STEP = 8192
AXES = ("seq", "sub")


def gelu_parts(values):
    normal_cdf = 0.5 * (1.0 + lax.erf(values * (1.0 / math.sqrt(2.0))))
    slope = normal_cdf + values * jnp.exp(-0.5 * values * values) * (1.0 / math.sqrt(2.0 * math.pi))
    return values * normal_cdf, slope


def contract_rows(left, right):
    return lax.dot_general(
        left, right, (((0,), (0,)), ((), ())), preferred_element_type=jnp.float32
    )


def times_transposed(left, right):
    return lax.dot_general(
        left, right, (((1,), (1,)), ((), ())), preferred_element_type=jnp.float32
    )


class Layout:
    def __init__(self, mesh_shape, rows):
        seq, sub = mesh_shape["seq"], mesh_shape["sub"]
        self.count = seq * sub
        self.plane = DILATION_STEP // rows
        self.ring = self.count // self.plane
        self.bins = rows * self.count

    def around(self, value, steps):
        hop = steps * self.plane
        pairs = [(i, (i + hop) % self.count) for i in range(self.count)]
        return lax.ppermute(value, AXES, pairs)

    def across(self, value, mask):
        return lax.ppermute(value, AXES, [(i, i ^ mask) for i in range(self.count)])

    def place(self):
        flat = lax.axis_index("seq") * lax.axis_size("sub") + lax.axis_index("sub")
        return flat % self.plane


def pick(stacked, index):
    return lax.dynamic_index_in_dim(stacked, index, 0, keepdims=False)


def encode(main, exact):
    parts = [main.astype(jnp.bfloat16)]
    if exact is not None:
        high = lax.reduce_precision(exact, 8, 7)
        low = lax.reduce_precision(exact - high, 8, 7)
        parts += [high.astype(jnp.bfloat16), low.astype(jnp.bfloat16)]
    return jnp.concatenate(parts, axis=-2) if len(parts) > 1 else parts[0]


def decode(sent, rows, extra):
    wide = sent.astype(jnp.float32)
    if not extra:
        return wide, None
    return wide[..., :rows, :], (
        wide[..., rows : rows + extra, :] + wide[..., rows + extra :, :]
    )


def plus(left, right):
    return left[0] + right[0], None if left[1] is None else left[1] + right[1]


def all_reduce(layout, main, exact):
    rows, extra = main.shape[1], 0 if exact is None else exact.shape[1]
    place = layout.place()
    core, block = place % 2, place // 2
    blocks = layout.plane // 2

    def cut(array, index):
        if array is None:
            return None
        return pick(array.reshape((blocks, 2) + array.shape[1:]).swapaxes(0, 1), index)

    arrived = layout.across(encode(cut(main, 1 - core), cut(exact, 1 - core)), 1)
    held = plus((cut(main, core), cut(exact, core)), decode(arrived, rows, extra))

    def one(index):
        return pick(held[0], index), None if exact is None else pick(held[1], index)

    arrived = [
        layout.across(encode(*one(block ^ k)), 2 * k) for k in range(1, blocks)
    ]
    total = one(block)
    for value in arrived:
        total = plus(total, decode(value, rows, extra))
    sent = encode(*total)
    level = [sent] + [layout.around(sent, -step) for step in range(1, layout.ring)]
    level = [decode(value, rows, extra) for value in level]
    while len(level) > 1:
        half = len(level) // 2
        level = [plus(level[i], level[i + half]) for i in range(half)]
    sent = encode(*level[0])
    gathered = jnp.zeros((blocks,) + sent.shape, sent.dtype)
    for k in range(blocks):
        value = sent if k == 0 else layout.across(sent, 2 * k)
        gathered = lax.dynamic_update_index_in_dim(gathered, value, block ^ k, 0)
    other = layout.across(gathered, 1)
    first = jnp.where(core == 0, gathered, other)
    second = jnp.where(core == 0, other, gathered)
    both = jnp.stack([first, second], axis=1).reshape((layout.plane,) + sent.shape)
    return decode(both, rows, extra)


def solution(mesh):
    mesh_shape = dict(mesh.shape)

    def local(features, kernel, offsets, mixer, biases, cotangent):
        rows, channels = features.shape
        width = kernel.shape[2]
        layout = Layout(mesh_shape, rows)
        factor = 1.0 / math.sqrt(layout.bins)
        plane = layout.plane
        cuts = [(0, 256), (256, width)]
        inputs = features.astype(jnp.float32)
        activated, slope_in = gelu_parts(inputs)
        activated = activated.astype(jnp.bfloat16)
        taps = []
        for low, high in cuts:
            early = jnp.dot(activated, kernel[0, :, low:high], preferred_element_type=jnp.float32)
            late = jnp.dot(activated, kernel[2, :, low:high], preferred_element_type=jnp.float32)
            taps.append(
                (
                    layout.around(early.astype(jnp.bfloat16), 1),
                    layout.around(late.astype(jnp.bfloat16), -1),
                )
            )
        center = jnp.dot(activated, kernel[1], preferred_element_type=jnp.float32)
        cot_float = cotangent.astype(jnp.float32)
        hidden_grad = times_transposed(cotangent, mixer)
        hidden, grads, arrived = [], [], []
        for (low, high), (early, late) in zip(cuts, taps):
            preact = (
                center[:, low:high]
                + early.astype(jnp.float32)
                + late.astype(jnp.float32)
                + offsets[low:high]
            )
            value, slope = gelu_parts(preact)
            hidden.append(value.astype(jnp.bfloat16))
            grad = (hidden_grad[:, low:high] * slope).astype(jnp.bfloat16)
            grads.append(grad)
            arrived.append((layout.around(grad, -1), layout.around(grad, 1)))
        hidden = jnp.concatenate(hidden, axis=1)
        grad = jnp.concatenate(grads, axis=1)
        layer_output = (
            inputs + jnp.dot(hidden, mixer, preferred_element_type=jnp.float32) + biases
        ).astype(jnp.bfloat16)
        mixer_part = contract_rows(cotangent, hidden) * factor
        center_part = contract_rows(activated, grad) * factor
        biases_part = jnp.sum(cot_float, axis=0) * factor
        offset_part = jnp.sum(grad.astype(jnp.float32), axis=0) * factor
        exact = jnp.concatenate([biases_part, offset_part]).reshape(plane, 1, -1)
        each = exact.shape[-1]
        exact = jnp.pad(exact, ((0, 0), (0, 7), (0, width - each)))
        first, vectors = all_reduce(
            layout,
            jnp.stack([center_part, mixer_part]).reshape(plane, -1, width),
            exact,
        )
        first = first.reshape(2, channels, width)
        vectors = vectors[:, 0, :each].reshape(-1)
        product = times_transposed(grad, kernel[1])
        sides = []
        for (low, high), (later, earlier) in zip(cuts, arrived):
            part = jnp.stack(
                [contract_rows(activated, later), contract_rows(activated, earlier)]
            ) * factor
            total, _ = all_reduce(layout, part.reshape(plane, -1, high - low), None)
            sides.append(total.reshape(2, channels, high - low))
            product = (
                product
                + times_transposed(later, kernel[0, :, low:high])
                + times_transposed(earlier, kernel[2, :, low:high])
            )
        input_grad = (cot_float + product * slope_in).astype(jnp.bfloat16)
        sides = jnp.concatenate(sides, axis=2)
        kernel_grad = jnp.stack([sides[0], first[0], sides[1]])
        mixer_grad = first[1].T
        return (
            layer_output,
            input_grad,
            kernel_grad,
            vectors[channels:],
            mixer_grad,
            vectors[:channels],
        )

    rows_split = P(AXES, None)
    return jax.shard_map(
        local,
        mesh=mesh,
        in_specs=(rows_split, P(), P(), P(), P(), rows_split),
        out_specs=(rows_split, rows_split, P(), P(), P(), P()),
        check_vma=False,
    )
```

time: 288 us -> 167 us (0.58)
  waiting for transfers between devices: 149 us -> 61.3 us
  blocking collectives: 69.3 us -> 0 us
  starting transfers between devices: 8.58 us -> 49.1 us
  between operations: 14.2 us -> 1.35 us
  local copies, waits for them, and re-layouts: 5.18 us -> 11.8 us
  other arithmetic: 10.4 us -> 14.3 us
    psum x1 -> x0, waiting for transfers between devices: 83.6 us -> none  [local(): lax.psum((kernel_part, offset_part, mixer_part, biases_part), ('seq', 'su...]
    psum x1 -> x0, blocking collectives: 69.3 us -> none  [local(): lax.psum((kernel_part, offset_part, mixer_part, biases_part), ('seq', 'su...]
    ppermute x4 -> x41, starting transfers between devices: 8.54 us -> 49.1 us  [the longest x17 25.7 us: around(): return lax.ppermute(value, AXES, pairs)]
    another operation x0 -> x7, other arithmetic: none -> 5.23 us  [the longest x1 3.35 us: local(): kernel_grad = jnp.stack([sides[0], first[0], sides[1]])]
    slice x0 -> x8, local copies, waits for them, and re-layouts: none -> 4.37 us  [the longest x1 1.59 us: local(): mixer_grad = first[1].T]
    ppermute x4 -> x41, waiting for transfers between devices: 65.5 us -> 61.3 us  [the longest x17 38.6 us: around(): return lax.ppermute(value, AXES, pairs)]
    dot_general x4 -> x6, matrix products: 8.25 us -> 6.61 us  [contract_rows(): lax.dot_general(left, right, (((0,), (0,)), ((), ())), preferred_element_...]
    convert_element_type x1 -> x22, other arithmetic: 8.04 us -> 6.53 us  [the longest x2 3.75 us: local(): grad = (hidden_grad[:, low:high] * slope).astype(jnp.bfloat16)]
  transfers between devices with their start and end apart: 5 -> 41, of which waited for: 3 -> 20; matrix products, arithmetic and copies ran while one was open for 6% -> 25% of each run, Pallas kernels for 0% -> 0%
where the time goes in v1:
time: 167 us; the launch traced here: 166 us
  waiting for transfers between devices  61.3 us (37%)
  starting transfers between devices  49.1 us (29%)
  matrix products  28.7 us (17%)
  other arithmetic  14.3 us (9%)
  local copies, waits for them, and re-layouts  11.8 us (7%)
    ppermute x17, waiting for transfers between devices, around(): return lax.ppermute(value, AXES, pairs)  38.6 us
    ppermute x17, starting transfers between devices, around(): return lax.ppermute(value, AXES, pairs)  25.7 us
    ppermute x24, starting transfers between devices, across(): return lax.ppermute(value, AXES, [(i, i ^ mask) for i in range(self.count)])  23.4 us
    ppermute x24, waiting for transfers between devices, across(): return lax.ppermute(value, AXES, [(i, i ^ mask) for i in range(self.count)])  22.7 us
    dot_general x6, matrix products, times_transposed(): lax.dot_general(left, right, (((1,), (1,)), ((), ())), preferred_element_...  13.2 us
    dot_general x6, matrix products, contract_rows(): lax.dot_general(left, right, (((0,), (0,)), ((), ())), preferred_element_...  6.61 us
    unnamed x41, local copies, waits for them, and re-layouts  4.58 us
    convert_element_type x2, other arithmetic, local(): grad = (hidden_grad[:, low:high] * slope).astype(jnp.bfloat16)  3.75 us
  transfers between devices with their start and end apart: 41, of which 20 were waited for; matrix products, arithmetic and copies ran while one was open for 25% of the time, Pallas kernels for 0%

profile of v1, /device:TPU:0, one launch (start us, length us, event | category | flops | bytes accessed | tf_op | source)
XLA Modules:
  0.0 166.5 jit_solution(8697605687875100518)
XLA Ops:
  0.7 2.1 %fusion.4 = bf16[1024,768]{1,0:T(8,128)(2,1)S(1)} fusion(bf16[1024,768]{1,0:T(8,128)(2,1)} %param.6), kind=kLoop, calls=%fused_computation.13 | loop fusion | flops 4718592 | bytes 3145728 | tf_op jit(solution)/shard_map/convert_element_type | solution.py:130
  3.4 3.1 %collective-permute-start = (bf16[1024,256]{0,1:T(8,128)(2,1)S(1)}, bf16[1024,256]{0,1:T(8,128)(2,1)S(1)}, u32[]{:S(2)}, u32[]{:S(2)}) collective-permute-start(bf16[1024,256]{0,1:T(8,128)(2,1)S(1)} %convolution_convert_fusion.1), channel_id=1, source_target_pairs={{0,8},{1,9},{2,10},{3,11},{4,12},{5,13},{6,14},{7,15},{8,16},{9,17... | collective-permute-start | bytes 1572872 | tf_op jit(solution)/shard_map/ppermute | solution.py:41
  6.4 1.4 convolution_convert_fusion
  7.9 2.0 %collective-permute-start.1 = (bf16[1024,256]{0,1:T(8,128)(2,1)}, bf16[1024,256]{0,1:T(8,128)(2,1)}, u32[]{:S(2)}, u32[]{:S(2)}) collective-permute-start(bf16[1024,256]{0,1:T(8,128)(2,1)} %convolution_convert_fusion), channel_id=1, source_target_pairs={{0,24},{1,25},{2,26},{3,27},{4,28},{5,29},{6,30},{7,31},{8,0},{9,1... | collective-permute-start | bytes 1572872 | tf_op jit(solution)/shard_map/ppermute | solution.py:41
  9.9 1.4 convolution_convert_fusion.3
  11.3 1.4 convolution_convert_fusion.2
  12.6 3.8 %collective-permute-start.3 = (bf16[1024,128]{0,1:T(8,128)(2,1)}, bf16[1024,128]{0,1:T(8,128)(2,1)}, u32[]{:S(2)}, u32[]{:S(2)}) collective-permute-start(bf16[1024,128]{0,1:T(8,128)(2,1)} %convolution_convert_fusion.2), channel_id=1, source_target_pairs={{0,24},{1,25},{2,26},{3,27},{4,28},{5,29},{6,30},{7,31},{8,0},{9,1... | collective-permute-start | bytes 786440 | tf_op jit(solution)/shard_map/ppermute | solution.py:41
  16.5 2.0 %fusion.24 = f32[1024,384]{0,1:T(8,128)} fusion(bf16[1024,768]{1,0:T(8,128)(2,1)S(1)} %fusion.4, bf16[3,768,384]{2,1,0:T(8,128)(2,1)S(1)} %copy-done.4), kind=kOutput, calls=%fused_computation.64 | convolution fusion | flops 603979776 | bytes 3735552 | tf_op jit(solution)/shard_map/dot_general | solution.py:141
  18.4 2.0 %fusion.108 = f32[1024,384]{0,1:T(8,128)} fusion(bf16[1024,768]{1,0:T(8,128)(2,1)S(1)} %copy-done.9, bf16[384,768]{1,0:T(8,128)(2,1)S(1)} %copy-done), kind=kOutput, calls=%fused_computation.213 | convolution fusion | flops 603979776 | bytes 3735552 | tf_op jit(solution)/shard_map/dot_general | solution.py:25
  21.1 17.1 %collective-permute-done.2 = bf16[1024,128]{0,1:T(8,128)(2,1)S(1)} collective-permute-done((bf16[1024,128]{0,1:T(8,128)(2,1)}, bf16[1024,128]{0,1:T(8,128)(2,1)S(1)}, u32[]{:S(2)}, u32[]{:S(2)}) %collective-permute-start.2) | collective-permute-done | bytes 262176 | tf_op jit(solution)/shard_map/ppermute | solution.py:41
  38.2 4.8 %collective-permute-done.3 = bf16[1024,128]{0,1:T(8,128)(2,1)} collective-permute-done((bf16[1024,128]{0,1:T(8,128)(2,1)}, bf16[1024,128]{0,1:T(8,128)(2,1)}, u32[]{:S(2)}, u32[]{:S(2)}) %collective-permute-start.3) | collective-permute-done | bytes 262176 | tf_op jit(solution)/shard_map/ppermute | solution.py:41
  43.0 1.7 fusion.31
  45.2 3.3 %collective-permute-start.6 = (bf16[1024,128]{0,1:T(8,128)(2,1)S(1)}, bf16[1024,128]{0,1:T(8,128)(2,1)S(1)}, u32[]{:S(2)}, u32[]{:S(2)}) collective-permute-start(bf16[1024,128]{0,1:T(8,128)(2,1)S(1)} %get-tuple-element.28), channel_id=1, source_target_pairs={{0,24},{1,25},{2,26},{3,27},{4,28},{5,29},{6,30},{7,31},{8,0},{9,1... | collective-permute-start | bytes 786440 | tf_op jit(solution)/shard_map/ppermute | solution.py:41
  48.5 2.1 %fusion.18 = (bf16[1024,256]{0,1:T(8,128)(2,1)S(1)}, bf16[1024,256]{0,1:T(8,128)(2,1)S(1)}) fusion(f32[1024,384]{0,1:T(8,128)} %fusion.108, f32[256]{0:T(256)S(1)} %slice-done, bf16[1024,256]{0,1:T(8,128)(2,1)} %collective-permute-done.1, bf16[1024,256]{0,1:T(8,128)(2,1)S(1)} %collective-permute-done, f32[1024,384]{0,1:T(8,128)S(1)} %copy-done.6), kind=kLoop, calls=%fused_computation.45 | loop fusion | flops 4456448 | bytes 4195328 | tf_op jit(solution)/shard_map/convert_element_type | solution.py:154
  50.7 3.8 %collective-permute-start.4 = (bf16[1024,256]{0,1:T(8,128)(2,1)S(1)}, bf16[1024,256]{0,1:T(8,128)(2,1)}, u32[]{:S(2)}, u32[]{:S(2)}) collective-permute-start(bf16[1024,256]{0,1:T(8,128)(2,1)S(1)} %get-tuple-element.20), channel_id=1, source_target_pairs={{0,24},{1,25},{2,26},{3,27},{4,28},{5,29},{6,30},{7,31},{8,0},{9,1... | collective-permute-start | bytes 1572872 | tf_op jit(solution)/shard_map/ppermute | solution.py:41
  54.5 3.8 %fusion.22 = f32[1024,768]{1,0:T(8,128)} fusion(bf16[3,768,384]{2,1,0:T(8,128)(2,1)} %param.7, bf16[1024,128]{0,1:T(8,128)(2,1)S(1)} %get-tuple-element.28, bf16[1024,256]{0,1:T(8,128)(2,1)S(1)} %get-tuple-element.20), kind=kOutput, calls=%fused_computation.62 | convolution fusion | flops 605552640 | bytes 4521984 | tf_op jit(solution)/shard_map/dot_general | solution.py:25
  59.8 1.0 fusion.12
  62.3 1.0 fusion.11
  63.7 2.2 %fusion.6 = bf16[1024,768]{1,0:T(8,128)(2,1)} fusion(bf16[1024,768]{1,0:T(8,128)(2,1)S(1)} %copy-done.7, bf16[384,768]{1,0:T(8,128)(2,1)S(1)} %copy-done, f32[768]{0:T(1024)S(1)} %copy-done.19, bf16[1024,128]{0,1:T(8,128)(2,1)S(1)} %get-tuple-element.29, bf16[1024,256]{0,1:T(8,128)(2,1)S(1)} %get-tuple-element.21), kind=kOutput, calls=%fused_computation.15 | convolution fusion | flops 608698368 | bytes 4525056 | tf_op jit(solution)/shard_map/dot_general | solution.py:160
  65.9 1.6 pad_maximum_fusion.1
  67.6 1.3 fusion.21
  69.0 1.1 bitcast_add_fusion.1
  70.1 1.6 collective-permute-start.20
  71.7 1.5 collective-permute-start.21
  74.3 1.7 %collective-permute-done.21 = bf16[192,128]{1,0:T(8,128)(2,1)S(1)} collective-permute-done((bf16[192,128]{1,0:T(8,128)(2,1)S(1)}, bf16[192,128]{1,0:T(8,128)(2,1)S(1)}, u32[]{:S(2)}, u32[]{:S(2)}) %collective-permute-start.21) | collective-permute-done | bytes 49184 | tf_op jit(solution)/shard_map/ppermute | solution.py:44
  76.0 2.2 %collective-permute-done.22 = bf16[192,128]{1,0:T(8,128)(2,1)S(1)} collective-permute-done((bf16[192,128]{1,0:T(8,128)(2,1)S(1)}, bf16[192,128]{1,0:T(8,128)(2,1)S(1)}, u32[]{:S(2)}, u32[]{:S(2)}) %collective-permute-start.22) | collective-permute-done | bytes 49184 | tf_op jit(solution)/shard_map/ppermute | solution.py:44
  78.2 1.1 collective-permute-start.23
  79.3 2.0 %collective-permute-start.24 = (bf16[192,128]{1,0:T(8,128)(2,1)S(1)}, bf16[192,128]{1,0:T(8,128)(2,1)S(1)}, u32[]{:S(2)}, u32[]{:S(2)}) collective-permute-start(bf16[192,128]{1,0:T(8,128)(2,1)S(1)} %fusion.74), channel_id=1, source_target_pairs={{0,24},{1,25},{2,26},{3,27},{4,28},{5,29},{6,30},{7,31},{8,0},{9,1... | collective-permute-start | bytes 147464 | tf_op jit(solution)/shard_map/ppermute | solution.py:41
  81.4 2.1 %collective-permute-done.23 = bf16[192,128]{1,0:T(8,128)(2,1)S(1)} collective-permute-done((bf16[192,128]{1,0:T(8,128)(2,1)S(1)}, bf16[192,128]{1,0:T(8,128)(2,1)S(1)}, u32[]{:S(2)}, u32[]{:S(2)}) %collective-permute-start.23) | collective-permute-done | bytes 49184 | tf_op jit(solution)/shard_map/ppermute | solution.py:41
  83.9 3.3 %collective-permute-done.25 = bf16[192,128]{1,0:T(8,128)(2,1)S(1)} collective-permute-done((bf16[192,128]{1,0:T(8,128)(2,1)S(1)}, bf16[192,128]{1,0:T(8,128)(2,1)S(1)}, u32[]{:S(2)}, u32[]{:S(2)}) %collective-permute-start.25) | collective-permute-done | bytes 49184 | tf_op jit(solution)/shard_map/ppermute | solution.py:41
  88.5 1.4 collective-permute-start.27
  89.9 1.6 collective-permute-done.26
  91.4 1.3 collective-permute-start.28
  92.8 3.7 %collective-permute-done.28 = bf16[192,128]{1,0:T(8,128)(2,1)S(1)} collective-permute-done((bf16[192,128]{1,0:T(8,128)(2,1)S(1)}, bf16[192,128]{1,0:T(8,128)(2,1)S(1)}, u32[]{:S(2)}, u32[]{:S(2)}) %collective-permute-start.28) | collective-permute-done | bytes 49184 | tf_op jit(solution)/shard_map/ppermute | solution.py:44
  96.5 1.7 convolution_bitcast_fusion
  98.2 1.7 convolution_bitcast_fusion.1
  100.6 1.8 %fusion.37 = f32[1024,768]{1,0:T(8,128)S(1)} fusion(bf16[1024,256]{0,1:T(8,128)(2,1)} %collective-permute-done.5, bf16[3,768,384]{2,1,0:T(8,128)(2,1)S(1)} %copy-done.5), kind=kOutput, calls=%fused_computation.82 | convolution fusion | flops 402653184 | bytes 4063232 | tf_op jit(solution)/shard_map/dot_general | solution.py:25
  102.5 1.8 %fusion.40 = f32[1024,768]{1,0:T(8,128)S(1)} fusion(bf16[1024,256]{0,1:T(8,128)(2,1)} %collective-permute-done.4, bf16[3,768,384]{2,1,0:T(8,128)(2,1)S(1)} %copy-done.5), kind=kOutput, calls=%fused_computation.85 | convolution fusion | flops 402653184 | bytes 4063232 | tf_op jit(solution)/shard_map/dot_general | solution.py:25
  104.6 3.2 %fusion = bf16[1024,768]{1,0:T(8,128)(2,1)} fusion(bf16[1024,768]{1,0:T(8,128)(2,1)S(1)} %copy-done.11, bf16[1024,768]{1,0:T(8,128)(2,1)S(1)} %copy-done.8, f32[1024,768]{1,0:T(8,128)S(1)} %fusion.59, f32[1024,768]{1,0:T(8,128)S(1)} %fusion.37, f32[1024,768]{1,0:T(8,128)S(1)} %copy-done.2, f32[1024,768]{1,0:T(8,128)S(1)} %fusion.40, ...), kind=kOutput, calls=%fused_computation.9 | convolution fusion | flops 214695936 | bytes 17760256 | tf_op jit(solution)/shard_map/dot_general | solution.py:25
  108.7 1.4 collective-permute-start.32
  110.2 1.7 %collective-permute-start.33 = (bf16[208,384]{1,0:T(8,128)(2,1)S(1)}, bf16[208,384]{1,0:T(8,128)(2,1)S(1)}, u32[]{:S(2)}, u32[]{:S(2)}) collective-permute-start(bf16[208,384]{1,0:T(8,128)(2,1)S(1)} %pad_maximum_fusion.13), channel_id=1, source_target_pairs={{0,6},{1,7},{2,4},{3,5},{4,2},{5,3},{6,0},{7,1},{8,14},{9,15},{10,... | collective-permute-start | bytes 479240 | tf_op jit(solution)/shard_map/ppermute | solution.py:44
  112.0 2.3 %collective-permute-done.31 = bf16[208,384]{1,0:T(8,128)(2,1)S(1)} collective-permute-done((bf16[208,384]{1,0:T(8,128)(2,1)S(1)}, bf16[208,384]{1,0:T(8,128)(2,1)S(1)}, u32[]{:S(2)}, u32[]{:S(2)}) %collective-permute-start.31) | collective-permute-done | bytes 159776 | tf_op jit(solution)/shard_map/ppermute | solution.py:44
  114.3 1.5 collective-permute-done.32
  115.8 3.1 %collective-permute-done.33 = bf16[208,384]{1,0:T(8,128)(2,1)S(1)} collective-permute-done((bf16[208,384]{1,0:T(8,128)(2,1)S(1)}, bf16[208,384]{1,0:T(8,128)(2,1)S(1)}, u32[]{:S(2)}, u32[]{:S(2)}) %collective-permute-start.33) | collective-permute-done | bytes 159776 | tf_op jit(solution)/shard_map/ppermute | solution.py:44
  119.2 1.1 collective-permute-start.35
  122.5 1.5 collective-permute-start.11
  123.9 7.0 %collective-permute-done.34 = bf16[208,384]{1,0:T(8,128)(2,1)S(1)} collective-permute-done((bf16[208,384]{1,0:T(8,128)(2,1)S(1)}, bf16[208,384]{1,0:T(8,128)(2,1)S(1)}, u32[]{:S(2)}, u32[]{:S(2)}) %collective-permute-start.34) | collective-permute-done | bytes 159776 | tf_op jit(solution)/shard_map/ppermute | solution.py:41
  131.0 1.0 collective-permute-start.9
  132.3 1.0 collective-permute-start.37
  133.3 1.1 collective-permute-start.38
  134.4 1.2 collective-permute-done.9
  135.6 1.6 collective-permute-start.12
  137.3 2.1 %collective-permute-start.13 = (bf16[192,256]{1,0:T(8,128)(2,1)S(1)}, bf16[192,256]{1,0:T(8,128)(2,1)S(1)}, u32[]{:S(2)}, u32[]{:S(2)}) collective-permute-start(bf16[192,256]{1,0:T(8,128)(2,1)S(1)} %fusion.53), channel_id=1, source_target_pairs={{0,24},{1,25},{2,26},{3,27},{4,28},{5,29},{6,30},{7,31},{8,0},{9,1... | collective-permute-start | bytes 294920 | tf_op jit(solution)/shard_map/ppermute | solution.py:41
  139.5 3.2 %collective-permute-done.12 = bf16[192,256]{1,0:T(8,128)(2,1)S(1)} collective-permute-done((bf16[192,256]{1,0:T(8,128)(2,1)S(1)}, bf16[192,256]{1,0:T(8,128)(2,1)S(1)}, u32[]{:S(2)}, u32[]{:S(2)}) %collective-permute-start.12) | collective-permute-done | bytes 98336 | tf_op jit(solution)/shard_map/ppermute | solution.py:41
  142.7 2.5 %collective-permute-start.39 = (bf16[208,384]{1,0:T(8,128)(2,1)S(1)}, bf16[208,384]{1,0:T(8,128)(2,1)S(1)}, u32[]{:S(2)}, u32[]{:S(2)}) collective-permute-start(bf16[208,384]{1,0:T(8,128)(2,1)S(1)} %pad_maximum_fusion.15), channel_id=1, source_target_pairs={{0,6},{1,7},{2,4},{3,5},{4,2},{5,3},{6,0},{7,1},{8,14},{9,15},{10,... | collective-permute-start | bytes 479240 | tf_op jit(solution)/shard_map/ppermute | solution.py:44
  146.5 1.1 collective-permute-start.16
  147.7 1.7 %collective-permute-start.17 = (bf16[192,256]{1,0:T(8,128)(2,1)S(1)}, bf16[192,256]{1,0:T(8,128)(2,1)S(1)}, u32[]{:S(2)}, u32[]{:S(2)}) collective-permute-start(bf16[192,256]{1,0:T(8,128)(2,1)S(1)} %get-tuple-element.17), channel_id=1, source_target_pairs={{0,6},{1,7},{2,4},{3,5},{4,2},{5,3},{6,0},{7,1},{8,14},{9,15},{10,... | collective-permute-start | bytes 294920 | tf_op jit(solution)/shard_map/ppermute | solution.py:44
  149.5 2.4 %collective-permute-done.15 = bf16[192,256]{1,0:T(8,128)(2,1)S(1)} collective-permute-done((bf16[192,256]{1,0:T(8,128)(2,1)S(1)}, bf16[192,256]{1,0:T(8,128)(2,1)S(1)}, u32[]{:S(2)}, u32[]{:S(2)}) %collective-permute-start.15) | collective-permute-done | bytes 98336 | tf_op jit(solution)/shard_map/ppermute | solution.py:44
  151.9 1.3 collective-permute-done.17
  153.9 1.1 collective-permute-done.18
  155.3 1.6 fusion.107
  158.7 1.6 fusion.105
  160.3 2.8 %copy.30 = f32[384,768]{1,0:T(8,128)} copy(f32[384,768]{0,1:T(8,128)} %bitcast.190) | data formatting | bytes 2359296
  163.1 3.4 %pad_maximum_fusion = f32[3,768,384]{2,1,0:T(8,128)} fusion(f32[1,768,384]{2,1,0:T(8,128)S(1)} %copy-done.13, f32[1,768,384]{2,1,0:T(8,128)} %bitcast.189, f32[1,768,384]{2,1,0:T(8,128)S(1)} %copy-done.12), kind=kLoop, calls=%fused_computation.8 | loop fusion | flops 1769472 | bytes 7077888 | tf_op jit(solution)/shard_map/stack | solution.py:191
  (157 shorter events, 17.4 us)
Async XLA Ops:
  0.6 17.8 %copy-start = (bf16[384,768]{1,0:T(8,128)(2,1)S(1)}, bf16[384,768]{1,0:T(8,128)(2,1)}, u32[]{:S(2)}) copy-start(bf16[384,768]{1,0:T(8,128)(2,1)} %param.9) | copy-start | bytes 1769476
  0.6 2.1 %copy-start.4 = (bf16[3,768,384]{2,1,0:T(8,128)(2,1)S(1)}, bf16[3,768,384]{2,1,0:T(8,128)(2,1)}, u32[]{:S(2)}) copy-start(bf16[3,768,384]{2,1,0:T(8,128)(2,1)} %param.7) | copy-start | bytes 5308420
  3.4 45.1 %collective-permute-start = (bf16[1024,256]{0,1:T(8,128)(2,1)S(1)}, bf16[1024,256]{0,1:T(8,128)(2,1)S(1)}, u32[]{:S(2)}, u32[]{:S(2)}) collective-permute-start(bf16[1024,256]{0,1:T(8,128)(2,1)S(1)} %convolution_convert_fusion.1), channel_id=1, source_target_pairs={{0,8},{1,9},{2,10},{3,11},{4,12},{5,13},{6,14},{7,15},{8,16},{9,17... | collective-permute-start | bytes 1572872 | tf_op jit(solution)/shard_map/ppermute | solution.py:41
  7.9 40.7 %collective-permute-start.1 = (bf16[1024,256]{0,1:T(8,128)(2,1)}, bf16[1024,256]{0,1:T(8,128)(2,1)}, u32[]{:S(2)}, u32[]{:S(2)}) collective-permute-start(bf16[1024,256]{0,1:T(8,128)(2,1)} %convolution_convert_fusion), channel_id=1, source_target_pairs={{0,24},{1,25},{2,26},{3,27},{4,28},{5,29},{6,30},{7,31},{8,0},{9,1... | collective-permute-start | bytes 1572872 | tf_op jit(solution)/shard_map/ppermute | solution.py:41
  11.3 26.9 %collective-permute-start.2 = (bf16[1024,128]{0,1:T(8,128)(2,1)}, bf16[1024,128]{0,1:T(8,128)(2,1)S(1)}, u32[]{:S(2)}, u32[]{:S(2)}) collective-permute-start(bf16[1024,128]{0,1:T(8,128)(2,1)} %convolution_convert_fusion.3), channel_id=1, source_target_pairs={{0,8},{1,9},{2,10},{3,11},{4,12},{5,13},{6,14},{7,15},{8,16},{9,17... | collective-permute-start | bytes 786440 | tf_op jit(solution)/shard_map/ppermute | solution.py:41
  12.6 5.8 %copy-start.9 = (bf16[1024,768]{1,0:T(8,128)(2,1)S(1)}, bf16[1024,768]{1,0:T(8,128)(2,1)}, u32[]{:S(2)}) copy-start(bf16[1024,768]{1,0:T(8,128)(2,1)} %param.11) | copy-start | bytes 4718596
  12.6 30.3 %collective-permute-start.3 = (bf16[1024,128]{0,1:T(8,128)(2,1)}, bf16[1024,128]{0,1:T(8,128)(2,1)}, u32[]{:S(2)}, u32[]{:S(2)}) collective-permute-start(bf16[1024,128]{0,1:T(8,128)(2,1)} %convolution_convert_fusion.2), channel_id=1, source_target_pairs={{0,24},{1,25},{2,26},{3,27},{4,28},{5,29},{6,30},{7,31},{8,0},{9,1... | collective-permute-start | bytes 786440 | tf_op jit(solution)/shard_map/ppermute | solution.py:41
  20.4 0.7 copy-start.18
  20.4 28.1 %slice-start = ((f32[384]{0:T(512)}), f32[256]{0:T(256)S(1)}, s32[]{:S(2)}) async-start(f32[384]{0:T(512)} %param.8), calls=%async_computation | async-start | bytes 2048 | tf_op jit(solution)/shard_map/slice | solution.py:150
  21.1 27.4 %copy-start.6 = (f32[1024,384]{0,1:T(8,128)S(1)}, f32[1024,384]{0,1:T(8,128)}, u32[]{:S(2)}) copy-start(f32[1024,384]{0,1:T(8,128)} %fusion.24) | copy-start | bytes 4718596
  44.6 13.8 %collective-permute-start.7 = (bf16[1024,128]{0,1:T(8,128)(2,1)S(1)}, bf16[1024,128]{0,1:T(8,128)(2,1)S(1)}, u32[]{:S(2)}, u32[]{:S(2)}) collective-permute-start(bf16[1024,128]{0,1:T(8,128)(2,1)S(1)} %get-tuple-element.28), channel_id=1, source_target_pairs={{0,8},{1,9},{2,10},{3,11},{4,12},{5,13},{6,14},{7,15},{8,16},{9,17... | collective-permute-start | bytes 786440 | tf_op jit(solution)/shard_map/ppermute | solution.py:41
  45.2 15.6 %collective-permute-start.6 = (bf16[1024,128]{0,1:T(8,128)(2,1)S(1)}, bf16[1024,128]{0,1:T(8,128)(2,1)S(1)}, u32[]{:S(2)}, u32[]{:S(2)}) collective-permute-start(bf16[1024,128]{0,1:T(8,128)(2,1)S(1)} %get-tuple-element.28), channel_id=1, source_target_pairs={{0,24},{1,25},{2,26},{3,27},{4,28},{5,29},{6,30},{7,31},{8,0},{9,1... | collective-permute-start | bytes 786440 | tf_op jit(solution)/shard_map/ppermute | solution.py:41
  50.6 45.9 %collective-permute-start.5 = (bf16[1024,256]{0,1:T(8,128)(2,1)S(1)}, bf16[1024,256]{0,1:T(8,128)(2,1)}, u32[]{:S(2)}, u32[]{:S(2)}) collective-permute-start(bf16[1024,256]{0,1:T(8,128)(2,1)S(1)} %get-tuple-element.20), channel_id=1, source_target_pairs={{0,8},{1,9},{2,10},{3,11},{4,12},{5,13},{6,14},{7,15},{8,16},{9,17... | collective-permute-start | bytes 1572872 | tf_op jit(solution)/shard_map/ppermute | solution.py:41
  50.7 47.5 %collective-permute-start.4 = (bf16[1024,256]{0,1:T(8,128)(2,1)S(1)}, bf16[1024,256]{0,1:T(8,128)(2,1)}, u32[]{:S(2)}, u32[]{:S(2)}) collective-permute-start(bf16[1024,256]{0,1:T(8,128)(2,1)S(1)} %get-tuple-element.20), channel_id=1, source_target_pairs={{0,24},{1,25},{2,26},{3,27},{4,28},{5,29},{6,30},{7,31},{8,0},{9,1... | collective-permute-start | bytes 1572872 | tf_op jit(solution)/shard_map/ppermute | solution.py:41
  58.4 0.7 copy-start.14
  60.8 1.5 copy-start.10
  60.8 0.7 copy-start.16
  62.3 6.7 %collective-permute-start.19 = (bf16[4,192,128]{2,1,0:T(8,128)(2,1)}, bf16[4,192,128]{2,1,0:T(8,128)(2,1)}, u32[]{:S(2)}, u32[]{:S(2)}) collective-permute-start(bf16[4,192,128]{2,1,0:T(8,128)(2,1)} %fusion.50), channel_id=1, source_target_pairs={{0,1},{1,0},{2,3},{3,2},{4,5},{5,4},{6,7},{7,6},{8,9},{9,8},{10,11... | collective-permute-start | bytes 589832 | tf_op jit(solution)/shard_map/ppermute | solution.py:44
  62.3 1.4 copy-start.7
  62.3 1.4 copy-start.19
  68.9 18.9 %copy-start.5 = (bf16[3,768,384]{2,1,0:T(8,128)(2,1)S(1)}, bf16[3,768,384]{2,1,0:T(8,128)(2,1)}, u32[]{:S(2)}) copy-start(bf16[3,768,384]{2,1,0:T(8,128)(2,1)} %param.7) | copy-start | bytes 5308420
  68.9 18.9 %copy-start.17 = (bf16[1024,128]{0,1:T(8,128)(2,1)S(1)}, bf16[1024,128]{0,1:T(8,128)(2,1)}, u32[]{:S(2)}) copy-start(bf16[1024,128]{0,1:T(8,128)(2,1)} %copy-done.16) | copy-start | bytes 786436
  70.1 4.2 %collective-permute-start.20 = (bf16[192,128]{1,0:T(8,128)(2,1)S(1)}, bf16[192,128]{1,0:T(8,128)(2,1)S(1)}, u32[]{:S(2)}, u32[]{:S(2)}) collective-permute-start(bf16[192,128]{1,0:T(8,128)(2,1)S(1)} %get-tuple-element.42), channel_id=1, source_target_pairs={{0,2},{1,3},{2,0},{3,1},{4,6},{5,7},{6,4},{7,5},{8,10},{9,11},{10,... | collective-permute-start | bytes 147464 | tf_op jit(solution)/shard_map/ppermute | solution.py:44
  71.7 4.3 %collective-permute-start.21 = (bf16[192,128]{1,0:T(8,128)(2,1)S(1)}, bf16[192,128]{1,0:T(8,128)(2,1)S(1)}, u32[]{:S(2)}, u32[]{:S(2)}) collective-permute-start(bf16[192,128]{1,0:T(8,128)(2,1)S(1)} %get-tuple-element.44), channel_id=1, source_target_pairs={{0,4},{1,5},{2,6},{3,7},{4,0},{5,1},{6,2},{7,3},{8,12},{9,13},{10,... | collective-permute-start | bytes 147464 | tf_op jit(solution)/shard_map/ppermute | solution.py:44
  73.2 5.0 %collective-permute-start.22 = (bf16[192,128]{1,0:T(8,128)(2,1)S(1)}, bf16[192,128]{1,0:T(8,128)(2,1)S(1)}, u32[]{:S(2)}, u32[]{:S(2)}) collective-permute-start(bf16[192,128]{1,0:T(8,128)(2,1)S(1)} %get-tuple-element.43), channel_id=1, source_target_pairs={{0,6},{1,7},{2,4},{3,5},{4,2},{5,3},{6,0},{7,1},{8,14},{9,15},{10,... | collective-permute-start | bytes 147464 | tf_op jit(solution)/shard_map/ppermute | solution.py:44
  78.2 5.3 %collective-permute-start.23 = (bf16[192,128]{1,0:T(8,128)(2,1)S(1)}, bf16[192,128]{1,0:T(8,128)(2,1)S(1)}, u32[]{:S(2)}, u32[]{:S(2)}) collective-permute-start(bf16[192,128]{1,0:T(8,128)(2,1)S(1)} %fusion.74), channel_id=1, source_target_pairs={{0,16},{1,17},{2,18},{3,19},{4,20},{5,21},{6,22},{7,23},{8,24},{9,... | collective-permute-start | bytes 147464 | tf_op jit(solution)/shard_map/ppermute | solution.py:41
  79.3 4.6 %collective-permute-start.24 = (bf16[192,128]{1,0:T(8,128)(2,1)S(1)}, bf16[192,128]{1,0:T(8,128)(2,1)S(1)}, u32[]{:S(2)}, u32[]{:S(2)}) collective-permute-start(bf16[192,128]{1,0:T(8,128)(2,1)S(1)} %fusion.74), channel_id=1, source_target_pairs={{0,24},{1,25},{2,26},{3,27},{4,28},{5,29},{6,30},{7,31},{8,0},{9,1... | collective-permute-start | bytes 147464 | tf_op jit(solution)/shard_map/ppermute | solution.py:41
  81.3 5.9 %collective-permute-start.25 = (bf16[192,128]{1,0:T(8,128)(2,1)S(1)}, bf16[192,128]{1,0:T(8,128)(2,1)S(1)}, u32[]{:S(2)}, u32[]{:S(2)}) collective-permute-start(bf16[192,128]{1,0:T(8,128)(2,1)S(1)} %fusion.74), channel_id=1, source_target_pairs={{0,8},{1,9},{2,10},{3,11},{4,12},{5,13},{6,14},{7,15},{8,16},{9,17... | collective-permute-start | bytes 147464 | tf_op jit(solution)/shard_map/ppermute | solution.py:41
  83.5 24.3 %collective-permute-start.30 = (bf16[4,208,384]{2,1,0:T(8,128)(2,1)S(1)}, bf16[4,208,384]{2,1,0:T(8,128)(2,1)S(1)}, u32[]{:S(2)}, u32[]{:S(2)}) collective-permute-start(bf16[4,208,384]{2,1,0:T(8,128)(2,1)S(1)} %pad_maximum_fusion.5), channel_id=1, source_target_pairs={{0,1},{1,0},{2,3},{3,2},{4,5},{5,4},{6,7},{7,6},{8,9},{9,8},{10,11... | collective-permute-start | bytes 1916936 | tf_op jit(solution)/shard_map/ppermute | solution.py:44
  87.3 4.2 %collective-permute-start.26 = (bf16[192,128]{1,0:T(8,128)(2,1)S(1)}, bf16[192,128]{1,0:T(8,128)(2,1)S(1)}, u32[]{:S(2)}, u32[]{:S(2)}) collective-permute-start(bf16[192,128]{1,0:T(8,128)(2,1)S(1)} %get-tuple-element.19), channel_id=1, source_target_pairs={{0,2},{1,3},{2,0},{3,1},{4,6},{5,7},{6,4},{7,5},{8,10},{9,11},{10,... | collective-permute-start | bytes 147464 | tf_op jit(solution)/shard_map/ppermute | solution.py:44
  88.5 4.3 %collective-permute-start.27 = (bf16[192,128]{1,0:T(8,128)(2,1)S(1)}, bf16[192,128]{1,0:T(8,128)(2,1)S(1)}, u32[]{:S(2)}, u32[]{:S(2)}) collective-permute-start(bf16[192,128]{1,0:T(8,128)(2,1)S(1)} %get-tuple-element.19), channel_id=1, source_target_pairs={{0,4},{1,5},{2,6},{3,7},{4,0},{5,1},{6,2},{7,3},{8,12},{9,13},{10,... | collective-permute-start | bytes 147464 | tf_op jit(solution)/shard_map/ppermute | solution.py:44
  91.4 5.0 %collective-permute-start.28 = (bf16[192,128]{1,0:T(8,128)(2,1)S(1)}, bf16[192,128]{1,0:T(8,128)(2,1)S(1)}, u32[]{:S(2)}, u32[]{:S(2)}) collective-permute-start(bf16[192,128]{1,0:T(8,128)(2,1)S(1)} %get-tuple-element.19), channel_id=1, source_target_pairs={{0,6},{1,7},{2,4},{3,5},{4,2},{5,3},{6,0},{7,1},{8,14},{9,15},{10,... | collective-permute-start | bytes 147464 | tf_op jit(solution)/shard_map/ppermute | solution.py:44
  96.4 15.4 %collective-permute-start.29 = (bf16[4,192,128]{2,1,0:T(8,128)(2,1)S(1)}, bf16[4,192,128]{2,1,0:T(8,128)(2,1)S(1)}, u32[]{:S(2)}, u32[]{:S(2)}) collective-permute-start(bf16[4,192,128]{2,1,0:T(8,128)(2,1)S(1)} %bitcast_dynamic-update-slice_fusion.8), channel_id=1, source_target_pairs={{0,1},{1,0},{2,3},{3,2},{4,5},{5,4},{6,7},{7,6},{8,9},{9,8},{10,11... | collective-permute-start | bytes 589832 | tf_op jit(solution)/shard_map/ppermute | solution.py:44
  100.1 21.2 %collective-permute-start.8 = (bf16[4,192,256]{2,1,0:T(8,128)(2,1)S(1)}, bf16[4,192,256]{2,1,0:T(8,128)(2,1)S(1)}, u32[]{:S(2)}, u32[]{:S(2)}) collective-permute-start(bf16[4,192,256]{2,1,0:T(8,128)(2,1)S(1)} %fusion.36), channel_id=1, source_target_pairs={{0,1},{1,0},{2,3},{3,2},{4,5},{5,4},{6,7},{7,6},{8,9},{9,8},{10,11... | collective-permute-start | bytes 1179656 | tf_op jit(solution)/shard_map/ppermute | solution.py:44
  100.6 3.7 %copy-start.8 = (bf16[1024,768]{1,0:T(8,128)(2,1)S(1)}, bf16[1024,768]{1,0:T(8,128)(2,1)}, u32[]{:S(2)}) copy-start(bf16[1024,768]{1,0:T(8,128)(2,1)} %param.6) | copy-start | bytes 4718596
  100.6 3.7 %copy-start.11 = (bf16[1024,768]{1,0:T(8,128)(2,1)S(1)}, bf16[1024,768]{1,0:T(8,128)(2,1)}, u32[]{:S(2)}) copy-start(bf16[1024,768]{1,0:T(8,128)(2,1)} %param.11) | copy-start | bytes 4718596
  102.5 2.1 %copy-start.2 = (f32[1024,768]{1,0:T(8,128)S(1)}, f32[1024,768]{1,0:T(8,128)}, u32[]{:S(2)}) copy-start(f32[1024,768]{1,0:T(8,128)} %fusion.22) | copy-start | bytes 9437188
  102.5 2.1 %copy-start.15 = (bf16[1024,128]{0,1:T(8,128)(2,1)S(1)}, bf16[1024,128]{0,1:T(8,128)(2,1)}, u32[]{:S(2)}) copy-start(bf16[1024,128]{0,1:T(8,128)(2,1)} %copy-done.14) | copy-start | bytes 786436
  104.6 3.3 %copy-start.3 = (f32[2,768,384]{2,1,0:T(8,128)S(1)}, f32[2,768,384]{2,1,0:T(8,128)}, u32[]{:S(2)}) copy-start(f32[2,768,384]{2,1,0:T(8,128)} %pad_maximum_fusion.1) | copy-start | bytes 7077892
  108.2 6.1 %collective-permute-start.31 = (bf16[208,384]{1,0:T(8,128)(2,1)S(1)}, bf16[208,384]{1,0:T(8,128)(2,1)S(1)}, u32[]{:S(2)}, u32[]{:S(2)}) collective-permute-start(bf16[208,384]{1,0:T(8,128)(2,1)S(1)} %pad_maximum_fusion.11), channel_id=1, source_target_pairs={{0,2},{1,3},{2,0},{3,1},{4,6},{5,7},{6,4},{7,5},{8,10},{9,11},{10,... | collective-permute-start | bytes 479240 | tf_op jit(solution)/shard_map/ppermute | solution.py:44
  108.7 7.1 %collective-permute-start.32 = (bf16[208,384]{1,0:T(8,128)(2,1)S(1)}, bf16[208,384]{1,0:T(8,128)(2,1)S(1)}, u32[]{:S(2)}, u32[]{:S(2)}) collective-permute-start(bf16[208,384]{1,0:T(8,128)(2,1)S(1)} %pad_maximum_fusion.12), channel_id=1, source_target_pairs={{0,4},{1,5},{2,6},{3,7},{4,0},{5,1},{6,2},{7,3},{8,12},{9,13},{10,... | collective-permute-start | bytes 479240 | tf_op jit(solution)/shard_map/ppermute | solution.py:44
  110.2 8.8 %collective-permute-start.33 = (bf16[208,384]{1,0:T(8,128)(2,1)S(1)}, bf16[208,384]{1,0:T(8,128)(2,1)S(1)}, u32[]{:S(2)}, u32[]{:S(2)}) collective-permute-start(bf16[208,384]{1,0:T(8,128)(2,1)S(1)} %pad_maximum_fusion.13), channel_id=1, source_target_pairs={{0,6},{1,7},{2,4},{3,5},{4,2},{5,3},{6,0},{7,1},{8,14},{9,15},{10,... | collective-permute-start | bytes 479240 | tf_op jit(solution)/shard_map/ppermute | solution.py:44
  119.2 11.8 %collective-permute-start.34 = (bf16[208,384]{1,0:T(8,128)(2,1)S(1)}, bf16[208,384]{1,0:T(8,128)(2,1)S(1)}, u32[]{:S(2)}, u32[]{:S(2)}) collective-permute-start(bf16[208,384]{1,0:T(8,128)(2,1)S(1)} %get-tuple-element.46), channel_id=1, source_target_pairs={{0,16},{1,17},{2,18},{3,19},{4,20},{5,21},{6,22},{7,23},{8,24},{9,... | collective-permute-start | bytes 479240 | tf_op jit(solution)/shard_map/ppermute | solution.py:41
  119.2 12.8 %collective-permute-start.35 = (bf16[208,384]{1,0:T(8,128)(2,1)S(1)}, bf16[208,384]{1,0:T(8,128)(2,1)S(1)}, u32[]{:S(2)}, u32[]{:S(2)}) collective-permute-start(bf16[208,384]{1,0:T(8,128)(2,1)S(1)} %get-tuple-element.46), channel_id=1, source_target_pairs={{0,24},{1,25},{2,26},{3,27},{4,28},{5,29},{6,30},{7,31},{8,0},{9,1... | collective-permute-start | bytes 479240 | tf_op jit(solution)/shard_map/ppermute | solution.py:41
  120.3 11.8 %collective-permute-start.36 = (bf16[208,384]{1,0:T(8,128)(2,1)S(1)}, bf16[208,384]{1,0:T(8,128)(2,1)S(1)}, u32[]{:S(2)}, u32[]{:S(2)}) collective-permute-start(bf16[208,384]{1,0:T(8,128)(2,1)S(1)} %get-tuple-element.46), channel_id=1, source_target_pairs={{0,8},{1,9},{2,10},{3,11},{4,12},{5,13},{6,14},{7,15},{8,16},{9,17... | collective-permute-start | bytes 479240 | tf_op jit(solution)/shard_map/ppermute | solution.py:41
  121.5 12.9 %collective-permute-start.10 = (bf16[192,256]{1,0:T(8,128)(2,1)S(1)}, bf16[192,256]{1,0:T(8,128)(2,1)S(1)}, u32[]{:S(2)}, u32[]{:S(2)}) collective-permute-start(bf16[192,256]{1,0:T(8,128)(2,1)S(1)} %get-tuple-element.39), channel_id=1, source_target_pairs={{0,4},{1,5},{2,6},{3,7},{4,0},{5,1},{6,2},{7,3},{8,12},{9,13},{10,... | collective-permute-start | bytes 294920 | tf_op jit(solution)/shard_map/ppermute | solution.py:44
  122.5 11.9 %collective-permute-start.11 = (bf16[192,256]{1,0:T(8,128)(2,1)S(1)}, bf16[192,256]{1,0:T(8,128)(2,1)S(1)}, u32[]{:S(2)}, u32[]{:S(2)}) collective-permute-start(bf16[192,256]{1,0:T(8,128)(2,1)S(1)} %get-tuple-element.38), channel_id=1, source_target_pairs={{0,6},{1,7},{2,4},{3,5},{4,2},{5,3},{6,0},{7,1},{8,14},{9,15},{10,... | collective-permute-start | bytes 294920 | tf_op jit(solution)/shard_map/ppermute | solution.py:44
  131.0 4.6 %collective-permute-start.9 = (bf16[192,256]{1,0:T(8,128)(2,1)S(1)}, bf16[192,256]{1,0:T(8,128)(2,1)S(1)}, u32[]{:S(2)}, u32[]{:S(2)}) collective-permute-start(bf16[192,256]{1,0:T(8,128)(2,1)S(1)} %get-tuple-element.37), channel_id=1, source_target_pairs={{0,2},{1,3},{2,0},{3,1},{4,6},{5,7},{6,4},{7,5},{8,10},{9,11},{10,... | collective-permute-start | bytes 294920 | tf_op jit(solution)/shard_map/ppermute | solution.py:44
  132.3 15.4 %collective-permute-start.37 = (bf16[208,384]{1,0:T(8,128)(2,1)S(1)}, bf16[208,384]{1,0:T(8,128)(2,1)S(1)}, u32[]{:S(2)}, u32[]{:S(2)}) collective-permute-start(bf16[208,384]{1,0:T(8,128)(2,1)S(1)} %pad_maximum_fusion.15), channel_id=1, source_target_pairs={{0,2},{1,3},{2,0},{3,1},{4,6},{5,7},{6,4},{7,5},{8,10},{9,11},{10,... | collective-permute-start | bytes 479240 | tf_op jit(solution)/shard_map/ppermute | solution.py:44
  133.3 20.0 %collective-permute-start.38 = (bf16[208,384]{1,0:T(8,128)(2,1)S(1)}, bf16[208,384]{1,0:T(8,128)(2,1)S(1)}, u32[]{:S(2)}, u32[]{:S(2)}) collective-permute-start(bf16[208,384]{1,0:T(8,128)(2,1)S(1)} %pad_maximum_fusion.15), channel_id=1, source_target_pairs={{0,4},{1,5},{2,6},{3,7},{4,0},{5,1},{6,2},{7,3},{8,12},{9,13},{10,... | collective-permute-start | bytes 479240 | tf_op jit(solution)/shard_map/ppermute | solution.py:44
  135.6 7.0 %collective-permute-start.12 = (bf16[192,256]{1,0:T(8,128)(2,1)S(1)}, bf16[192,256]{1,0:T(8,128)(2,1)S(1)}, u32[]{:S(2)}, u32[]{:S(2)}) collective-permute-start(bf16[192,256]{1,0:T(8,128)(2,1)S(1)} %fusion.53), channel_id=1, source_target_pairs={{0,16},{1,17},{2,18},{3,19},{4,20},{5,21},{6,22},{7,23},{8,24},{9,... | collective-permute-start | bytes 294920 | tf_op jit(solution)/shard_map/ppermute | solution.py:41
  137.3 7.9 %collective-permute-start.13 = (bf16[192,256]{1,0:T(8,128)(2,1)S(1)}, bf16[192,256]{1,0:T(8,128)(2,1)S(1)}, u32[]{:S(2)}, u32[]{:S(2)}) collective-permute-start(bf16[192,256]{1,0:T(8,128)(2,1)S(1)} %fusion.53), channel_id=1, source_target_pairs={{0,24},{1,25},{2,26},{3,27},{4,28},{5,29},{6,30},{7,31},{8,0},{9,1... | collective-permute-start | bytes 294920 | tf_op jit(solution)/shard_map/ppermute | solution.py:41
  139.4 6.4 %collective-permute-start.14 = (bf16[192,256]{1,0:T(8,128)(2,1)S(1)}, bf16[192,256]{1,0:T(8,128)(2,1)S(1)}, u32[]{:S(2)}, u32[]{:S(2)}) collective-permute-start(bf16[192,256]{1,0:T(8,128)(2,1)S(1)} %fusion.53), channel_id=1, source_target_pairs={{0,8},{1,9},{2,10},{3,11},{4,12},{5,13},{6,14},{7,15},{8,16},{9,17... | collective-permute-start | bytes 294920 | tf_op jit(solution)/shard_map/ppermute | solution.py:41
  142.7 10.7 %collective-permute-start.39 = (bf16[208,384]{1,0:T(8,128)(2,1)S(1)}, bf16[208,384]{1,0:T(8,128)(2,1)S(1)}, u32[]{:S(2)}, u32[]{:S(2)}) collective-permute-start(bf16[208,384]{1,0:T(8,128)(2,1)S(1)} %pad_maximum_fusion.15), channel_id=1, source_target_pairs={{0,6},{1,7},{2,4},{3,5},{4,2},{5,3},{6,0},{7,1},{8,14},{9,15},{10,... | collective-permute-start | bytes 479240 | tf_op jit(solution)/shard_map/ppermute | solution.py:44
  145.9 6.0 %collective-permute-start.15 = (bf16[192,256]{1,0:T(8,128)(2,1)S(1)}, bf16[192,256]{1,0:T(8,128)(2,1)S(1)}, u32[]{:S(2)}, u32[]{:S(2)}) collective-permute-start(bf16[192,256]{1,0:T(8,128)(2,1)S(1)} %get-tuple-element.17), channel_id=1, source_target_pairs={{0,2},{1,3},{2,0},{3,1},{4,6},{5,7},{6,4},{7,5},{8,10},{9,11},{10,... | collective-permute-start | bytes 294920 | tf_op jit(solution)/shard_map/ppermute | solution.py:44
  146.5 5.3 %collective-permute-start.16 = (bf16[192,256]{1,0:T(8,128)(2,1)S(1)}, bf16[192,256]{1,0:T(8,128)(2,1)S(1)}, u32[]{:S(2)}, u32[]{:S(2)}) collective-permute-start(bf16[192,256]{1,0:T(8,128)(2,1)S(1)} %get-tuple-element.17), channel_id=1, source_target_pairs={{0,4},{1,5},{2,6},{3,7},{4,0},{5,1},{6,2},{7,3},{8,12},{9,13},{10,... | collective-permute-start | bytes 294920 | tf_op jit(solution)/shard_map/ppermute | solution.py:44
  147.7 5.5 %collective-permute-start.17 = (bf16[192,256]{1,0:T(8,128)(2,1)S(1)}, bf16[192,256]{1,0:T(8,128)(2,1)S(1)}, u32[]{:S(2)}, u32[]{:S(2)}) collective-permute-start(bf16[192,256]{1,0:T(8,128)(2,1)S(1)} %get-tuple-element.17), channel_id=1, source_target_pairs={{0,6},{1,7},{2,4},{3,5},{4,2},{5,3},{6,0},{7,1},{8,14},{9,15},{10,... | collective-permute-start | bytes 294920 | tf_op jit(solution)/shard_map/ppermute | solution.py:44
  153.2 1.8 %collective-permute-start.18 = (bf16[4,192,256]{2,1,0:T(8,128)(2,1)S(1)}, bf16[4,192,256]{2,1,0:T(8,128)(2,1)S(1)}, u32[]{:S(2)}, u32[]{:S(2)}) collective-permute-start(bf16[4,192,256]{2,1,0:T(8,128)(2,1)S(1)} %bitcast_dynamic-update-slice_fusion.4), channel_id=1, source_target_pairs={{0,1},{1,0},{2,3},{3,2},{4,5},{5,4},{6,7},{7,6},{8,9},{9,8},{10,11... | collective-permute-start | bytes 1179656 | tf_op jit(solution)/shard_map/ppermute | solution.py:44
  153.4 3.5 %collective-permute-start.40 = (bf16[4,208,384]{2,1,0:T(8,128)(2,1)S(1)}, bf16[4,208,384]{2,1,0:T(8,128)(2,1)S(1)}, u32[]{:S(2)}, u32[]{:S(2)}) collective-permute-start(bf16[4,208,384]{2,1,0:T(8,128)(2,1)S(1)} %bitcast_dynamic-update-slice_fusion), channel_id=1, source_target_pairs={{0,1},{1,0},{2,3},{3,2},{4,5},{5,4},{6,7},{7,6},{8,9},{9,8},{10,11... | collective-permute-start | bytes 1916936 | tf_op jit(solution)/shard_map/ppermute | solution.py:44
  160.3 2.8 %copy-start.12 = (f32[1,768,384]{2,1,0:T(8,128)S(1)}, f32[1,768,384]{2,1,0:T(8,128)}, u32[]{:S(2)}) copy-start(f32[1,768,384]{2,1,0:T(8,128)} %get-tuple-element.26) | copy-start | bytes 3538948
  160.3 2.8 %copy-start.13 = (f32[1,768,384]{2,1,0:T(8,128)S(1)}, f32[1,768,384]{2,1,0:T(8,128)}, u32[]{:S(2)}) copy-start(f32[1,768,384]{2,1,0:T(8,128)} %get-tuple-element.27) | copy-start | bytes 3538948
  163.1 3.4 %copy-start.1 = (bf16[384,768]{1,0:T(8,128)(2,1)S(1)}, bf16[384,768]{1,0:T(8,128)(2,1)}, u32[]{:S(2)}) copy-start(bf16[384,768]{1,0:T(8,128)(2,1)} %param.9) | copy-start | bytes 1769476

commit v2 on v0

v2 whole, which is shorter than its diff:
```python
import math

import jax
import jax.numpy as jnp
from jax import lax
from jax.experimental import pallas as pl
from jax.experimental.pallas import tpu as pltpu
from jax.sharding import PartitionSpec as P

DILATION_STEP = 8192
AXES = ("seq", "sub")
VMEM_LIMIT = 32 * 1024 * 1024
BF16, F32 = jnp.bfloat16, jnp.float32


def gelu_parts(values):
    normal_cdf = 0.5 * (1.0 + lax.erf(values * (1.0 / math.sqrt(2.0))))
    slope = normal_cdf + values * jnp.exp(-0.5 * values * values) * (1.0 / math.sqrt(2.0 * math.pi))
    return values * normal_cdf, slope


def contract_rows(left, right):
    return lax.dot_general(
        left, right, (((0,), (0,)), ((), ())), preferred_element_type=jnp.float32
    )


def times_transposed(left, right):
    return lax.dot_general(
        left, right, (((1,), (1,)), ((), ())), preferred_element_type=jnp.float32
    )


class Chain:
    def __init__(self):
        self.last = ()

    def call(self, body, outs, operands, scratch=()):
        count, earlier = len(operands), self.last

        def kernel(*refs):
            body(*refs[:count], *refs[count + len(earlier) :])

        made = pl.pallas_call(
            kernel,
            out_shape=[jax.ShapeDtypeStruct(shape, dtype) for shape, dtype in outs],
            in_specs=[pl.BlockSpec(memory_space=pltpu.VMEM)] * count
            + [pl.BlockSpec(memory_space=pl.ANY)] * len(earlier),
            out_specs=[pl.BlockSpec(memory_space=pltpu.VMEM)] * len(outs),
            scratch_shapes=list(scratch),
            compiler_params=pltpu.CompilerParams(vmem_limit_bytes=VMEM_LIMIT),
            cost_estimate=pl.CostEstimate(flops=0, bytes_accessed=0, transcendentals=0),
        )(*operands, *earlier)
        self.last = (made[0],)
        return made


def blocks_of(rows, size=256):
    def run(body):
        def step(index, carry):
            body(pl.ds(pl.multiple_of(index * size, size), size))
            return carry

        lax.fori_loop(0, rows // size, step, 0)

    return run


def dot(left, right):
    return jnp.dot(left, right, preferred_element_type=jnp.float32)


class Layout:
    def __init__(self, mesh_shape, rows):
        seq, self.sub = mesh_shape["seq"], mesh_shape["sub"]
        self.count = seq * self.sub
        self.plane = DILATION_STEP // rows
        self.blocks = self.plane // 2
        self.ring = self.count // self.plane
        self.bins = rows * self.count

    def around(self, value, steps):
        hop = steps * self.plane
        pairs = [(i, (i + hop) % self.count) for i in range(self.count)]
        return lax.ppermute(value, AXES, pairs)

    def across(self, value, mask):
        return lax.ppermute(value, AXES, [(i, i ^ mask) for i in range(self.count)])

    def along(self, value, mask):
        return self.across(value, mask * self.plane)

    def place(self):
        flat = lax.axis_index("seq") * self.sub + lax.axis_index("sub")
        return flat & 1, lax.div(flat & (self.plane - 1), 2)


LANES, EXTRA = 128, 8


class Sum:
    def __init__(self, layout, channels, units, has_exact=False):
        self.layout, self.channels, self.units = layout, channels, units
        self.part = channels // layout.plane
        self.rows = self.part * units
        self.extra = EXTRA * has_exact
        self.held_type = ((layout.blocks, self.rows + self.extra, LANES), F32)
        self.sent_type = ((self.rows + 2 * self.extra, LANES), BF16)

    def store(self, ref, at, value):
        rows = self.rows
        if not self.extra:
            ref[at] = value.astype(BF16)
            return
        ref[at + (slice(0, rows),)] = value[:rows].astype(BF16)
        high = value[rows:].astype(BF16)
        low = (value[rows:] - high.astype(F32)).astype(BF16)
        ref[at + (slice(rows, None),)] = jnp.concatenate([high, low], axis=0)

    def load(self, value):
        value = value.astype(F32)
        if not self.extra:
            return value
        rows = self.rows
        exact = value[rows : rows + EXTRA] + value[rows + EXTRA :]
        return jnp.concatenate([value[:rows], exact], axis=0)

    def split(self, tall, wide, exact, held, away):
        core, _ = self.layout.place()
        part, plane = self.part, self.layout.plane
        thin = LANES // plane

        for block in range(self.layout.blocks):
            for mine in (True, False):
                piece = 2 * block + (core if mine else 1 - core)
                at = 0
                chunks = []
                for ref in tall:
                    for low in range(0, ref.shape[1], LANES):
                        chunks.append(ref[pl.ds(pl.multiple_of(piece * part, 8), part), low : low + LANES])
                for ref in wide:
                    for top in range(0, ref.shape[0], LANES):
                        for low in range(0, self.channels, LANES):
                            chunks.append(
                                ref[pl.ds(pl.multiple_of(top + piece * thin, 8), thin), low : low + LANES]
                            )
                if self.extra:
                    chunks.append(exact[pl.ds(pl.multiple_of(piece * EXTRA, 8), EXTRA), :])
                for value in chunks:
                    size = value.shape[0]
                    if mine:
                        held[block, at : at + size, :] = value
                    elif at < self.rows:
                        away[block, at : at + size, :] = value.astype(BF16)
                    else:
                        high = value.astype(BF16)
                        low = (value - high.astype(F32)).astype(BF16)
                        away[block, at : at + 2 * size, :] = jnp.concatenate([high, low], axis=0)
                    at += size


def sent_rows(sums):
    return sum(group.sent_type[0][0] for group in sums)


def over_plane(chain, layout, sums, halves):
    blocks, rows = layout.blocks, sent_rows(sums)

    def run(*refs):
        inputs, own, sent = refs[: 2 * len(sums)], refs[2 * len(sums)], refs[2 * len(sums) + 1 :]
        _, block = layout.place()
        top = base = 0
        for group, held, away in zip(sums, inputs[::2], inputs[1::2]):
            size, mine = group.sent_type[0][0], group.held_type[0][1]
            own[base : base + mine, :] = held[block] + group.load(away[block])
            for k in range(1, blocks):
                there = block ^ k
                group.store(sent[k - 1].at[top : top + size], (), held[there] + group.load(away[there]))
            top, base = top + size, base + mine

    mine = sum(group.held_type[0][1] for group in sums)
    outs = [((mine, LANES), F32)] + [((rows, LANES), BF16)] * (blocks - 1)
    own, *sent = chain.call(run, outs, [ref for pair in halves for ref in pair])
    return [own] + [layout.across(value, 2 * k) for k, value in enumerate(sent, 1)]


def plane_sum(chain, layout, sums, parts):
    def run(own, *refs):
        away, out = refs[:-1], refs[-1]
        top = base = 0
        for group in sums:
            size, mine = group.sent_type[0][0], group.held_type[0][1]
            value = own[base : base + mine, :]
            for ref in away:
                value = value + group.load(ref[top : top + size, :])
            group.store(out.at[top : top + size], (), value)
            top, base = top + size, base + mine

    return chain.call(run, [((sent_rows(sums), LANES), BF16)], parts)[0]


def pair_sum(chain, sums, mine, arrived):
    def run(left, right, out):
        top = 0
        for group in sums:
            size = group.sent_type[0][0]
            value = group.load(left[top : top + size, :]) + group.load(right[top : top + size, :])
            group.store(out.at[top : top + size], (), value)
            top += size

    return chain.call(run, [(mine.shape, BF16)], (mine, arrived))[0]


def back_plane(layout, sent):
    return [sent] + [layout.across(sent, 2 * k) for k in range(1, layout.blocks)]


def back_core(layout, own):
    return own + [layout.across(value, 1) for value in own]


def unsplit(layout, sums, refs, tall, wide, exact):
    core, block = layout.place()
    for at, ref in enumerate(refs):
        other, k = divmod(at, layout.blocks)
        piece = 2 * (block ^ k) + (core ^ other)
        top = 0
        for number, group in enumerate(sums):
            part = group.part
            for target, low in tall[number]:
                target[pl.ds(pl.multiple_of(piece * part, 8), part), low : low + LANES] = ref[
                    top : top + part, :
                ].astype(F32)
                top += part
            thin = LANES // layout.plane
            for target, upper in wide[number]:
                for low in range(0, group.channels, LANES):
                    target[pl.ds(pl.multiple_of(upper + piece * thin, 8), thin), low : low + LANES] = ref[
                        top : top + thin, :
                    ].astype(F32)
                    top += thin
            if group.extra:
                value = ref[top : top + 2 * EXTRA, :].astype(F32)
                exact[pl.ds(pl.multiple_of(piece * EXTRA, 8), EXTRA), :] = value[:EXTRA] + value[EXTRA:]
                top += 2 * EXTRA


def solution(mesh):
    mesh_shape = dict(mesh.shape)

    def local(features, kernel, offsets, mixer, biases, cotangent):
        rows, channels = features.shape
        width = kernel.shape[2]
        layout = Layout(mesh_shape, rows)
        factor = 1.0 / math.sqrt(layout.bins)
        plane = layout.plane
        cuts = [(0, 256), (256, width)]
        chain = Chain()

        def forward_taps(source, weights, early, late, activated):
            @blocks_of(rows)
            def _(block):
                active = gelu_parts(source[block, :].astype(F32))[0].astype(BF16)
                activated[block, :] = active
                early[block, :] = dot(active, weights[0]).astype(BF16)
                late[block, :] = dot(active, weights[2]).astype(BF16)

        early, late, activated = chain.call(
            forward_taps,
            [((rows, width), BF16)] * 2 + [((rows, channels), BF16)],
            (features, kernel),
        )
        early, late = layout.around(early, 1), layout.around(late, -1)

        def local_parts(active, weights, shift, cot, mix, center, hidden_grad):
            @blocks_of(rows)
            def _(block):
                center[block, :] = dot(active[block, :], weights[1]) + shift[...]
                hidden_grad[block, :] = times_transposed(cot[block, :], mix[...])

        center, hidden_grad = chain.call(
            local_parts,
            [((rows, width), F32)] * 2,
            (activated, kernel, offsets.reshape(1, width), cotangent, mixer),
        )

        def input_slope(source, slope):
            @blocks_of(rows)
            def _(block):
                slope[block, :] = gelu_parts(source[block, :].astype(F32))[1]

        (slope_in,) = chain.call(input_slope, [((rows, channels), F32)], (features,))

        def own_grads(low, high):
            def run(center, hidden_grad, early, late, hidden, grad):
                @blocks_of(rows)
                def _(block):
                    preact = (
                        center[block, low:high]
                        + early[block, low:high].astype(F32)
                        + late[block, low:high].astype(F32)
                    )
                    value, slope = gelu_parts(preact)
                    hidden[block, :] = value.astype(BF16)
                    grad[block, :] = (hidden_grad[block, low:high] * slope).astype(BF16)

            return run

        hidden, grads, arrived = [], [], []
        for low, high in cuts:
            outs = [((rows, high - low), BF16)] * 2
            value, grad = chain.call(own_grads(low, high), outs, (center, hidden_grad, early, late))
            hidden.append(value)
            grads.append(grad)
            arrived.append((layout.around(grad, -1), layout.around(grad, 1)))

        count = len(cuts)

        def vector_sums(cot, *refs):
            grads, out = refs[:-1], refs[-1]
            sources = [(cot, low) for low in range(0, channels, LANES)]
            sources += [(ref, low) for ref in grads for low in range(0, ref.shape[1], LANES)]
            out[...] = jnp.zeros_like(out)
            for row, (ref, low) in enumerate(sources):
                value = ref[:, low : low + LANES].astype(F32)
                out[row : row + 1, :] = jnp.sum(value, axis=0, keepdims=True) * factor

        (vectors,) = chain.call(vector_sums, [((plane * EXTRA, LANES), F32)], (cotangent, *grads))

        def split_types(group):
            shape, _ = group.held_type
            return [group.held_type, (shape[:1] + group.sent_type[0], BF16)]

        def own_weights(active, cot, exact, *refs):
            hidden, grads = refs[:count], refs[count : 2 * count]
            held, away, tall, wide = refs[2 * count :]
            for (low, high), value, grad in zip(cuts, hidden, grads):
                tall[:, low:high] = contract_rows(active[...], grad[...]) * factor
                wide[low:high, :] = contract_rows(value[...], cot[...]) * factor
            own.split([tall], [wide], exact, held, away)

        own_sums = [Sum(layout, channels, 2 * width // LANES, True)]
        own = own_sums[0]
        held, away = chain.call(
            own_weights,
            split_types(own),
            (activated, cotangent, vectors, *hidden, *grads),
            [pltpu.VMEM((channels, width), F32), pltpu.VMEM((width, channels), F32)],
        )

        own_half = (held, layout.across(away, 1))

        def output_parts(source, mix, shift, weights, *refs):
            hidden, grads = refs[:count], refs[count : 2 * count]
            output, product = refs[2 * count :]

            @blocks_of(rows)
            def _(block):
                total = source[block, :].astype(F32) + shift[...]
                back = jnp.zeros((total.shape[0], channels), F32)
                for (low, high), value, grad in zip(cuts, hidden, grads):
                    total = total + dot(value[block, :], mix[low:high, :])
                    back = back + times_transposed(grad[block, :], weights[1, :, low:high])
                output[block, :] = total.astype(BF16)
                product[block, :] = back

        layer_output, product = chain.call(
            output_parts,
            [((rows, channels), BF16), ((rows, channels), F32)],
            (features, mixer, biases.reshape(1, channels), kernel, *hidden, *grads),
        )

        def side_weights(group, low, high):
            def run(active, later, earlier, held, away, first, second):
                first[...] = contract_rows(active[...], later[...]) * factor
                second[...] = contract_rows(active[...], earlier[...]) * factor
                group.split([first, second], [], None, held, away)

            return run

        def side_product(low, high, is_last):
            def run(product, later, earlier, weights, *refs):
                @blocks_of(rows)
                def _(block):
                    total = (
                        product[block, :]
                        + times_transposed(later[block, :], weights[0, :, low:high])
                        + times_transposed(earlier[block, :], weights[2, :, low:high])
                    )
                    if is_last:
                        cot, slope, out = refs
                        total = cot[block, :].astype(F32) + total * slope[block, :]
                    else:
                        (out,) = refs
                    out[block, :] = total.astype(out.dtype)

            return run

        side_sums = [Sum(layout, channels, 2 * (high - low) // LANES) for low, high in cuts]

        def start_side(at):
            low, high = cuts[at]
            return chain.call(
                side_weights(side_sums[at], low, high),
                split_types(side_sums[at]),
                (activated, *arrived[at]),
                [pltpu.VMEM((channels, high - low), F32)] * 2,
            )

        def add_side(at, product):
            low, high = cuts[at]
            is_last = high == width
            return chain.call(
                side_product(low, high, is_last),
                [((rows, channels), BF16 if is_last else F32)],
                (product, *arrived[at], kernel) + ((cotangent, slope_in) if is_last else ()),
            )[0]

        held, away = start_side(0)
        halves = [(held, layout.across(away, 1))]
        own_parts = over_plane(chain, layout, own_sums, [own_half])
        product = add_side(0, product)
        held, away = start_side(1)
        own_sent = plane_sum(chain, layout, own_sums, own_parts)
        halves.append((held, layout.across(away, 1)))
        masks = [1 << bit for bit in range(layout.ring.bit_length() - 1)]
        arrived_own = layout.along(own_sent, masks[0])
        parts = over_plane(chain, layout, side_sums, halves)
        own_sent = pair_sum(chain, own_sums, own_sent, arrived_own)
        for mask in masks[1:-1]:
            own_sent = pair_sum(chain, own_sums, own_sent, layout.along(own_sent, mask))
        arrived_own = layout.along(own_sent, masks[-1])
        input_grad = add_side(count - 1, product)
        side_sent = plane_sum(chain, layout, side_sums, parts)
        arrived_side = layout.along(side_sent, masks[0])
        own_level = back_plane(layout, pair_sum(chain, own_sums, own_sent, arrived_own))
        side_sent = pair_sum(chain, side_sums, side_sent, arrived_side)
        for mask in masks[1:]:
            side_sent = pair_sum(chain, side_sums, side_sent, layout.along(side_sent, mask))
        side_level = back_core(layout, back_plane(layout, side_sent))
        own_level = back_core(layout, own_level)

        def finish(*refs):
            each = 2 * layout.blocks
            own_refs, side_refs = refs[:each], refs[each : 2 * each]
            kernel_grad, mixer_grad, exact = refs[2 * each :]
            units = [range(low, high, LANES) for low, high in cuts]
            unsplit(
                layout,
                own_sums,
                own_refs,
                [[(kernel_grad.at[1], low) for low in range(0, width, LANES)]],
                [[(mixer_grad, low) for low in range(0, width, LANES)]],
                exact,
            )
            unsplit(
                layout,
                side_sums,
                side_refs,
                [[(kernel_grad.at[i], low) for i in (0, 2) for low in unit] for unit in units],
                [[] for unit in units],
                None,
            )

        kernel_grad, mixer_grad, vectors = chain.call(
            finish,
            [
                ((3, channels, width), F32),
                ((width, channels), F32),
                ((plane * EXTRA, LANES), F32),
            ],
            (*own_level, *side_level),
        )
        vectors = vectors.reshape(-1)
        return (
            layer_output,
            input_grad,
            kernel_grad,
            vectors[channels : channels + width],
            mixer_grad,
            vectors[:channels],
        )

    rows_split = P(AXES, None)
    return jax.shard_map(
        local,
        mesh=mesh,
        in_specs=(rows_split, P(), P(), P(), P(), rows_split),
        out_specs=(rows_split, rows_split, P(), P(), P(), P()),
        check_vma=False,
    )
```

time: 288 us -> 137 us (0.48)
  waiting for transfers between devices: 149 us -> 72.9 us
  blocking collectives: 69.3 us -> 0 us
  matrix products: 31.2 us -> 0 us
  starting transfers between devices: 8.58 us -> 32.3 us
  Pallas kernels: 0 us -> 22.3 us
  between operations: 14.2 us -> 0.84 us
  other arithmetic: 10.4 us -> 0 us
    psum x1 -> x0, waiting for transfers between devices: 83.6 us -> none  [local(): lax.psum((kernel_part, offset_part, mixer_part, biases_part), ('seq', 'su...]
    psum x1 -> x0, blocking collectives: 69.3 us -> none  [local(): lax.psum((kernel_part, offset_part, mixer_part, biases_part), ('seq', 'su...]
    dot_general x12 -> x0, matrix products: 31.2 us -> none  [the longest x4 13.1 us: times_transposed(): lax.dot_general(left, right, (((1,), (1,)), ((), ())), preferred_element_...]
    ppermute x4 -> x33, starting transfers between devices: 8.54 us -> 32.3 us  [the longest x27 20.9 us: across(): return lax.ppermute(value, AXES, [(i, i ^ mask) for i in range(self.count)])]
    pallas_call x0 -> x21, Pallas kernels: none -> 22.3 us  [call(): pl.pallas_call(kernel, out_shape=[jax.ShapeDtypeStruct(shape, dtype) for...]
    convert_element_type x1 -> x0, other arithmetic: 8.04 us -> none  [local(): activated_output = gelu_exact(inputs).astype(jnp.bfloat16)]
    ppermute x4 -> x33, waiting for transfers between devices: 65.5 us -> 72.9 us  [the longest x6 48.6 us: around(): return lax.ppermute(value, AXES, pairs)]
  transfers between devices with their start and end apart: 5 -> 33, of which waited for: 3 -> 19; matrix products, arithmetic and copies ran while one was open for 6% -> 0% of each run, Pallas kernels for 0% -> 12%
where the time goes in v2:
time: 137 us; the launch traced here: 136 us
  waiting for transfers between devices  72.9 us (53%)
  starting transfers between devices  32.3 us (24%)
  Pallas kernels  22.3 us (16%)
  local copies, waits for them, and re-layouts  7.95 us (6%)
    ppermute x6, waiting for transfers between devices, around(): return lax.ppermute(value, AXES, pairs)  48.6 us
    ppermute x27, waiting for transfers between devices, across(): return lax.ppermute(value, AXES, [(i, i ^ mask) for i in range(self.count)])  24.4 us
    pallas_call x21, Pallas kernels, call(): pl.pallas_call(kernel, out_shape=[jax.ShapeDtypeStruct(shape, dtype) for...  22.3 us
    ppermute x27, starting transfers between devices, across(): return lax.ppermute(value, AXES, [(i, i ^ mask) for i in range(self.count)])  20.9 us
    ppermute x6, starting transfers between devices, around(): return lax.ppermute(value, AXES, pairs)  11.4 us
    unnamed x20, local copies, waits for them, and re-layouts  6.77 us
  transfers between devices with their start and end apart: 33, of which 19 were waited for; matrix products, arithmetic and copies ran while one was open for 0% of the time, Pallas kernels for 12%

profile of v2, /device:TPU:0, one launch (start us, length us, event | category | flops | bytes accessed | tf_op | source)
XLA Modules:
  0.0 136.4 jit_solution(13402716770287239751)
XLA Ops:
  0.6 1.5 %copy-done = bf16[3,768,384]{2,1,0:T(8,128)(2,1)S(1)} copy-done((bf16[3,768,384]{2,1,0:T(8,128)(2,1)S(1)}, bf16[3,768,384]{2,1,0:T(8,128)(2,1)}, u32[]{:S(2)}) %copy-start) | copy-done | bytes 1769496
  2.1 1.4 %copy-done.3 = bf16[1024,768]{1,0:T(8,128)(2,1)S(1)} copy-done((bf16[1024,768]{1,0:T(8,128)(2,1)S(1)}, bf16[1024,768]{1,0:T(8,128)(2,1)}, u32[]{:S(2)}) %copy-start.3) | copy-done | bytes 1572888
  3.5 2.3 %shard_map.109 = (bf16[1024,384]{1,0:T(8,128)(2,1)S(1)}, bf16[1024,384]{1,0:T(8,128)(2,1)S(1)}, bf16[1024,768]{1,0:T(8,128)(2,1)S(1)}) custom-call(bf16[1024,768]{1,0:T(8,128)(2,1)S(1)} %copy-done.3, bf16[3,768,384]{2,1,0:T(8,128)(2,1)S(1)} %copy-done), custom_call_target="tpu_custom_call" | custom-call | tf_op jit(solution)/shard_map/pallas_call | solution.py:44
  5.9 3.1 %collective-permute-start = (bf16[1024,384]{1,0:T(8,128)(2,1)S(1)}, bf16[1024,384]{1,0:T(8,128)(2,1)S(1)}, u32[]{:S(2)}, u32[]{:S(2)}) collective-permute-start(bf16[1024,384]{1,0:T(8,128)(2,1)S(1)} %get-tuple-element.35.refs_5_), channel_id=1, source_target_pairs={{0,8},{1,9},{2,10},{3,11},{4,12},{5,13},{6,14},{7,15},{8,16},{9,17... | collective-permute-start | bytes 2359304 | tf_op jit(solution)/shard_map/ppermute | solution.py:85
  9.0 2.1 %collective-permute-start.1 = (bf16[1024,384]{1,0:T(8,128)(2,1)S(1)}, bf16[1024,384]{1,0:T(8,128)(2,1)S(1)}, u32[]{:S(2)}, u32[]{:S(2)}) collective-permute-start(bf16[1024,384]{1,0:T(8,128)(2,1)S(1)} %get-tuple-element.38), channel_id=1, source_target_pairs={{0,24},{1,25},{2,26},{3,27},{4,28},{5,29},{6,30},{7,31},{8,0},{9,1... | collective-permute-start | bytes 2359304 | tf_op jit(solution)/shard_map/ppermute | solution.py:85
  11.1 1.1 copy-done.6
  12.1 2.2 %shard_map.110 = (f32[1024,384]{1,0:T(8,128)S(1)}, f32[1024,384]{1,0:T(8,128)S(1)}) custom-call(bf16[1024,768]{1,0:T(8,128)(2,1)S(1)} %get-tuple-element.34.refs_0_, bf16[3,768,384]{2,1,0:T(8,128)(2,1)S(1)} %copy-done.1, f32[1,384]{1,0:T(1,128)S(1)} %reshape.22.refs_2_, bf16[1024,768]{1,0:T(8,128)(2,1)S(1)} %copy-done.2, bf16[384,768]{1,0:T(8,128)(2,1)S(1)} %copy-done.6, ...), custom_call_target="tpu_custom_call" | custom-call | tf_op jit(solution)/shard_map/pallas_call | solution.py:44
  14.4 1.3 shard_map.111.refs_4_.refs_5_
  15.6 13.7 %collective-permute-done.refs_2_ = bf16[1024,384]{1,0:T(8,128)(2,1)S(1)} collective-permute-done((bf16[1024,384]{1,0:T(8,128)(2,1)S(1)}, bf16[1024,384]{1,0:T(8,128)(2,1)S(1)}, u32[]{:S(2)}, u32[]{:S(2)}) %collective-permute-start) | collective-permute-done | bytes 786464 | tf_op jit(solution)/shard_map/ppermute | solution.py:85
  29.4 15.4 %collective-permute-done.1.refs_3_ = bf16[1024,384]{1,0:T(8,128)(2,1)S(1)} collective-permute-done((bf16[1024,384]{1,0:T(8,128)(2,1)S(1)}, bf16[1024,384]{1,0:T(8,128)(2,1)S(1)}, u32[]{:S(2)}, u32[]{:S(2)}) %collective-permute-start.1) | collective-permute-done | bytes 786464 | tf_op jit(solution)/shard_map/ppermute | solution.py:85
  44.8 0.7 shard_map.112
  45.5 2.4 %collective-permute-start.2 = (bf16[1024,256]{1,0:T(8,128)(2,1)S(1)}, bf16[1024,256]{1,0:T(8,128)(2,1)S(1)}, u32[]{:S(2)}, u32[]{:S(2)}) collective-permute-start(bf16[1024,256]{1,0:T(8,128)(2,1)S(1)} %get-tuple-element.41.refs_1_.refs_5_.refs_6_), channel_id=1, source_target_pairs={{0,24},{1,25},{2,26},{3,27},{4,28},{5,29},{6,30},{7,31},{8,0},{9,1... | collective-permute-start | bytes 1572872 | tf_op jit(solution)/shard_map/ppermute | solution.py:85
  47.9 0.4 shard_map.113
  48.2 0.4 shard_map.114.refs_2_.refs_7_
  48.6 2.0 %shard_map.115 = (f32[4,584,128]{2,1,0:T(8,128)S(1)}, bf16[4,592,128]{2,1,0:T(8,128)(2,1)S(1)}) custom-call(bf16[1024,768]{1,0:T(8,128)(2,1)S(1)} %get-tuple-element.34.refs_0_, bf16[1024,768]{1,0:T(8,128)(2,1)S(1)} %copy-done.2, f32[64,128]{1,0:T(8,128)S(1)} %shard_map.114.refs_2_.refs_7_, bf16[1024,256]{1,0:T(8,128)(2,1)S(1)} %get-tuple-element.39.refs_4_.refs_3_, ...), custom_call_target="tpu_custom_call" | custom-call | tf_op jit(solution)/shard_map/pallas_call | solution.py:44
  50.7 3.9 %collective-permute-start.5 = (bf16[1024,128]{1,0:T(8,128)(2,1)S(1)}, bf16[1024,128]{1,0:T(8,128)(2,1)S(1)}, u32[]{:S(2)}, u32[]{:S(2)}) collective-permute-start(bf16[1024,128]{1,0:T(8,128)(2,1)S(1)} %get-tuple-element.42.refs_2_.refs_6_.refs_7_), channel_id=1, source_target_pairs={{0,24},{1,25},{2,26},{3,27},{4,28},{5,29},{6,30},{7,31},{8,0},{9,1... | collective-permute-start | bytes 786440 | tf_op jit(solution)/shard_map/ppermute | solution.py:85
  54.6 3.4 %shard_map.116 = (bf16[1024,768]{1,0:T(8,128)(2,1)}, f32[1024,768]{1,0:T(8,128)S(1)}) custom-call(bf16[1024,768]{1,0:T(8,128)(2,1)S(1)} %copy-done.4, bf16[384,768]{1,0:T(8,128)(2,1)S(1)} %copy-done.6, f32[1,768]{1,0:T(1,128)S(1)} %reshape.21.refs_2_, bf16[3,768,384]{2,1,0:T(8,128)(2,1)S(1)} %copy-done.1, ...), custom_call_target="tpu_custom_call" | custom-call | tf_op jit(solution)/shard_map/pallas_call | solution.py:44
  58.0 12.9 %collective-permute-done.2.refs_1_ = bf16[1024,256]{1,0:T(8,128)(2,1)S(1)} collective-permute-done((bf16[1024,256]{1,0:T(8,128)(2,1)S(1)}, bf16[1024,256]{1,0:T(8,128)(2,1)S(1)}, u32[]{:S(2)}, u32[]{:S(2)}) %collective-permute-start.2) | collective-permute-done | bytes 524320 | tf_op jit(solution)/shard_map/ppermute | solution.py:85
  70.9 1.5 %collective-permute-done.3.refs_2_ = bf16[1024,256]{1,0:T(8,128)(2,1)S(1)} collective-permute-done((bf16[1024,256]{1,0:T(8,128)(2,1)S(1)}, bf16[1024,256]{1,0:T(8,128)(2,1)S(1)}, u32[]{:S(2)}, u32[]{:S(2)}) %collective-permute-start.3) | collective-permute-done | bytes 524320 | tf_op jit(solution)/shard_map/ppermute | solution.py:85
  72.4 1.4 %copy-done.7 = bf16[1024,768]{1,0:T(8,128)(2,1)S(1)} copy-done((bf16[1024,768]{1,0:T(8,128)(2,1)S(1)}, bf16[1024,768]{1,0:T(8,128)(2,1)}, u32[]{:S(2)}) %copy-start.7) | copy-done | bytes 1572888
  73.8 1.2 shard_map.117
  75.1 0.2 shard_map.118
  75.3 1.6 %shard_map.119.refs_3_.refs_0_ = f32[1024,768]{1,0:T(8,128)S(1)} custom-call(f32[1024,768]{1,0:T(8,128)S(1)} %get-tuple-element.45.refs_0_, bf16[1024,256]{1,0:T(8,128)(2,1)S(1)} %collective-permute-done.2.refs_1_, bf16[1024,256]{1,0:T(8,128)(2,1)S(1)} %collective-permute-done.3.refs_2_, bf16[3,768,384]{2,1,0:T(8,128)(2,1)S(1)} %copy-done.1, ...), custom_call_target="tpu_custom_call" | custom-call | tf_op jit(solution)/shard_map/pallas_call | solution.py:44
  76.9 0.2 collective-permute-done.5.refs_1_
  77.1 4.7 %collective-permute-done.6.refs_2_ = bf16[1024,128]{1,0:T(8,128)(2,1)S(1)} collective-permute-done((bf16[1024,128]{1,0:T(8,128)(2,1)S(1)}, bf16[1024,128]{1,0:T(8,128)(2,1)S(1)}, u32[]{:S(2)}, u32[]{:S(2)}) %collective-permute-start.6) | collective-permute-done | bytes 262176 | tf_op jit(solution)/shard_map/ppermute | solution.py:85
  81.9 1.1 shard_map.120
  83.0 1.4 collective-permute-start.7
  84.4 1.5 %collective-permute-start.8 = (bf16[592,128]{1,0:T(8,128)(2,1)S(1)}, bf16[592,128]{1,0:T(8,128)(2,1)S(1)}, u32[]{:S(2)}, u32[]{:S(2)}) collective-permute-start(bf16[592,128]{1,0:T(8,128)(2,1)S(1)} %get-tuple-element.50), channel_id=1, source_target_pairs={{0,4},{1,5},{2,6},{3,7},{4,0},{5,1},{6,2},{7,3},{8,12},{9,13},{10,... | collective-permute-start | bytes 454664 | tf_op jit(solution)/shard_map/ppermute | solution.py:88
  85.9 0.7 collective-permute-start.9
  86.6 2.8 %collective-permute-done.7.refs_1_ = bf16[592,128]{1,0:T(8,128)(2,1)S(1)} collective-permute-done((bf16[592,128]{1,0:T(8,128)(2,1)S(1)}, bf16[592,128]{1,0:T(8,128)(2,1)S(1)}, u32[]{:S(2)}, u32[]{:S(2)}) %collective-permute-start.7) | collective-permute-done | bytes 151584 | tf_op jit(solution)/shard_map/ppermute | solution.py:88
  89.4 1.8 %collective-permute-done.8.refs_2_ = bf16[592,128]{1,0:T(8,128)(2,1)S(1)} collective-permute-done((bf16[592,128]{1,0:T(8,128)(2,1)S(1)}, bf16[592,128]{1,0:T(8,128)(2,1)S(1)}, u32[]{:S(2)}, u32[]{:S(2)}) %collective-permute-start.8) | collective-permute-done | bytes 151584 | tf_op jit(solution)/shard_map/ppermute | solution.py:88
  91.2 2.6 %collective-permute-done.9.refs_3_ = bf16[592,128]{1,0:T(8,128)(2,1)S(1)} collective-permute-done((bf16[592,128]{1,0:T(8,128)(2,1)S(1)}, bf16[592,128]{1,0:T(8,128)(2,1)S(1)}, u32[]{:S(2)}, u32[]{:S(2)}) %collective-permute-start.9) | collective-permute-done | bytes 151584 | tf_op jit(solution)/shard_map/ppermute | solution.py:88
  93.8 0.1 shard_map.121.refs_4_.refs_0_
  93.9 1.2 collective-permute-start.10
  95.1 0.1 shard_map.122
  95.2 1.6 %collective-permute-start.14 = (bf16[576,128]{1,0:T(8,128)(2,1)S(1)}, bf16[576,128]{1,0:T(8,128)(2,1)S(1)}, u32[]{:S(2)}, u32[]{:S(2)}) collective-permute-start(bf16[576,128]{1,0:T(8,128)(2,1)S(1)} %get-tuple-element.56), channel_id=1, source_target_pairs={{0,2},{1,3},{2,0},{3,1},{4,6},{5,7},{6,4},{7,5},{8,10},{9,11},{10,... | collective-permute-start | bytes 442376 | tf_op jit(solution)/shard_map/ppermute | solution.py:88
  96.8 1.5 %collective-permute-start.15 = (bf16[576,128]{1,0:T(8,128)(2,1)S(1)}, bf16[576,128]{1,0:T(8,128)(2,1)S(1)}, u32[]{:S(2)}, u32[]{:S(2)}) collective-permute-start(bf16[576,128]{1,0:T(8,128)(2,1)S(1)} %get-tuple-element.57), channel_id=1, source_target_pairs={{0,4},{1,5},{2,6},{3,7},{4,0},{5,1},{6,2},{7,3},{8,12},{9,13},{10,... | collective-permute-start | bytes 442376 | tf_op jit(solution)/shard_map/ppermute | solution.py:88
  98.3 0.5 collective-permute-start.16
  98.8 0.4 collective-permute-done.10.refs_1_
  99.2 2.0 %collective-permute-start.13 = (bf16[592,128]{1,0:T(8,128)(2,1)S(1)}, bf16[592,128]{1,0:T(8,128)(2,1)S(1)}, u32[]{:S(2)}, u32[]{:S(2)}) collective-permute-start(bf16[592,128]{1,0:T(8,128)(2,1)S(1)} %shard_map.123.refs_6_.refs_0_), channel_id=1, source_target_pairs={{0,16},{1,17},{2,18},{3,19},{4,20},{5,21},{6,22},{7,23},{8,24},{9,... | collective-permute-start | bytes 454664 | tf_op jit(solution)/shard_map/ppermute | solution.py:88
  101.2 2.7 %shard_map.124.refs_4_ = bf16[1024,768]{1,0:T(8,128)(2,1)} custom-call(f32[1024,768]{1,0:T(8,128)S(1)} %shard_map.119.refs_3_.refs_0_, bf16[1024,128]{1,0:T(8,128)(2,1)S(1)} %collective-permute-done.5.refs_1_, bf16[1024,128]{1,0:T(8,128)(2,1)S(1)} %collective-permute-done.6.refs_2_, bf16[3,768,384]{2,1,0:T(8,128)(2,1)S(1)} %copy-done.1, ...), custom_call_target="tpu_custom_call" | custom-call | tf_op jit(solution)/shard_map/pallas_call | solution.py:44
  103.9 1.1 collective-permute-done.16.refs_3_
  105.0 1.4 %copy-done.5 = bf16[1024,768]{1,0:T(8,128)(2,1)S(1)} copy-done((bf16[1024,768]{1,0:T(8,128)(2,1)S(1)}, bf16[1024,768]{1,0:T(8,128)(2,1)}, u32[]{:S(2)}) %copy-start.5) | copy-done | bytes 1572888
  106.5 0.7 collective-permute-start.24
  107.3 0.2 collective-permute-done.13.refs_1_
  107.5 1.5 %collective-permute-start.17 = (bf16[592,128]{1,0:T(8,128)(2,1)S(1)}, bf16[592,128]{1,0:T(8,128)(2,1)S(1)}, u32[]{:S(2)}, u32[]{:S(2)}) collective-permute-start(bf16[592,128]{1,0:T(8,128)(2,1)S(1)} %shard_map.126.refs_2_.refs_0_), channel_id=1, source_target_pairs={{0,2},{1,3},{2,0},{3,1},{4,6},{5,7},{6,4},{7,5},{8,10},{9,11},{10,... | collective-permute-start | bytes 454664 | tf_op jit(solution)/shard_map/ppermute | solution.py:88
  109.0 1.5 %collective-permute-start.18 = (bf16[592,128]{1,0:T(8,128)(2,1)S(1)}, bf16[592,128]{1,0:T(8,128)(2,1)S(1)}, u32[]{:S(2)}, u32[]{:S(2)}) collective-permute-start(bf16[592,128]{1,0:T(8,128)(2,1)S(1)} %shard_map.126.refs_2_.refs_0_), channel_id=1, source_target_pairs={{0,4},{1,5},{2,6},{3,7},{4,0},{5,1},{6,2},{7,3},{8,12},{9,13},{10,... | collective-permute-start | bytes 454664 | tf_op jit(solution)/shard_map/ppermute | solution.py:88
  110.4 0.6 collective-permute-start.19
  111.0 0.7 collective-permute-done.24.refs_1_
  111.8 1.5 %collective-permute-start.25 = (bf16[576,128]{1,0:T(8,128)(2,1)S(1)}, bf16[576,128]{1,0:T(8,128)(2,1)S(1)}, u32[]{:S(2)}, u32[]{:S(2)}) collective-permute-start(bf16[576,128]{1,0:T(8,128)(2,1)S(1)} %shard_map.127.refs_0_.refs_2_), channel_id=1, source_target_pairs={{0,16},{1,17},{2,18},{3,19},{4,20},{5,21},{6,22},{7,23},{8,24},{9,... | collective-permute-start | bytes 442376 | tf_op jit(solution)/shard_map/ppermute | solution.py:88
  113.3 1.1 collective-permute-done.17.refs_1_
  114.4 0.5 collective-permute-start.22
  114.9 6.6 %collective-permute-done.25.refs_1_ = bf16[576,128]{1,0:T(8,128)(2,1)S(1)} collective-permute-done((bf16[576,128]{1,0:T(8,128)(2,1)S(1)}, bf16[576,128]{1,0:T(8,128)(2,1)S(1)}, u32[]{:S(2)}, u32[]{:S(2)}) %collective-permute-start.25) | collective-permute-done | bytes 147488 | tf_op jit(solution)/shard_map/ppermute | solution.py:88
  121.5 1.5 %collective-permute-start.26 = (bf16[576,128]{1,0:T(8,128)(2,1)S(1)}, bf16[576,128]{1,0:T(8,128)(2,1)S(1)}, u32[]{:S(2)}, u32[]{:S(2)}) collective-permute-start(bf16[576,128]{1,0:T(8,128)(2,1)S(1)} %shard_map.128.refs_8_.refs_16_), channel_id=1, source_target_pairs={{0,2},{1,3},{2,0},{3,1},{4,6},{5,7},{6,4},{7,5},{8,10},{9,11},{10,... | collective-permute-start | bytes 442376 | tf_op jit(solution)/shard_map/ppermute | solution.py:88
  123.0 1.5 %collective-permute-start.27 = (bf16[576,128]{1,0:T(8,128)(2,1)S(1)}, bf16[576,128]{1,0:T(8,128)(2,1)S(1)}, u32[]{:S(2)}, u32[]{:S(2)}) collective-permute-start(bf16[576,128]{1,0:T(8,128)(2,1)S(1)} %shard_map.128.refs_8_.refs_16_), channel_id=1, source_target_pairs={{0,4},{1,5},{2,6},{3,7},{4,0},{5,1},{6,2},{7,3},{8,12},{9,13},{10,... | collective-permute-start | bytes 442376 | tf_op jit(solution)/shard_map/ppermute | solution.py:88
  124.5 0.6 collective-permute-start.28
  125.1 0.5 collective-permute-start.29
  125.6 1.2 collective-permute-done.26.refs_9_
  126.8 2.9 %collective-permute-done.27.refs_10_ = bf16[576,128]{1,0:T(8,128)(2,1)S(1)} collective-permute-done((bf16[576,128]{1,0:T(8,128)(2,1)S(1)}, bf16[576,128]{1,0:T(8,128)(2,1)S(1)}, u32[]{:S(2)}, u32[]{:S(2)}) %collective-permute-start.27) | collective-permute-done | bytes 147488 | tf_op jit(solution)/shard_map/ppermute | solution.py:88
  129.8 1.6 %collective-permute-done.28.refs_11_ = bf16[576,128]{1,0:T(8,128)(2,1)S(1)} collective-permute-done((bf16[576,128]{1,0:T(8,128)(2,1)S(1)}, bf16[576,128]{1,0:T(8,128)(2,1)S(1)}, u32[]{:S(2)}, u32[]{:S(2)}) %collective-permute-start.28) | collective-permute-done | bytes 147488 | tf_op jit(solution)/shard_map/ppermute | solution.py:88
  131.4 1.3 collective-permute-done.32.refs_15_
  132.7 2.5 %shard_map.129 = (f32[3,768,384]{2,1,0:T(8,128)}, f32[384,768]{1,0:T(8,128)}, f32[64,128]{1,0:T(8,128)S(1)}) custom-call(bf16[592,128]{1,0:T(8,128)(2,1)S(1)} %shard_map.126.refs_2_.refs_0_, bf16[592,128]{1,0:T(8,128)(2,1)S(1)} %collective-permute-done.17.refs_1_, bf16[592,128]{1,0:T(8,128)(2,1)S(1)} %collective-permute-done.18.refs_2_, ...), custom_call_target="tpu_custom_call" | custom-call | tf_op jit(solution)/shard_map/pallas_call | solution.py:44
  135.2 0.6 slice_bitcast_fusion
  135.8 0.6 slice_bitcast_fusion.1
  (47 shorter events, 0.6 us)
Async XLA Ops:
  0.6 1.5 %copy-start = (bf16[3,768,384]{2,1,0:T(8,128)(2,1)S(1)}, bf16[3,768,384]{2,1,0:T(8,128)(2,1)}, u32[]{:S(2)}) copy-start(bf16[3,768,384]{2,1,0:T(8,128)(2,1)} %refs_3_.7) | copy-start | bytes 5308420
  2.1 1.4 %copy-start.3 = (bf16[1024,768]{1,0:T(8,128)(2,1)S(1)}, bf16[1024,768]{1,0:T(8,128)(2,1)}, u32[]{:S(2)}) copy-start(bf16[1024,768]{1,0:T(8,128)(2,1)} %refs_0_.7) | copy-start | bytes 4718596
  3.5 7.5 %copy-start.9 = (f32[384]{0:T(512)S(1)}, f32[384]{0:T(512)}, u32[]{:S(2)}) copy-start(f32[384]{0:T(512)} %param.8) | copy-start | bytes 4612
  3.5 7.5 %copy-start.1 = (bf16[3,768,384]{2,1,0:T(8,128)(2,1)S(1)}, bf16[3,768,384]{2,1,0:T(8,128)(2,1)}, u32[]{:S(2)}) copy-start(bf16[3,768,384]{2,1,0:T(8,128)(2,1)} %refs_3_.7) | copy-start | bytes 5308420
  3.5 7.5 %copy-start.2 = (bf16[1024,768]{1,0:T(8,128)(2,1)S(1)}, bf16[1024,768]{1,0:T(8,128)(2,1)}, u32[]{:S(2)}) copy-start(bf16[1024,768]{1,0:T(8,128)(2,1)} %refs_4_.3) | copy-start | bytes 4718596
  5.9 23.5 %collective-permute-start = (bf16[1024,384]{1,0:T(8,128)(2,1)S(1)}, bf16[1024,384]{1,0:T(8,128)(2,1)S(1)}, u32[]{:S(2)}, u32[]{:S(2)}) collective-permute-start(bf16[1024,384]{1,0:T(8,128)(2,1)S(1)} %get-tuple-element.35.refs_5_), channel_id=1, source_target_pairs={{0,8},{1,9},{2,10},{3,11},{4,12},{5,13},{6,14},{7,15},{8,16},{9,17... | collective-permute-start | bytes 2359304 | tf_op jit(solution)/shard_map/ppermute | solution.py:85
  9.0 35.9 %collective-permute-start.1 = (bf16[1024,384]{1,0:T(8,128)(2,1)S(1)}, bf16[1024,384]{1,0:T(8,128)(2,1)S(1)}, u32[]{:S(2)}, u32[]{:S(2)}) collective-permute-start(bf16[1024,384]{1,0:T(8,128)(2,1)S(1)} %get-tuple-element.38), channel_id=1, source_target_pairs={{0,24},{1,25},{2,26},{3,27},{4,28},{5,29},{6,30},{7,31},{8,0},{9,1... | collective-permute-start | bytes 2359304 | tf_op jit(solution)/shard_map/ppermute | solution.py:85
  11.1 1.1 copy-start.6
  45.5 25.4 %collective-permute-start.2 = (bf16[1024,256]{1,0:T(8,128)(2,1)S(1)}, bf16[1024,256]{1,0:T(8,128)(2,1)S(1)}, u32[]{:S(2)}, u32[]{:S(2)}) collective-permute-start(bf16[1024,256]{1,0:T(8,128)(2,1)S(1)} %get-tuple-element.41.refs_1_.refs_5_.refs_6_), channel_id=1, source_target_pairs={{0,24},{1,25},{2,26},{3,27},{4,28},{5,29},{6,30},{7,31},{8,0},{9,1... | collective-permute-start | bytes 1572872 | tf_op jit(solution)/shard_map/ppermute | solution.py:85
  47.9 24.6 %collective-permute-start.3 = (bf16[1024,256]{1,0:T(8,128)(2,1)S(1)}, bf16[1024,256]{1,0:T(8,128)(2,1)S(1)}, u32[]{:S(2)}, u32[]{:S(2)}) collective-permute-start(bf16[1024,256]{1,0:T(8,128)(2,1)S(1)} %get-tuple-element.41.refs_1_.refs_5_.refs_6_), channel_id=1, source_target_pairs={{0,8},{1,9},{2,10},{3,11},{4,12},{5,13},{6,14},{7,15},{8,16},{9,17... | collective-permute-start | bytes 1572872 | tf_op jit(solution)/shard_map/ppermute | solution.py:85
  48.6 6.0 %copy-start.8 = (f32[768]{0:T(1024)S(1)}, f32[768]{0:T(1024)}, u32[]{:S(2)}) copy-start(f32[768]{0:T(1024)} %param.10) | copy-start | bytes 9220
  48.6 6.0 %copy-start.4 = (bf16[1024,768]{1,0:T(8,128)(2,1)S(1)}, bf16[1024,768]{1,0:T(8,128)(2,1)}, u32[]{:S(2)}) copy-start(bf16[1024,768]{1,0:T(8,128)(2,1)} %refs_0_.7) | copy-start | bytes 4718596
  50.7 24.5 %collective-permute-start.4 = (bf16[4,592,128]{2,1,0:T(8,128)(2,1)S(1)}, bf16[4,592,128]{2,1,0:T(8,128)(2,1)S(1)}, u32[]{:S(2)}, u32[]{:S(2)}) collective-permute-start(bf16[4,592,128]{2,1,0:T(8,128)(2,1)S(1)} %get-tuple-element.46), channel_id=1, source_target_pairs={{0,1},{1,0},{2,3},{3,2},{4,5},{5,4},{6,7},{7,6},{8,9},{9,8},{10,11... | collective-permute-start | bytes 1818632 | tf_op jit(solution)/shard_map/ppermute | solution.py:88
  50.7 26.4 %collective-permute-start.5 = (bf16[1024,128]{1,0:T(8,128)(2,1)S(1)}, bf16[1024,128]{1,0:T(8,128)(2,1)S(1)}, u32[]{:S(2)}, u32[]{:S(2)}) collective-permute-start(bf16[1024,128]{1,0:T(8,128)(2,1)S(1)} %get-tuple-element.42.refs_2_.refs_6_.refs_7_), channel_id=1, source_target_pairs={{0,24},{1,25},{2,26},{3,27},{4,28},{5,29},{6,30},{7,31},{8,0},{9,1... | collective-permute-start | bytes 786440 | tf_op jit(solution)/shard_map/ppermute | solution.py:85
  54.6 27.3 %collective-permute-start.6 = (bf16[1024,128]{1,0:T(8,128)(2,1)S(1)}, bf16[1024,128]{1,0:T(8,128)(2,1)S(1)}, u32[]{:S(2)}, u32[]{:S(2)}) collective-permute-start(bf16[1024,128]{1,0:T(8,128)(2,1)S(1)} %get-tuple-element.42.refs_2_.refs_6_.refs_7_), channel_id=1, source_target_pairs={{0,8},{1,9},{2,10},{3,11},{4,12},{5,13},{6,14},{7,15},{8,16},{9,17... | collective-permute-start | bytes 786440 | tf_op jit(solution)/shard_map/ppermute | solution.py:85
  72.4 1.4 %copy-start.7 = (bf16[1024,768]{1,0:T(8,128)(2,1)S(1)}, bf16[1024,768]{1,0:T(8,128)(2,1)}, u32[]{:S(2)}) copy-start(bf16[1024,768]{1,0:T(8,128)(2,1)} %get-tuple-element.28.refs_3_) | copy-start | bytes 4718596
  75.0 20.1 %collective-permute-start.11 = (bf16[4,384,128]{2,1,0:T(8,128)(2,1)S(1)}, bf16[4,384,128]{2,1,0:T(8,128)(2,1)S(1)}, u32[]{:S(2)}, u32[]{:S(2)}) collective-permute-start(bf16[4,384,128]{2,1,0:T(8,128)(2,1)S(1)} %get-tuple-element.53), channel_id=1, source_target_pairs={{0,1},{1,0},{2,3},{3,2},{4,5},{5,4},{6,7},{7,6},{8,9},{9,8},{10,11... | collective-permute-start | bytes 1179656 | tf_op jit(solution)/shard_map/ppermute | solution.py:88
  83.0 12.2 %collective-permute-start.12 = (bf16[4,192,128]{2,1,0:T(8,128)(2,1)S(1)}, bf16[4,192,128]{2,1,0:T(8,128)(2,1)S(1)}, u32[]{:S(2)}, u32[]{:S(2)}) collective-permute-start(bf16[4,192,128]{2,1,0:T(8,128)(2,1)S(1)} %get-tuple-element.54), channel_id=1, source_target_pairs={{0,1},{1,0},{2,3},{3,2},{4,5},{5,4},{6,7},{7,6},{8,9},{9,8},{10,11... | collective-permute-start | bytes 589832 | tf_op jit(solution)/shard_map/ppermute | solution.py:88
  83.0 6.4 %collective-permute-start.7 = (bf16[592,128]{1,0:T(8,128)(2,1)S(1)}, bf16[592,128]{1,0:T(8,128)(2,1)S(1)}, u32[]{:S(2)}, u32[]{:S(2)}) collective-permute-start(bf16[592,128]{1,0:T(8,128)(2,1)S(1)} %get-tuple-element.49), channel_id=1, source_target_pairs={{0,2},{1,3},{2,0},{3,1},{4,6},{5,7},{6,4},{7,5},{8,10},{9,11},{10,... | collective-permute-start | bytes 454664 | tf_op jit(solution)/shard_map/ppermute | solution.py:88
  84.4 6.8 %collective-permute-start.8 = (bf16[592,128]{1,0:T(8,128)(2,1)S(1)}, bf16[592,128]{1,0:T(8,128)(2,1)S(1)}, u32[]{:S(2)}, u32[]{:S(2)}) collective-permute-start(bf16[592,128]{1,0:T(8,128)(2,1)S(1)} %get-tuple-element.50), channel_id=1, source_target_pairs={{0,4},{1,5},{2,6},{3,7},{4,0},{5,1},{6,2},{7,3},{8,12},{9,13},{10,... | collective-permute-start | bytes 454664 | tf_op jit(solution)/shard_map/ppermute | solution.py:88
  85.9 7.9 %collective-permute-start.9 = (bf16[592,128]{1,0:T(8,128)(2,1)S(1)}, bf16[592,128]{1,0:T(8,128)(2,1)S(1)}, u32[]{:S(2)}, u32[]{:S(2)}) collective-permute-start(bf16[592,128]{1,0:T(8,128)(2,1)S(1)} %get-tuple-element.51), channel_id=1, source_target_pairs={{0,6},{1,7},{2,4},{3,5},{4,2},{5,3},{6,0},{7,1},{8,14},{9,15},{10,... | collective-permute-start | bytes 454664 | tf_op jit(solution)/shard_map/ppermute | solution.py:88
  93.9 5.3 %collective-permute-start.10 = (bf16[592,128]{1,0:T(8,128)(2,1)S(1)}, bf16[592,128]{1,0:T(8,128)(2,1)S(1)}, u32[]{:S(2)}, u32[]{:S(2)}) collective-permute-start(bf16[592,128]{1,0:T(8,128)(2,1)S(1)} %shard_map.121.refs_4_.refs_0_), channel_id=1, source_target_pairs={{0,8},{1,9},{2,10},{3,11},{4,12},{5,13},{6,14},{7,15},{8,0},{9,1},... | collective-permute-start | bytes 454664 | tf_op jit(solution)/shard_map/ppermute | solution.py:88
  95.2 8.7 %collective-permute-start.14 = (bf16[576,128]{1,0:T(8,128)(2,1)S(1)}, bf16[576,128]{1,0:T(8,128)(2,1)S(1)}, u32[]{:S(2)}, u32[]{:S(2)}) collective-permute-start(bf16[576,128]{1,0:T(8,128)(2,1)S(1)} %get-tuple-element.56), channel_id=1, source_target_pairs={{0,2},{1,3},{2,0},{3,1},{4,6},{5,7},{6,4},{7,5},{8,10},{9,11},{10,... | collective-permute-start | bytes 442376 | tf_op jit(solution)/shard_map/ppermute | solution.py:88
  96.8 7.1 %collective-permute-start.15 = (bf16[576,128]{1,0:T(8,128)(2,1)S(1)}, bf16[576,128]{1,0:T(8,128)(2,1)S(1)}, u32[]{:S(2)}, u32[]{:S(2)}) collective-permute-start(bf16[576,128]{1,0:T(8,128)(2,1)S(1)} %get-tuple-element.57), channel_id=1, source_target_pairs={{0,4},{1,5},{2,6},{3,7},{4,0},{5,1},{6,2},{7,3},{8,12},{9,13},{10,... | collective-permute-start | bytes 442376 | tf_op jit(solution)/shard_map/ppermute | solution.py:88
  98.3 6.7 %collective-permute-start.16 = (bf16[576,128]{1,0:T(8,128)(2,1)S(1)}, bf16[576,128]{1,0:T(8,128)(2,1)S(1)}, u32[]{:S(2)}, u32[]{:S(2)}) collective-permute-start(bf16[576,128]{1,0:T(8,128)(2,1)S(1)} %get-tuple-element.58), channel_id=1, source_target_pairs={{0,6},{1,7},{2,4},{3,5},{4,2},{5,3},{6,0},{7,1},{8,14},{9,15},{10,... | collective-permute-start | bytes 442376 | tf_op jit(solution)/shard_map/ppermute | solution.py:88
  99.2 8.2 %collective-permute-start.13 = (bf16[592,128]{1,0:T(8,128)(2,1)S(1)}, bf16[592,128]{1,0:T(8,128)(2,1)S(1)}, u32[]{:S(2)}, u32[]{:S(2)}) collective-permute-start(bf16[592,128]{1,0:T(8,128)(2,1)S(1)} %shard_map.123.refs_6_.refs_0_), channel_id=1, source_target_pairs={{0,16},{1,17},{2,18},{3,19},{4,20},{5,21},{6,22},{7,23},{8,24},{9,... | collective-permute-start | bytes 454664 | tf_op jit(solution)/shard_map/ppermute | solution.py:88
  105.0 1.4 %copy-start.5 = (bf16[1024,768]{1,0:T(8,128)(2,1)S(1)}, bf16[1024,768]{1,0:T(8,128)(2,1)}, u32[]{:S(2)}) copy-start(bf16[1024,768]{1,0:T(8,128)(2,1)} %shard_map.124.refs_4_) | copy-start | bytes 4718596
  106.5 5.2 %collective-permute-start.24 = (bf16[576,128]{1,0:T(8,128)(2,1)S(1)}, bf16[576,128]{1,0:T(8,128)(2,1)S(1)}, u32[]{:S(2)}, u32[]{:S(2)}) collective-permute-start(bf16[576,128]{1,0:T(8,128)(2,1)S(1)} %shard_map.125.refs_2_.refs_0_), channel_id=1, source_target_pairs={{0,8},{1,9},{2,10},{3,11},{4,12},{5,13},{6,14},{7,15},{8,0},{9,1},... | collective-permute-start | bytes 442376 | tf_op jit(solution)/shard_map/ppermute | solution.py:88
  107.5 6.9 %collective-permute-start.17 = (bf16[592,128]{1,0:T(8,128)(2,1)S(1)}, bf16[592,128]{1,0:T(8,128)(2,1)S(1)}, u32[]{:S(2)}, u32[]{:S(2)}) collective-permute-start(bf16[592,128]{1,0:T(8,128)(2,1)S(1)} %shard_map.126.refs_2_.refs_0_), channel_id=1, source_target_pairs={{0,2},{1,3},{2,0},{3,1},{4,6},{5,7},{6,4},{7,5},{8,10},{9,11},{10,... | collective-permute-start | bytes 454664 | tf_op jit(solution)/shard_map/ppermute | solution.py:88
  109.0 5.4 %collective-permute-start.18 = (bf16[592,128]{1,0:T(8,128)(2,1)S(1)}, bf16[592,128]{1,0:T(8,128)(2,1)S(1)}, u32[]{:S(2)}, u32[]{:S(2)}) collective-permute-start(bf16[592,128]{1,0:T(8,128)(2,1)S(1)} %shard_map.126.refs_2_.refs_0_), channel_id=1, source_target_pairs={{0,4},{1,5},{2,6},{3,7},{4,0},{5,1},{6,2},{7,3},{8,12},{9,13},{10,... | collective-permute-start | bytes 454664 | tf_op jit(solution)/shard_map/ppermute | solution.py:88
  110.4 12.5 %collective-permute-start.19 = (bf16[592,128]{1,0:T(8,128)(2,1)S(1)}, bf16[592,128]{1,0:T(8,128)(2,1)S(1)}, u32[]{:S(2)}, u32[]{:S(2)}) collective-permute-start(bf16[592,128]{1,0:T(8,128)(2,1)S(1)} %shard_map.126.refs_2_.refs_0_), channel_id=1, source_target_pairs={{0,6},{1,7},{2,4},{3,5},{4,2},{5,3},{6,0},{7,1},{8,14},{9,15},{10,... | collective-permute-start | bytes 454664 | tf_op jit(solution)/shard_map/ppermute | solution.py:88
  111.0 13.4 %collective-permute-start.20 = (bf16[592,128]{1,0:T(8,128)(2,1)S(1)}, bf16[592,128]{1,0:T(8,128)(2,1)S(1)}, u32[]{:S(2)}, u32[]{:S(2)}) collective-permute-start(bf16[592,128]{1,0:T(8,128)(2,1)S(1)} %shard_map.126.refs_2_.refs_0_), channel_id=1, source_target_pairs={{0,1},{1,0},{2,3},{3,2},{4,5},{5,4},{6,7},{7,6},{8,9},{9,8},{10,11... | collective-permute-start | bytes 454664 | tf_op jit(solution)/shard_map/ppermute | solution.py:88
  111.8 9.7 %collective-permute-start.25 = (bf16[576,128]{1,0:T(8,128)(2,1)S(1)}, bf16[576,128]{1,0:T(8,128)(2,1)S(1)}, u32[]{:S(2)}, u32[]{:S(2)}) collective-permute-start(bf16[576,128]{1,0:T(8,128)(2,1)S(1)} %shard_map.127.refs_0_.refs_2_), channel_id=1, source_target_pairs={{0,16},{1,17},{2,18},{3,19},{4,20},{5,21},{6,22},{7,23},{8,24},{9,... | collective-permute-start | bytes 442376 | tf_op jit(solution)/shard_map/ppermute | solution.py:88
  114.4 10.7 %collective-permute-start.21 = (bf16[592,128]{1,0:T(8,128)(2,1)S(1)}, bf16[592,128]{1,0:T(8,128)(2,1)S(1)}, u32[]{:S(2)}, u32[]{:S(2)}) collective-permute-start(bf16[592,128]{1,0:T(8,128)(2,1)S(1)} %collective-permute-done.17.refs_1_), channel_id=1, source_target_pairs={{0,1},{1,0},{2,3},{3,2},{4,5},{5,4},{6,7},{7,6},{8,9},{9,8},{10,11... | collective-permute-start | bytes 454664 | tf_op jit(solution)/shard_map/ppermute | solution.py:88
  114.4 10.7 %collective-permute-start.22 = (bf16[592,128]{1,0:T(8,128)(2,1)S(1)}, bf16[592,128]{1,0:T(8,128)(2,1)S(1)}, u32[]{:S(2)}, u32[]{:S(2)}) collective-permute-start(bf16[592,128]{1,0:T(8,128)(2,1)S(1)} %collective-permute-done.18.refs_2_), channel_id=1, source_target_pairs={{0,1},{1,0},{2,3},{3,2},{4,5},{5,4},{6,7},{7,6},{8,9},{9,8},{10,11... | collective-permute-start | bytes 454664 | tf_op jit(solution)/shard_map/ppermute | solution.py:88
  121.5 5.3 %collective-permute-start.26 = (bf16[576,128]{1,0:T(8,128)(2,1)S(1)}, bf16[576,128]{1,0:T(8,128)(2,1)S(1)}, u32[]{:S(2)}, u32[]{:S(2)}) collective-permute-start(bf16[576,128]{1,0:T(8,128)(2,1)S(1)} %shard_map.128.refs_8_.refs_16_), channel_id=1, source_target_pairs={{0,2},{1,3},{2,0},{3,1},{4,6},{5,7},{6,4},{7,5},{8,10},{9,11},{10,... | collective-permute-start | bytes 442376 | tf_op jit(solution)/shard_map/ppermute | solution.py:88
  123.0 6.8 %collective-permute-start.27 = (bf16[576,128]{1,0:T(8,128)(2,1)S(1)}, bf16[576,128]{1,0:T(8,128)(2,1)S(1)}, u32[]{:S(2)}, u32[]{:S(2)}) collective-permute-start(bf16[576,128]{1,0:T(8,128)(2,1)S(1)} %shard_map.128.refs_8_.refs_16_), channel_id=1, source_target_pairs={{0,4},{1,5},{2,6},{3,7},{4,0},{5,1},{6,2},{7,3},{8,12},{9,13},{10,... | collective-permute-start | bytes 442376 | tf_op jit(solution)/shard_map/ppermute | solution.py:88
  124.5 6.9 %collective-permute-start.28 = (bf16[576,128]{1,0:T(8,128)(2,1)S(1)}, bf16[576,128]{1,0:T(8,128)(2,1)S(1)}, u32[]{:S(2)}, u32[]{:S(2)}) collective-permute-start(bf16[576,128]{1,0:T(8,128)(2,1)S(1)} %shard_map.128.refs_8_.refs_16_), channel_id=1, source_target_pairs={{0,6},{1,7},{2,4},{3,5},{4,2},{5,3},{6,0},{7,1},{8,14},{9,15},{10,... | collective-permute-start | bytes 442376 | tf_op jit(solution)/shard_map/ppermute | solution.py:88
  125.1 6.3 %collective-permute-start.23 = (bf16[592,128]{1,0:T(8,128)(2,1)S(1)}, bf16[592,128]{1,0:T(8,128)(2,1)S(1)}, u32[]{:S(2)}, u32[]{:S(2)}) collective-permute-start(bf16[592,128]{1,0:T(8,128)(2,1)S(1)} %collective-permute-done.19.refs_3_), channel_id=1, source_target_pairs={{0,1},{1,0},{2,3},{3,2},{4,5},{5,4},{6,7},{7,6},{8,9},{9,8},{10,11... | collective-permute-start | bytes 454664 | tf_op jit(solution)/shard_map/ppermute | solution.py:88
  125.1 6.3 %collective-permute-start.29 = (bf16[576,128]{1,0:T(8,128)(2,1)S(1)}, bf16[576,128]{1,0:T(8,128)(2,1)S(1)}, u32[]{:S(2)}, u32[]{:S(2)}) collective-permute-start(bf16[576,128]{1,0:T(8,128)(2,1)S(1)} %shard_map.128.refs_8_.refs_16_), channel_id=1, source_target_pairs={{0,1},{1,0},{2,3},{3,2},{4,5},{5,4},{6,7},{7,6},{8,9},{9,8},{10,11... | collective-permute-start | bytes 442376 | tf_op jit(solution)/shard_map/ppermute | solution.py:88
  126.8 4.5 %collective-permute-start.30 = (bf16[576,128]{1,0:T(8,128)(2,1)S(1)}, bf16[576,128]{1,0:T(8,128)(2,1)S(1)}, u32[]{:S(2)}, u32[]{:S(2)}) collective-permute-start(bf16[576,128]{1,0:T(8,128)(2,1)S(1)} %collective-permute-done.26.refs_9_), channel_id=1, source_target_pairs={{0,1},{1,0},{2,3},{3,2},{4,5},{5,4},{6,7},{7,6},{8,9},{9,8},{10,11... | collective-permute-start | bytes 442376 | tf_op jit(solution)/shard_map/ppermute | solution.py:88
  129.8 1.6 %collective-permute-start.31 = (bf16[576,128]{1,0:T(8,128)(2,1)S(1)}, bf16[576,128]{1,0:T(8,128)(2,1)S(1)}, u32[]{:S(2)}, u32[]{:S(2)}) collective-permute-start(bf16[576,128]{1,0:T(8,128)(2,1)S(1)} %collective-permute-done.27.refs_10_), channel_id=1, source_target_pairs={{0,1},{1,0},{2,3},{3,2},{4,5},{5,4},{6,7},{7,6},{8,9},{9,8},{10,11... | collective-permute-start | bytes 442376 | tf_op jit(solution)/shard_map/ppermute | solution.py:88
  131.4 1.4 %collective-permute-start.32 = (bf16[576,128]{1,0:T(8,128)(2,1)S(1)}, bf16[576,128]{1,0:T(8,128)(2,1)S(1)}, u32[]{:S(2)}, u32[]{:S(2)}) collective-permute-start(bf16[576,128]{1,0:T(8,128)(2,1)S(1)} %collective-permute-done.28.refs_11_), channel_id=1, source_target_pairs={{0,1},{1,0},{2,3},{3,2},{4,5},{5,4},{6,7},{7,6},{8,9},{9,8},{10,11... | collective-permute-start | bytes 442376 | tf_op jit(solution)/shard_map/ppermute | solution.py:88

commit v3 on v2

--- a/solution.py
+++ b/solution.py
@@ -9,7 +9,8 @@
 
 DILATION_STEP = 8192
 AXES = ("seq", "sub")
-VMEM_LIMIT = 32 * 1024 * 1024
+VMEM_LIMIT = 16 * 1024 * 1024
+LONG = 8 * 10**9
 BF16, F32 = jnp.bfloat16, jnp.float32
 
 
@@ -35,23 +36,34 @@
     def __init__(self):
         self.last = ()
 
-    def call(self, body, outs, operands, scratch=()):
+    def call(self, body, outs, operands, scratch=(), flops=0, blocked=(), key=0, far=(), alias=False):
         count, earlier = len(operands), self.last
 
         def kernel(*refs):
             body(*refs[:count], *refs[count + len(earlier) :])
 
+        def spec(shape, at):
+            if at in far:
+                return pl.BlockSpec(memory_space=pltpu.HBM)
+            if not blocked:
+                return pl.BlockSpec(memory_space=pltpu.VMEM)
+            if blocked[at]:
+                return pl.BlockSpec((shape[0] // 4,) + shape[1:], lambda i: (i, 0))
+            return pl.BlockSpec(shape, lambda i: (0,) * len(shape))
+
         made = pl.pallas_call(
             kernel,
+            grid=(4,) if blocked else (),
             out_shape=[jax.ShapeDtypeStruct(shape, dtype) for shape, dtype in outs],
-            in_specs=[pl.BlockSpec(memory_space=pltpu.VMEM)] * count
+            in_specs=[spec(value.shape, at) for at, value in enumerate(operands)]
             + [pl.BlockSpec(memory_space=pl.ANY)] * len(earlier),
-            out_specs=[pl.BlockSpec(memory_space=pltpu.VMEM)] * len(outs),
+            out_specs=[spec(shape, count + at) for at, (shape, _) in enumerate(outs)],
             scratch_shapes=list(scratch),
+            input_output_aliases={0: 0} if alias else {},
             compiler_params=pltpu.CompilerParams(vmem_limit_bytes=VMEM_LIMIT),
-            cost_estimate=pl.CostEstimate(flops=0, bytes_accessed=0, transcendentals=0),
+            cost_estimate=pl.CostEstimate(flops=flops, bytes_accessed=0, transcendentals=0),
         )(*operands, *earlier)
-        self.last = (made[0],)
+        self.last = (made[key],)
         return made
 
 
@@ -184,7 +196,7 @@
     return [own] + [layout.across(value, 2 * k) for k, value in enumerate(sent, 1)]
 
 
-def plane_sum(chain, layout, sums, parts):
+def plane_sum(chain, layout, sums, parts, flops=0):
     def run(own, *refs):
         away, out = refs[:-1], refs[-1]
         top = base = 0
@@ -196,10 +208,10 @@
             group.store(out.at[top : top + size], (), value)
             top, base = top + size, base + mine
 
-    return chain.call(run, [((sent_rows(sums), LANES), BF16)], parts)[0]
-
-
-def pair_sum(chain, sums, mine, arrived):
+    return chain.call(run, [((sent_rows(sums), LANES), BF16)], parts, flops=flops)[0]
+
+
+def pair_sum(chain, sums, mine, arrived, flops=0):
     def run(left, right, out):
         top = 0
         for group in sums:
@@ -208,21 +220,27 @@
             group.store(out.at[top : top + size], (), value)
             top += size
 
-    return chain.call(run, [(mine.shape, BF16)], (mine, arrived))[0]
+    return chain.call(run, [(mine.shape, BF16)], (mine, arrived), flops=flops)[0]
 
 
 def back_plane(layout, sent):
     return [sent] + [layout.across(sent, 2 * k) for k in range(1, layout.blocks)]
 
 
-def back_core(layout, own):
-    return own + [layout.across(value, 1) for value in own]
+def back_core(chain, layout, parts, flops=0):
+    def run(*refs):
+        for at, ref in enumerate(refs[:-1]):
+            refs[-1][at] = ref[...]
+
+    (own,) = chain.call(run, [((len(parts),) + parts[0].shape, BF16)], parts, flops=flops)
+    return own, layout.across(own, 1)
 
 
 def unsplit(layout, sums, refs, tall, wide, exact):
     core, block = layout.place()
-    for at, ref in enumerate(refs):
+    for at in range(2 * layout.blocks):
         other, k = divmod(at, layout.blocks)
+        ref = refs[other].at[k]
         piece = 2 * (block ^ k) + (core ^ other)
         top = 0
         for number, group in enumerate(sums):
@@ -254,7 +272,7 @@
         layout = Layout(mesh_shape, rows)
         factor = 1.0 / math.sqrt(layout.bins)
         plane = layout.plane
-        cuts = [(0, 256), (256, width)]
+        cuts = [(0, LANES), (LANES, width)]
         chain = Chain()
 
         def forward_taps(source, weights, early, late, activated):
@@ -283,13 +301,6 @@
             [((rows, width), F32)] * 2,
             (activated, kernel, offsets.reshape(1, width), cotangent, mixer),
         )
-
-        def input_slope(source, slope):
-            @blocks_of(rows)
-            def _(block):
-                slope[block, :] = gelu_parts(source[block, :].astype(F32))[1]
-
-        (slope_in,) = chain.call(input_slope, [((rows, channels), F32)], (features,))
 
         def own_grads(low, high):
             def run(center, hidden_grad, early, late, hidden, grad):
@@ -339,8 +350,7 @@
                 wide[low:high, :] = contract_rows(value[...], cot[...]) * factor
             own.split([tall], [wide], exact, held, away)
 
-        own_sums = [Sum(layout, channels, 2 * width // LANES, True)]
-        own = own_sums[0]
+        own = Sum(layout, channels, 2 * width // LANES, True)
         held, away = chain.call(
             own_weights,
             split_types(own),
@@ -368,6 +378,8 @@
             output_parts,
             [((rows, channels), BF16), ((rows, channels), F32)],
             (features, mixer, biases.reshape(1, channels), kernel, *hidden, *grads),
+            flops=LONG,
+            key=1,
         )
 
         def side_weights(group, low, high):
@@ -378,25 +390,33 @@
 
             return run
 
-        def side_product(low, high, is_last):
-            def run(product, later, earlier, weights, *refs):
-                @blocks_of(rows)
-                def _(block):
-                    total = (
-                        product[block, :]
-                        + times_transposed(later[block, :], weights[0, :, low:high])
-                        + times_transposed(earlier[block, :], weights[2, :, low:high])
-                    )
-                    if is_last:
-                        cot, slope, out = refs
-                        total = cot[block, :].astype(F32) + total * slope[block, :]
-                    else:
-                        (out,) = refs
-                    out[block, :] = total.astype(out.dtype)
-
-            return run
+        def side_product(product, later, earlier, weights, out):
+            low, high = cuts[0]
+
+            @blocks_of(rows)
+            def _(block):
+                out[block, :] = (
+                    product[block, :]
+                    + times_transposed(later[block, :], weights[0, :, low:high])
+                    + times_transposed(earlier[block, :], weights[2, :, low:high])
+                )
+
+        def input_grads(product, later, earlier, weights, cot, slope, out, done):
+            low, high = cuts[1]
+            done[...] = jnp.zeros_like(done)
+
+            @blocks_of(rows)
+            def _(block):
+                total = (
+                    product[block, :]
+                    + times_transposed(later[block, :], weights[0, :, low:high])
+                    + times_transposed(earlier[block, :], weights[2, :, low:high])
+                )
+                out[block, :] = (cot[block, :].astype(F32) + total * slope[block, :]).astype(BF16)
 
         side_sums = [Sum(layout, channels, 2 * (high - low) // LANES) for low, high in cuts]
+
+        FLOPS = (LONG, LONG)
 
         def start_side(at):
             low, high = cuts[at]
@@ -405,80 +425,147 @@
                 split_types(side_sums[at]),
                 (activated, *arrived[at]),
                 [pltpu.VMEM((channels, high - low), F32)] * 2,
+                FLOPS[at],
             )
 
-        def add_side(at, product):
-            low, high = cuts[at]
-            is_last = high == width
-            return chain.call(
-                side_product(low, high, is_last),
-                [((rows, channels), BF16 if is_last else F32)],
-                (product, *arrived[at], kernel) + ((cotangent, slope_in) if is_last else ()),
-            )[0]
+        def input_slope(source, slope):
+            @blocks_of(rows)
+            def _(block):
+                slope[block, :] = gelu_parts(source[block, :].astype(F32))[1]
+
 
         held, away = start_side(0)
+        halves = [own_half, (held, layout.across(away, 1))]
+        (product,) = chain.call(
+            side_product,
+            [((rows, channels), F32)],
+            (product, *arrived[0], kernel),
+            flops=LONG,
+        )
+        first_sums, last_sums = [own, side_sums[0]], side_sums[1:]
+        parts = over_plane(chain, layout, first_sums, halves)
+        (slope_in,) = chain.call(input_slope, [((rows, channels), F32)], (features,), flops=LONG)
+        first_sent = plane_sum(chain, layout, first_sums, parts, LONG)
+        masks = [1 << bit for bit in range(layout.ring.bit_length() - 1)]
+        first_arrived = layout.along(first_sent, masks[0])
+
+        held, away = start_side(1)
         halves = [(held, layout.across(away, 1))]
-        own_parts = over_plane(chain, layout, own_sums, [own_half])
-        product = add_side(0, product)
-        held, away = start_side(1)
-        own_sent = plane_sum(chain, layout, own_sums, own_parts)
-        halves.append((held, layout.across(away, 1)))
-        masks = [1 << bit for bit in range(layout.ring.bit_length() - 1)]
-        arrived_own = layout.along(own_sent, masks[0])
-        parts = over_plane(chain, layout, side_sums, halves)
-        own_sent = pair_sum(chain, own_sums, own_sent, arrived_own)
-        for mask in masks[1:-1]:
-            own_sent = pair_sum(chain, own_sums, own_sent, layout.along(own_sent, mask))
-        arrived_own = layout.along(own_sent, masks[-1])
-        input_grad = add_side(count - 1, product)
-        side_sent = plane_sum(chain, layout, side_sums, parts)
-        arrived_side = layout.along(side_sent, masks[0])
-        own_level = back_plane(layout, pair_sum(chain, own_sums, own_sent, arrived_own))
-        side_sent = pair_sum(chain, side_sums, side_sent, arrived_side)
         for mask in masks[1:]:
-            side_sent = pair_sum(chain, side_sums, side_sent, layout.along(side_sent, mask))
-        side_level = back_core(layout, back_plane(layout, side_sent))
-        own_level = back_core(layout, own_level)
-
-        def finish(*refs):
-            each = 2 * layout.blocks
-            own_refs, side_refs = refs[:each], refs[each : 2 * each]
-            kernel_grad, mixer_grad, exact = refs[2 * each :]
-            units = [range(low, high, LANES) for low, high in cuts]
+            first_sent = pair_sum(chain, first_sums, first_sent, first_arrived, LONG)
+            first_arrived = layout.along(first_sent, mask)
+        parts = over_plane(chain, layout, last_sums, halves)
+        last_sent = plane_sum(chain, layout, last_sums, parts)
+        last_arrived = layout.along(last_sent, masks[0])
+        first_level = back_plane(layout, pair_sum(chain, first_sums, first_sent, first_arrived))
+        for mask in masks[1:]:
+            last_sent = pair_sum(chain, last_sums, last_sent, last_arrived)
+            last_arrived = layout.along(last_sent, mask)
+        input_grad, _ = chain.call(
+            input_grads,
+            [((rows, channels), BF16), ((8, LANES), F32)],
+            (product, *arrived[1], kernel, cotangent, slope_in),
+            flops=LONG,
+            key=1,
+        )
+        last_sent = pair_sum(chain, last_sums, last_sent, last_arrived)
+        last_level = back_plane(layout, last_sent)
+        first_level = back_core(chain, layout, first_level, LONG)
+        last_level = back_core(chain, layout, last_level, LONG)
+
+        def side_targets(kernel_grad, low, high):
+            return [(kernel_grad.at[i], at) for i in (0, 2) for at in range(low, high, LANES)]
+
+        def finish_first(*refs):
+            arrived, refs = refs[:2], refs[2:]
+            kernel_grad, mixer_grad, biases_grad, offset_grad = refs[:4]
+            center, sides, exact, sems = refs[4:]
+            targets = range(0, width, LANES)
+            low, high = cuts[0]
             unsplit(
                 layout,
-                own_sums,
-                own_refs,
-                [[(kernel_grad.at[1], low) for low in range(0, width, LANES)]],
-                [[(mixer_grad, low) for low in range(0, width, LANES)]],
+                first_sums,
+                arrived,
+                [
+                    [(center, at) for at in targets],
+                    [(sides.at[i], at) for i in (0, 1) for at in range(0, high - low, LANES)],
+                ],
+                [[(mixer_grad, at) for at in targets], []],
                 exact,
             )
-            unsplit(
-                layout,
-                side_sums,
-                side_refs,
-                [[(kernel_grad.at[i], low) for i in (0, 2) for low in unit] for unit in units],
-                [[] for unit in units],
-                None,
-            )
-
-        kernel_grad, mixer_grad, vectors = chain.call(
-            finish,
+            copies = [pltpu.make_async_copy(center, kernel_grad.at[1], sems.at[0])]
+            for i in (0, 1):
+                copies.append(
+                    pltpu.make_async_copy(
+                        sides.at[i], kernel_grad.at[2 * i, :, low:high], sems.at[1 + i]
+                    )
+                )
+            for copy in copies:
+                copy.start()
+            for at in range(0, channels, LANES):
+                biases_grad[at : at + LANES] = exact[at // LANES, :]
+            for at in range(0, width, LANES):
+                offset_grad[at : at + LANES] = exact[(channels + at) // LANES, :]
+            for copy in copies:
+                copy.wait()
+
+        low, high = cuts[0]
+        kernel_grad, mixer_grad, biases_grad, offset_grad = chain.call(
+            finish_first,
             [
                 ((3, channels, width), F32),
                 ((width, channels), F32),
-                ((plane * EXTRA, LANES), F32),
+                ((channels,), F32),
+                ((width,), F32),
             ],
-            (*own_level, *side_level),
-        )
-        vectors = vectors.reshape(-1)
+            first_level,
+            [
+                pltpu.VMEM((channels, width), F32),
+                pltpu.VMEM((2, channels, high - low), F32),
+                pltpu.VMEM((plane * EXTRA, LANES), F32),
+                pltpu.SemaphoreType.DMA((3,)),
+            ],
+            far=(2,),
+            key=3,
+        )
+
+        def finish_last(begun, *refs):
+            arrived, (kernel_grad, sides, sems) = refs[:2], refs[2:]
+            low, high = cuts[1]
+            unsplit(
+                layout,
+                last_sums,
+                arrived,
+                [[(sides.at[i], at) for i in (0, 1) for at in range(0, high - low, LANES)]],
+                [[]],
+                None,
+            )
+            copies = [
+                pltpu.make_async_copy(sides.at[i], kernel_grad.at[2 * i, :, low:high], sems.at[i])
+                for i in (0, 1)
+            ]
+            for copy in copies:
+                copy.start()
+            for copy in copies:
+                copy.wait()
+
+        low, high = cuts[1]
+        chain.last = ()
+        (kernel_grad,) = chain.call(
+            finish_last,
+            [((3, channels, width), F32)],
+            (kernel_grad, *last_level),
+            [pltpu.VMEM((2, channels, high - low), F32), pltpu.SemaphoreType.DMA((2,))],
+            far=(0, 3),
+            alias=True,
+        )
         return (
             layer_output,
             input_grad,
             kernel_grad,
-            vectors[channels : channels + width],
+            offset_grad,
             mixer_grad,
-            vectors[:channels],
+            biases_grad,
         )
 
     rows_split = P(AXES, None)

time: 137 us -> 120 us (0.88)
  waiting for transfers between devices: 72.9 us -> 59.3 us
  local copies, waits for them, and re-layouts: 7.95 us -> 4.65 us
    ppermute x6, waiting for transfers between devices: 48.6 us -> 36.6 us  [around(): return lax.ppermute(value, AXES, pairs)]
    unnamed x20 -> x16, local copies, waits for them, and re-layouts: 6.77 us -> 3.96 us
    ppermute x27 -> x21, waiting for transfers between devices: 24.4 us -> 22.7 us  [across(): return lax.ppermute(value, AXES, [(i, i ^ mask) for i in range(self.count)])]
    pallas_call x21 -> x24, Pallas kernels: 22.3 us -> 23.6 us  [call(): pl.pallas_call(kernel, grid=(4,) if blocked else (), out_shape=[jax.Shape...]
    ppermute x27 -> x21, starting transfers between devices: 20.9 us -> 19.8 us  [across(): return lax.ppermute(value, AXES, [(i, i ^ mask) for i in range(self.count)])]
  transfers between devices with their start and end apart: 33 -> 27, of which waited for: 19 -> 17; matrix products, arithmetic and copies ran while one was open for 0% -> 1% of each run, Pallas kernels for 12% -> 16%
where the time goes in v3:
time: 120 us
  waiting for transfers between devices  59.3 us (49%)
  starting transfers between devices  31.2 us (26%)
  Pallas kernels  23.6 us (20%)
  local copies, waits for them, and re-layouts  4.65 us (4%)
    ppermute x6, waiting for transfers between devices, around(): return lax.ppermute(value, AXES, pairs)  36.6 us
    pallas_call x24, Pallas kernels, call(): pl.pallas_call(kernel, grid=(4,) if blocked else (), out_shape=[jax.Shape...  23.6 us
    ppermute x21, waiting for transfers between devices, across(): return lax.ppermute(value, AXES, [(i, i ^ mask) for i in range(self.count)])  22.7 us
    ppermute x21, starting transfers between devices, across(): return lax.ppermute(value, AXES, [(i, i ^ mask) for i in range(self.count)])  19.8 us
    ppermute x6, starting transfers between devices, around(): return lax.ppermute(value, AXES, pairs)  11.4 us
    unnamed x16, local copies, waits for them, and re-layouts  3.96 us
  transfers between devices with their start and end apart: 27, of which 17 were waited for; matrix products, arithmetic and copies ran while one was open for 1% of the time, Pallas kernels for 16%

profile of v3, /device:TPU:0, one launch (start us, length us, event | category | flops | bytes accessed | tf_op | source)
XLA Modules:
  0.0 119.7 jit_solution(13354730613930656542)
XLA Ops:
  0.6 1.5 %copy-done.1 = bf16[3,768,384]{2,1,0:T(8,128)(2,1)S(1)} copy-done((bf16[3,768,384]{2,1,0:T(8,128)(2,1)S(1)}, bf16[3,768,384]{2,1,0:T(8,128)(2,1)}, u32[]{:S(2)}) %copy-start.1) | copy-done | bytes 1769496
  2.1 1.4 %copy-done.3 = bf16[1024,768]{1,0:T(8,128)(2,1)S(1)} copy-done((bf16[1024,768]{1,0:T(8,128)(2,1)S(1)}, bf16[1024,768]{1,0:T(8,128)(2,1)}, u32[]{:S(2)}) %copy-start.3) | copy-done | bytes 1572888
  3.5 2.3 %shard_map.109 = (bf16[1024,384]{1,0:T(8,128)(2,1)S(1)}, bf16[1024,384]{1,0:T(8,128)(2,1)S(1)}, bf16[1024,768]{1,0:T(8,128)(2,1)S(1)}) custom-call(bf16[1024,768]{1,0:T(8,128)(2,1)S(1)} %copy-done.3, bf16[3,768,384]{2,1,0:T(8,128)(2,1)S(1)} %copy-done.1), custom_call_target="tpu_custom_call" | custom-call | tf_op jit(solution)/shard_map/pallas_call | solution.py:54
  5.9 3.1 %collective-permute-start = (bf16[1024,384]{1,0:T(8,128)(2,1)S(1)}, bf16[1024,384]{1,0:T(8,128)(2,1)S(1)}, u32[]{:S(2)}, u32[]{:S(2)}) collective-permute-start(bf16[1024,384]{1,0:T(8,128)(2,1)S(1)} %get-tuple-element.38.refs_5_), channel_id=1, source_target_pairs={{0,8},{1,9},{2,10},{3,11},{4,12},{5,13},{6,14},{7,15},{8,16},{9,17... | collective-permute-start | bytes 2359304 | tf_op jit(solution)/shard_map/ppermute | solution.py:97
  9.0 2.1 %collective-permute-start.1 = (bf16[1024,384]{1,0:T(8,128)(2,1)S(1)}, bf16[1024,384]{1,0:T(8,128)(2,1)S(1)}, u32[]{:S(2)}, u32[]{:S(2)}) collective-permute-start(bf16[1024,384]{1,0:T(8,128)(2,1)S(1)} %get-tuple-element.41), channel_id=1, source_target_pairs={{0,24},{1,25},{2,26},{3,27},{4,28},{5,29},{6,30},{7,31},{8,0},{9,1... | collective-permute-start | bytes 2359304 | tf_op jit(solution)/shard_map/ppermute | solution.py:97
  11.0 0.7 reshape.18.refs_2_
  11.8 1.1 copy-done.5
  12.8 2.2 %shard_map.110 = (f32[1024,384]{1,0:T(8,128)S(1)}, f32[1024,384]{1,0:T(8,128)S(1)}) custom-call(bf16[1024,768]{1,0:T(8,128)(2,1)S(1)} %get-tuple-element.37.refs_0_, bf16[3,768,384]{2,1,0:T(8,128)(2,1)S(1)} %copy-done.2, f32[1,384]{1,0:T(1,128)S(1)} %reshape.19.refs_2_, bf16[1024,768]{1,0:T(8,128)(2,1)S(1)} %copy-done, bf16[384,768]{1,0:T(8,128)(2,1)S(1)} %copy-done.5, ...), custom_call_target="tpu_custom_call" | custom-call | tf_op jit(solution)/shard_map/pallas_call | solution.py:54
  15.1 14.3 %collective-permute-done.refs_2_ = bf16[1024,384]{1,0:T(8,128)(2,1)S(1)} collective-permute-done((bf16[1024,384]{1,0:T(8,128)(2,1)S(1)}, bf16[1024,384]{1,0:T(8,128)(2,1)S(1)}, u32[]{:S(2)}, u32[]{:S(2)}) %collective-permute-start) | collective-permute-done | bytes 786464 | tf_op jit(solution)/shard_map/ppermute | solution.py:97
  29.4 15.4 %collective-permute-done.1.refs_3_ = bf16[1024,384]{1,0:T(8,128)(2,1)S(1)} collective-permute-done((bf16[1024,384]{1,0:T(8,128)(2,1)S(1)}, bf16[1024,384]{1,0:T(8,128)(2,1)S(1)}, u32[]{:S(2)}, u32[]{:S(2)}) %collective-permute-start.1) | collective-permute-done | bytes 786464 | tf_op jit(solution)/shard_map/ppermute | solution.py:97
  44.8 0.3 shard_map.111
  45.2 2.4 %collective-permute-start.2 = (bf16[1024,128]{1,0:T(8,128)(2,1)S(1)}, bf16[1024,128]{1,0:T(8,128)(2,1)S(1)}, u32[]{:S(2)}, u32[]{:S(2)}) collective-permute-start(bf16[1024,128]{1,0:T(8,128)(2,1)S(1)} %get-tuple-element.44.refs_1_.refs_5_.refs_6_), channel_id=1, source_target_pairs={{0,24},{1,25},{2,26},{3,27},{4,28},{5,29},{6,30},{7,31},{8,0},{9,1... | collective-permute-start | bytes 786440 | tf_op jit(solution)/shard_map/ppermute | solution.py:97
  47.5 0.7 shard_map.112
  48.2 3.9 %collective-permute-start.4 = (bf16[1024,256]{1,0:T(8,128)(2,1)S(1)}, bf16[1024,256]{1,0:T(8,128)(2,1)S(1)}, u32[]{:S(2)}, u32[]{:S(2)}) collective-permute-start(bf16[1024,256]{1,0:T(8,128)(2,1)S(1)} %get-tuple-element.45.refs_2_.refs_6_.refs_7_), channel_id=1, source_target_pairs={{0,24},{1,25},{2,26},{3,27},{4,28},{5,29},{6,30},{7,31},{8,0},{9,1... | collective-permute-start | bytes 1572872 | tf_op jit(solution)/shard_map/ppermute | solution.py:97
  52.1 0.4 shard_map.113.refs_2_.refs_7_
  52.5 2.1 %shard_map.114 = (f32[4,584,128]{2,1,0:T(8,128)S(1)}, bf16[4,592,128]{2,1,0:T(8,128)(2,1)S(1)}) custom-call(bf16[1024,768]{1,0:T(8,128)(2,1)S(1)} %get-tuple-element.37.refs_0_, bf16[1024,768]{1,0:T(8,128)(2,1)S(1)} %copy-done, f32[64,128]{1,0:T(8,128)S(1)} %shard_map.113.refs_2_.refs_7_, bf16[1024,128]{1,0:T(8,128)(2,1)S(1)} %get-tuple-element.42.refs_4_.refs_3_, ...), custom_call_target="tpu_custom_call" | custom-call | tf_op jit(solution)/shard_map/pallas_call | solution.py:54
  54.6 0.1 collective-permute-start.6
  54.7 3.3 %shard_map.115 = (bf16[1024,768]{1,0:T(8,128)(2,1)}, f32[1024,768]{1,0:T(8,128)S(1)}) custom-call(bf16[1024,768]{1,0:T(8,128)(2,1)S(1)} %copy-done.4, bf16[384,768]{1,0:T(8,128)(2,1)S(1)} %copy-done.6, f32[1,768]{1,0:T(1,128)S(1)} %reshape.18.refs_2_, bf16[3,768,384]{2,1,0:T(8,128)(2,1)S(1)} %copy-done.2, ...), custom_call_target="tpu_custom_call" | custom-call | flops 8000000000 | tf_op jit(solution)/shard_map/pallas_call | solution.py:54
  58.0 1.3 %collective-permute-done.2.refs_1_ = bf16[1024,128]{1,0:T(8,128)(2,1)S(1)} collective-permute-done((bf16[1024,128]{1,0:T(8,128)(2,1)S(1)}, bf16[1024,128]{1,0:T(8,128)(2,1)S(1)}, u32[]{:S(2)}, u32[]{:S(2)}) %collective-permute-start.2) | collective-permute-done | bytes 262176 | tf_op jit(solution)/shard_map/ppermute | solution.py:97
  59.3 1.5 %collective-permute-done.3.refs_2_ = bf16[1024,128]{1,0:T(8,128)(2,1)S(1)} collective-permute-done((bf16[1024,128]{1,0:T(8,128)(2,1)S(1)}, bf16[1024,128]{1,0:T(8,128)(2,1)S(1)}, u32[]{:S(2)}, u32[]{:S(2)}) %collective-permute-start.3) | collective-permute-done | bytes 262176 | tf_op jit(solution)/shard_map/ppermute | solution.py:97
  60.8 1.1 shard_map.116
  61.9 0.1 collective-permute-start.7
  62.0 1.5 %shard_map.117.refs_4_.refs_0_ = f32[1024,768]{1,0:T(8,128)S(1)} custom-call(f32[1024,768]{1,0:T(8,128)S(1)} %get-tuple-element.48.refs_3_.refs_0_, bf16[1024,128]{1,0:T(8,128)(2,1)S(1)} %collective-permute-done.2.refs_1_, bf16[1024,128]{1,0:T(8,128)(2,1)S(1)} %collective-permute-done.3.refs_2_, bf16[3,768,384]{2,1,0:T(8,128)(2,1)S(1)} %copy-done.2, ...), custom_call_target="tpu_custom_call" | custom-call | flops 8000000000 | tf_op jit(solution)/shard_map/pallas_call | solution.py:54
  63.5 0.2 shard_map.118
  63.7 1.6 %collective-permute-start.8 = (bf16[784,128]{1,0:T(8,128)(2,1)S(1)}, bf16[784,128]{1,0:T(8,128)(2,1)S(1)}, u32[]{:S(2)}, u32[]{:S(2)}) collective-permute-start(bf16[784,128]{1,0:T(8,128)(2,1)S(1)} %get-tuple-element.53), channel_id=1, source_target_pairs={{0,2},{1,3},{2,0},{3,1},{4,6},{5,7},{6,4},{7,5},{8,10},{9,11},{10,... | collective-permute-start | bytes 602120 | tf_op jit(solution)/shard_map/ppermute | solution.py:100
  65.3 1.5 %collective-permute-start.9 = (bf16[784,128]{1,0:T(8,128)(2,1)S(1)}, bf16[784,128]{1,0:T(8,128)(2,1)S(1)}, u32[]{:S(2)}, u32[]{:S(2)}) collective-permute-start(bf16[784,128]{1,0:T(8,128)(2,1)S(1)} %get-tuple-element.54), channel_id=1, source_target_pairs={{0,4},{1,5},{2,6},{3,7},{4,0},{5,1},{6,2},{7,3},{8,12},{9,13},{10,... | collective-permute-start | bytes 602120 | tf_op jit(solution)/shard_map/ppermute | solution.py:100
  66.8 0.5 collective-permute-start.10
  67.2 1.2 %shard_map.119.refs_4_.refs_5_ = f32[1024,768]{1,0:T(8,128)S(1)} custom-call(bf16[1024,768]{1,0:T(8,128)(2,1)S(1)} %copy-done.4, f32[776,128]{1,0:T(8,128)S(1)} %get-tuple-element.52.refs_1_.refs_0_), custom_call_target="tpu_custom_call" | custom-call | flops 8000000000 | tf_op jit(solution)/shard_map/pallas_call | solution.py:54
  68.5 2.6 %collective-permute-done.8.refs_1_ = bf16[784,128]{1,0:T(8,128)(2,1)S(1)} collective-permute-done((bf16[784,128]{1,0:T(8,128)(2,1)S(1)}, bf16[784,128]{1,0:T(8,128)(2,1)S(1)}, u32[]{:S(2)}, u32[]{:S(2)}) %collective-permute-start.8) | collective-permute-done | bytes 200736 | tf_op jit(solution)/shard_map/ppermute | solution.py:100
  71.1 2.0 %collective-permute-done.9.refs_2_ = bf16[784,128]{1,0:T(8,128)(2,1)S(1)} collective-permute-done((bf16[784,128]{1,0:T(8,128)(2,1)S(1)}, bf16[784,128]{1,0:T(8,128)(2,1)S(1)}, u32[]{:S(2)}, u32[]{:S(2)}) %collective-permute-start.9) | collective-permute-done | bytes 200736 | tf_op jit(solution)/shard_map/ppermute | solution.py:100
  73.1 3.5 %collective-permute-done.10.refs_3_ = bf16[784,128]{1,0:T(8,128)(2,1)S(1)} collective-permute-done((bf16[784,128]{1,0:T(8,128)(2,1)S(1)}, bf16[784,128]{1,0:T(8,128)(2,1)S(1)}, u32[]{:S(2)}, u32[]{:S(2)}) %collective-permute-start.10) | collective-permute-done | bytes 200736 | tf_op jit(solution)/shard_map/ppermute | solution.py:100
  76.6 0.1 shard_map.120.refs_3_.refs_0_
  76.7 1.6 %collective-permute-start.12 = (bf16[784,128]{1,0:T(8,128)(2,1)S(1)}, bf16[784,128]{1,0:T(8,128)(2,1)S(1)}, u32[]{:S(2)}, u32[]{:S(2)}) collective-permute-start(bf16[784,128]{1,0:T(8,128)(2,1)S(1)} %shard_map.120.refs_3_.refs_0_), channel_id=1, source_target_pairs={{0,8},{1,9},{2,10},{3,11},{4,12},{5,13},{6,14},{7,15},{8,0},{9,1},... | collective-permute-start | bytes 602120 | tf_op jit(solution)/shard_map/ppermute | solution.py:100
  78.3 4.0 %collective-permute-done.5.refs_2_ = bf16[1024,256]{1,0:T(8,128)(2,1)S(1)} collective-permute-done((bf16[1024,256]{1,0:T(8,128)(2,1)S(1)}, bf16[1024,256]{1,0:T(8,128)(2,1)S(1)}, u32[]{:S(2)}, u32[]{:S(2)}) %collective-permute-start.5) | collective-permute-done | bytes 524320 | tf_op jit(solution)/shard_map/ppermute | solution.py:97
  82.4 1.2 shard_map.121
  83.6 0.1 collective-permute-start.11
  83.7 2.2 %collective-permute-done.12.refs_1_ = bf16[784,128]{1,0:T(8,128)(2,1)S(1)} collective-permute-done((bf16[784,128]{1,0:T(8,128)(2,1)S(1)}, bf16[784,128]{1,0:T(8,128)(2,1)S(1)}, u32[]{:S(2)}, u32[]{:S(2)}) %collective-permute-start.12) | collective-permute-done | bytes 200736 | tf_op jit(solution)/shard_map/ppermute | solution.py:100
  85.9 0.6 collective-permute-start.17
  86.5 0.1 shard_map.123
  86.5 1.4 %collective-permute-start.13 = (bf16[384,128]{1,0:T(8,128)(2,1)S(1)}, bf16[384,128]{1,0:T(8,128)(2,1)S(1)}, u32[]{:S(2)}, u32[]{:S(2)}) collective-permute-start(bf16[384,128]{1,0:T(8,128)(2,1)S(1)} %get-tuple-element.59), channel_id=1, source_target_pairs={{0,2},{1,3},{2,0},{3,1},{4,6},{5,7},{6,4},{7,5},{8,10},{9,11},{10,... | collective-permute-start | bytes 294920 | tf_op jit(solution)/shard_map/ppermute | solution.py:100
  87.9 1.5 %collective-permute-start.14 = (bf16[384,128]{1,0:T(8,128)(2,1)S(1)}, bf16[384,128]{1,0:T(8,128)(2,1)S(1)}, u32[]{:S(2)}, u32[]{:S(2)}) collective-permute-start(bf16[384,128]{1,0:T(8,128)(2,1)S(1)} %get-tuple-element.60), channel_id=1, source_target_pairs={{0,4},{1,5},{2,6},{3,7},{4,0},{5,1},{6,2},{7,3},{8,12},{9,13},{10,... | collective-permute-start | bytes 294920 | tf_op jit(solution)/shard_map/ppermute | solution.py:100
  89.4 0.7 collective-permute-start.15
  90.1 1.1 collective-permute-done.13.refs_1_
  91.2 1.8 %collective-permute-done.14.refs_2_ = bf16[384,128]{1,0:T(8,128)(2,1)S(1)} collective-permute-done((bf16[384,128]{1,0:T(8,128)(2,1)S(1)}, bf16[384,128]{1,0:T(8,128)(2,1)S(1)}, u32[]{:S(2)}, u32[]{:S(2)}) %collective-permute-start.14) | collective-permute-done | bytes 98336 | tf_op jit(solution)/shard_map/ppermute | solution.py:100
  93.0 1.9 %collective-permute-done.15.refs_3_ = bf16[384,128]{1,0:T(8,128)(2,1)S(1)} collective-permute-done((bf16[384,128]{1,0:T(8,128)(2,1)S(1)}, bf16[384,128]{1,0:T(8,128)(2,1)S(1)}, u32[]{:S(2)}, u32[]{:S(2)}) %collective-permute-start.15) | collective-permute-done | bytes 98336 | tf_op jit(solution)/shard_map/ppermute | solution.py:100
  95.0 2.4 %collective-permute-start.16 = (bf16[384,128]{1,0:T(8,128)(2,1)S(1)}, bf16[384,128]{1,0:T(8,128)(2,1)S(1)}, u32[]{:S(2)}, u32[]{:S(2)}) collective-permute-start(bf16[384,128]{1,0:T(8,128)(2,1)S(1)} %shard_map.124.refs_2_.refs_0_), channel_id=1, source_target_pairs={{0,8},{1,9},{2,10},{3,11},{4,12},{5,13},{6,14},{7,15},{8,0},{9,1},... | collective-permute-start | bytes 294920 | tf_op jit(solution)/shard_map/ppermute | solution.py:100
  97.3 0.8 collective-permute-done.17.refs_1_
  98.2 1.4 %collective-permute-start.18 = (bf16[784,128]{1,0:T(8,128)(2,1)S(1)}, bf16[784,128]{1,0:T(8,128)(2,1)S(1)}, u32[]{:S(2)}, u32[]{:S(2)}) collective-permute-start(bf16[784,128]{1,0:T(8,128)(2,1)S(1)} %shard_map.125.refs_2_.refs_0_), channel_id=1, source_target_pairs={{0,2},{1,3},{2,0},{3,1},{4,6},{5,7},{6,4},{7,5},{8,10},{9,11},{10,... | collective-permute-start | bytes 602120 | tf_op jit(solution)/shard_map/ppermute | solution.py:100
  99.6 1.5 %collective-permute-start.19 = (bf16[784,128]{1,0:T(8,128)(2,1)S(1)}, bf16[784,128]{1,0:T(8,128)(2,1)S(1)}, u32[]{:S(2)}, u32[]{:S(2)}) collective-permute-start(bf16[784,128]{1,0:T(8,128)(2,1)S(1)} %shard_map.125.refs_2_.refs_0_), channel_id=1, source_target_pairs={{0,4},{1,5},{2,6},{3,7},{4,0},{5,1},{6,2},{7,3},{8,12},{9,13},{10,... | collective-permute-start | bytes 602120 | tf_op jit(solution)/shard_map/ppermute | solution.py:100
  101.1 0.7 collective-permute-start.20
  101.8 0.7 collective-permute-start.21
  102.5 2.8 %shard_map.127 = (bf16[1024,768]{1,0:T(8,128)(2,1)}, f32[8,128]{1,0:T(8,128)S(1)}) custom-call(f32[1024,768]{1,0:T(8,128)S(1)} %shard_map.117.refs_4_.refs_0_, bf16[1024,256]{1,0:T(8,128)(2,1)S(1)} %collective-permute-done.4.refs_1_, bf16[1024,256]{1,0:T(8,128)(2,1)S(1)} %collective-permute-done.5.refs_2_, bf16[3,768,384]{2,1,0:T(8,128)(2,1)S(1)} %copy-done.2, ...), custom_call_target="tpu_custom_call" | custom-call | flops 8000000000 | tf_op jit(solution)/shard_map/pallas_call | solution.py:54
  105.3 2.7 %collective-permute-done.21.refs_1_ = bf16[384,128]{1,0:T(8,128)(2,1)S(1)} collective-permute-done((bf16[384,128]{1,0:T(8,128)(2,1)S(1)}, bf16[384,128]{1,0:T(8,128)(2,1)S(1)}, u32[]{:S(2)}, u32[]{:S(2)}) %collective-permute-start.21) | collective-permute-done | bytes 98336 | tf_op jit(solution)/shard_map/ppermute | solution.py:100
  108.1 0.7 collective-permute-start.23
  108.8 1.5 %collective-permute-start.24 = (bf16[384,128]{1,0:T(8,128)(2,1)S(1)}, bf16[384,128]{1,0:T(8,128)(2,1)S(1)}, u32[]{:S(2)}, u32[]{:S(2)}) collective-permute-start(bf16[384,128]{1,0:T(8,128)(2,1)S(1)} %shard_map.128.refs_4_.refs_0_), channel_id=1, source_target_pairs={{0,4},{1,5},{2,6},{3,7},{4,0},{5,1},{6,2},{7,3},{8,12},{9,13},{10,... | collective-permute-start | bytes 294920 | tf_op jit(solution)/shard_map/ppermute | solution.py:100
  110.3 1.4 %collective-permute-start.25 = (bf16[384,128]{1,0:T(8,128)(2,1)S(1)}, bf16[384,128]{1,0:T(8,128)(2,1)S(1)}, u32[]{:S(2)}, u32[]{:S(2)}) collective-permute-start(bf16[384,128]{1,0:T(8,128)(2,1)S(1)} %shard_map.128.refs_4_.refs_0_), channel_id=1, source_target_pairs={{0,6},{1,7},{2,4},{3,5},{4,2},{5,3},{6,0},{7,1},{8,14},{9,15},{10,... | collective-permute-start | bytes 294920 | tf_op jit(solution)/shard_map/ppermute | solution.py:100
  111.6 0.1 collective-permute-done.20.refs_3_
  111.7 0.1 shard_map.129.refs_4_.refs_0_
  111.8 0.1 collective-permute-start.22
  111.9 1.7 %collective-permute-done.23.refs_1_ = bf16[384,128]{1,0:T(8,128)(2,1)S(1)} collective-permute-done((bf16[384,128]{1,0:T(8,128)(2,1)S(1)}, bf16[384,128]{1,0:T(8,128)(2,1)S(1)}, u32[]{:S(2)}, u32[]{:S(2)}) %collective-permute-start.23) | collective-permute-done | bytes 98336 | tf_op jit(solution)/shard_map/ppermute | solution.py:100
  113.6 2.2 %collective-permute-done.25.refs_3_ = bf16[384,128]{1,0:T(8,128)(2,1)S(1)} collective-permute-done((bf16[384,128]{1,0:T(8,128)(2,1)S(1)}, bf16[384,128]{1,0:T(8,128)(2,1)S(1)}, u32[]{:S(2)}, u32[]{:S(2)}) %collective-permute-start.25) | collective-permute-done | bytes 98336 | tf_op jit(solution)/shard_map/ppermute | solution.py:100
  115.8 0.1 collective-permute-start.26
  115.9 2.5 %shard_map.131 = (f32[3,768,384]{2,1,0:T(8,128)}, f32[384,768]{1,0:T(8,128)}, f32[768]{0:T(1024)}, f32[384]{0:T(512)}) custom-call(bf16[4,784,128]{2,1,0:T(8,128)(2,1)S(1)} %shard_map.129.refs_4_.refs_0_, bf16[4,784,128]{2,1,0:T(8,128)(2,1)S(1)} %collective-permute-done.22.refs_1_, bf16[4,384,128]{2,1,0:T(8,128)(2,1)S(1)} %shard_map.130.refs_2_.refs_1_), custom_call_target="tpu_custom_call" | custom-call | tf_op jit(solution)/shard_map/pallas_call | solution.py:54
  118.4 1.3 %shard_map.132 = f32[3,768,384]{2,1,0:T(8,128)} custom-call(f32[3,768,384]{2,1,0:T(8,128)} %get-tuple-element.64.refs_0_, bf16[4,384,128]{2,1,0:T(8,128)(2,1)S(1)} %shard_map.130.refs_2_.refs_1_, bf16[4,384,128]{2,1,0:T(8,128)(2,1)S(1)} %collective-permute-done.26.refs_2_), custom_call_target="tpu_custom_call", output_to_operand_aliasing={{}: (0, {})} | custom-call | tf_op jit(solution)/shard_map/pallas_call | solution.py:54
  (32 shorter events, 0.3 us)
Async XLA Ops:
  0.6 1.5 %copy-start.1 = (bf16[3,768,384]{2,1,0:T(8,128)(2,1)S(1)}, bf16[3,768,384]{2,1,0:T(8,128)(2,1)}, u32[]{:S(2)}) copy-start(bf16[3,768,384]{2,1,0:T(8,128)(2,1)} %refs_3_.7) | copy-start | bytes 5308420
  2.1 1.4 %copy-start.3 = (bf16[1024,768]{1,0:T(8,128)(2,1)S(1)}, bf16[1024,768]{1,0:T(8,128)(2,1)}, u32[]{:S(2)}) copy-start(bf16[1024,768]{1,0:T(8,128)(2,1)} %refs_0_.7) | copy-start | bytes 4718596
  3.5 8.2 %copy-start.7 = (f32[384]{0:T(512)S(1)}, f32[384]{0:T(512)}, u32[]{:S(2)}) copy-start(f32[384]{0:T(512)} %param.8) | copy-start | bytes 4612
  3.5 8.2 %copy-start = (bf16[1024,768]{1,0:T(8,128)(2,1)S(1)}, bf16[1024,768]{1,0:T(8,128)(2,1)}, u32[]{:S(2)}) copy-start(bf16[1024,768]{1,0:T(8,128)(2,1)} %refs_4_.3) | copy-start | bytes 4718596
  3.5 8.2 %copy-start.2 = (bf16[3,768,384]{2,1,0:T(8,128)(2,1)S(1)}, bf16[3,768,384]{2,1,0:T(8,128)(2,1)}, u32[]{:S(2)}) copy-start(bf16[3,768,384]{2,1,0:T(8,128)(2,1)} %refs_3_.7) | copy-start | bytes 5308420
  5.9 23.5 %collective-permute-start = (bf16[1024,384]{1,0:T(8,128)(2,1)S(1)}, bf16[1024,384]{1,0:T(8,128)(2,1)S(1)}, u32[]{:S(2)}, u32[]{:S(2)}) collective-permute-start(bf16[1024,384]{1,0:T(8,128)(2,1)S(1)} %get-tuple-element.38.refs_5_), channel_id=1, source_target_pairs={{0,8},{1,9},{2,10},{3,11},{4,12},{5,13},{6,14},{7,15},{8,16},{9,17... | collective-permute-start | bytes 2359304 | tf_op jit(solution)/shard_map/ppermute | solution.py:97
  9.0 35.9 %collective-permute-start.1 = (bf16[1024,384]{1,0:T(8,128)(2,1)S(1)}, bf16[1024,384]{1,0:T(8,128)(2,1)S(1)}, u32[]{:S(2)}, u32[]{:S(2)}) collective-permute-start(bf16[1024,384]{1,0:T(8,128)(2,1)S(1)} %get-tuple-element.41), channel_id=1, source_target_pairs={{0,24},{1,25},{2,26},{3,27},{4,28},{5,29},{6,30},{7,31},{8,0},{9,1... | collective-permute-start | bytes 2359304 | tf_op jit(solution)/shard_map/ppermute | solution.py:97
  11.8 1.1 copy-start.5
  45.2 14.1 %collective-permute-start.2 = (bf16[1024,128]{1,0:T(8,128)(2,1)S(1)}, bf16[1024,128]{1,0:T(8,128)(2,1)S(1)}, u32[]{:S(2)}, u32[]{:S(2)}) collective-permute-start(bf16[1024,128]{1,0:T(8,128)(2,1)S(1)} %get-tuple-element.44.refs_1_.refs_5_.refs_6_), channel_id=1, source_target_pairs={{0,24},{1,25},{2,26},{3,27},{4,28},{5,29},{6,30},{7,31},{8,0},{9,1... | collective-permute-start | bytes 786440 | tf_op jit(solution)/shard_map/ppermute | solution.py:97
  47.5 13.3 %collective-permute-start.3 = (bf16[1024,128]{1,0:T(8,128)(2,1)S(1)}, bf16[1024,128]{1,0:T(8,128)(2,1)S(1)}, u32[]{:S(2)}, u32[]{:S(2)}) collective-permute-start(bf16[1024,128]{1,0:T(8,128)(2,1)S(1)} %get-tuple-element.44.refs_1_.refs_5_.refs_6_), channel_id=1, source_target_pairs={{0,8},{1,9},{2,10},{3,11},{4,12},{5,13},{6,14},{7,15},{8,16},{9,17... | collective-permute-start | bytes 786440 | tf_op jit(solution)/shard_map/ppermute | solution.py:97
  48.2 30.2 %collective-permute-start.4 = (bf16[1024,256]{1,0:T(8,128)(2,1)S(1)}, bf16[1024,256]{1,0:T(8,128)(2,1)S(1)}, u32[]{:S(2)}, u32[]{:S(2)}) collective-permute-start(bf16[1024,256]{1,0:T(8,128)(2,1)S(1)} %get-tuple-element.45.refs_2_.refs_6_.refs_7_), channel_id=1, source_target_pairs={{0,24},{1,25},{2,26},{3,27},{4,28},{5,29},{6,30},{7,31},{8,0},{9,1... | collective-permute-start | bytes 1572872 | tf_op jit(solution)/shard_map/ppermute | solution.py:97
  52.1 30.3 %collective-permute-start.5 = (bf16[1024,256]{1,0:T(8,128)(2,1)S(1)}, bf16[1024,256]{1,0:T(8,128)(2,1)S(1)}, u32[]{:S(2)}, u32[]{:S(2)}) collective-permute-start(bf16[1024,256]{1,0:T(8,128)(2,1)S(1)} %get-tuple-element.45.refs_2_.refs_6_.refs_7_), channel_id=1, source_target_pairs={{0,8},{1,9},{2,10},{3,11},{4,12},{5,13},{6,14},{7,15},{8,16},{9,17... | collective-permute-start | bytes 1572872 | tf_op jit(solution)/shard_map/ppermute | solution.py:97
  52.5 2.3 %copy-start.4 = (bf16[1024,768]{1,0:T(8,128)(2,1)S(1)}, bf16[1024,768]{1,0:T(8,128)(2,1)}, u32[]{:S(2)}) copy-start(bf16[1024,768]{1,0:T(8,128)(2,1)} %refs_0_.7) | copy-start | bytes 4718596
  52.5 2.3 %copy-start.6 = (bf16[384,768]{1,0:T(8,128)(2,1)S(1)}, bf16[384,768]{1,0:T(8,128)(2,1)}, u32[]{:S(2)}) copy-start(bf16[384,768]{1,0:T(8,128)(2,1)} %refs_1_.7) | copy-start | bytes 1769476
  54.6 8.9 %collective-permute-start.6 = (bf16[4,592,128]{2,1,0:T(8,128)(2,1)S(1)}, bf16[4,592,128]{2,1,0:T(8,128)(2,1)S(1)}, u32[]{:S(2)}, u32[]{:S(2)}) collective-permute-start(bf16[4,592,128]{2,1,0:T(8,128)(2,1)S(1)} %get-tuple-element.50), channel_id=1, source_target_pairs={{0,1},{1,0},{2,3},{3,2},{4,5},{5,4},{6,7},{7,6},{8,9},{9,8},{10,11... | collective-permute-start | bytes 1818632 | tf_op jit(solution)/shard_map/ppermute | solution.py:100
  61.9 1.6 %collective-permute-start.7 = (bf16[4,192,128]{2,1,0:T(8,128)(2,1)S(1)}, bf16[4,192,128]{2,1,0:T(8,128)(2,1)S(1)}, u32[]{:S(2)}, u32[]{:S(2)}) collective-permute-start(bf16[4,192,128]{2,1,0:T(8,128)(2,1)S(1)} %get-tuple-element.51), channel_id=1, source_target_pairs={{0,1},{1,0},{2,3},{3,2},{4,5},{5,4},{6,7},{7,6},{8,9},{9,8},{10,11... | collective-permute-start | bytes 589832 | tf_op jit(solution)/shard_map/ppermute | solution.py:100
  63.7 7.5 %collective-permute-start.8 = (bf16[784,128]{1,0:T(8,128)(2,1)S(1)}, bf16[784,128]{1,0:T(8,128)(2,1)S(1)}, u32[]{:S(2)}, u32[]{:S(2)}) collective-permute-start(bf16[784,128]{1,0:T(8,128)(2,1)S(1)} %get-tuple-element.53), channel_id=1, source_target_pairs={{0,2},{1,3},{2,0},{3,1},{4,6},{5,7},{6,4},{7,5},{8,10},{9,11},{10,... | collective-permute-start | bytes 602120 | tf_op jit(solution)/shard_map/ppermute | solution.py:100
  65.3 7.8 %collective-permute-start.9 = (bf16[784,128]{1,0:T(8,128)(2,1)S(1)}, bf16[784,128]{1,0:T(8,128)(2,1)S(1)}, u32[]{:S(2)}, u32[]{:S(2)}) collective-permute-start(bf16[784,128]{1,0:T(8,128)(2,1)S(1)} %get-tuple-element.54), channel_id=1, source_target_pairs={{0,4},{1,5},{2,6},{3,7},{4,0},{5,1},{6,2},{7,3},{8,12},{9,13},{10,... | collective-permute-start | bytes 602120 | tf_op jit(solution)/shard_map/ppermute | solution.py:100
  66.8 9.8 %collective-permute-start.10 = (bf16[784,128]{1,0:T(8,128)(2,1)S(1)}, bf16[784,128]{1,0:T(8,128)(2,1)S(1)}, u32[]{:S(2)}, u32[]{:S(2)}) collective-permute-start(bf16[784,128]{1,0:T(8,128)(2,1)S(1)} %get-tuple-element.55), channel_id=1, source_target_pairs={{0,6},{1,7},{2,4},{3,5},{4,2},{5,3},{6,0},{7,1},{8,14},{9,15},{10,... | collective-permute-start | bytes 602120 | tf_op jit(solution)/shard_map/ppermute | solution.py:100
  76.7 9.1 %collective-permute-start.12 = (bf16[784,128]{1,0:T(8,128)(2,1)S(1)}, bf16[784,128]{1,0:T(8,128)(2,1)S(1)}, u32[]{:S(2)}, u32[]{:S(2)}) collective-permute-start(bf16[784,128]{1,0:T(8,128)(2,1)S(1)} %shard_map.120.refs_3_.refs_0_), channel_id=1, source_target_pairs={{0,8},{1,9},{2,10},{3,11},{4,12},{5,13},{6,14},{7,15},{8,0},{9,1},... | collective-permute-start | bytes 602120 | tf_op jit(solution)/shard_map/ppermute | solution.py:100
  83.6 2.9 %collective-permute-start.11 = (bf16[4,384,128]{2,1,0:T(8,128)(2,1)S(1)}, bf16[4,384,128]{2,1,0:T(8,128)(2,1)S(1)}, u32[]{:S(2)}, u32[]{:S(2)}) collective-permute-start(bf16[4,384,128]{2,1,0:T(8,128)(2,1)S(1)} %get-tuple-element.57), channel_id=1, source_target_pairs={{0,1},{1,0},{2,3},{3,2},{4,5},{5,4},{6,7},{7,6},{8,9},{9,8},{10,11... | collective-permute-start | bytes 1179656 | tf_op jit(solution)/shard_map/ppermute | solution.py:100
  85.9 12.3 %collective-permute-start.17 = (bf16[784,128]{1,0:T(8,128)(2,1)S(1)}, bf16[784,128]{1,0:T(8,128)(2,1)S(1)}, u32[]{:S(2)}, u32[]{:S(2)}) collective-permute-start(bf16[784,128]{1,0:T(8,128)(2,1)S(1)} %shard_map.122.refs_2_.refs_0_), channel_id=1, source_target_pairs={{0,16},{1,17},{2,18},{3,19},{4,20},{5,21},{6,22},{7,23},{8,24},{9,... | collective-permute-start | bytes 602120 | tf_op jit(solution)/shard_map/ppermute | solution.py:100
  86.5 4.7 %collective-permute-start.13 = (bf16[384,128]{1,0:T(8,128)(2,1)S(1)}, bf16[384,128]{1,0:T(8,128)(2,1)S(1)}, u32[]{:S(2)}, u32[]{:S(2)}) collective-permute-start(bf16[384,128]{1,0:T(8,128)(2,1)S(1)} %get-tuple-element.59), channel_id=1, source_target_pairs={{0,2},{1,3},{2,0},{3,1},{4,6},{5,7},{6,4},{7,5},{8,10},{9,11},{10,... | collective-permute-start | bytes 294920 | tf_op jit(solution)/shard_map/ppermute | solution.py:100
  87.9 5.1 %collective-permute-start.14 = (bf16[384,128]{1,0:T(8,128)(2,1)S(1)}, bf16[384,128]{1,0:T(8,128)(2,1)S(1)}, u32[]{:S(2)}, u32[]{:S(2)}) collective-permute-start(bf16[384,128]{1,0:T(8,128)(2,1)S(1)} %get-tuple-element.60), channel_id=1, source_target_pairs={{0,4},{1,5},{2,6},{3,7},{4,0},{5,1},{6,2},{7,3},{8,12},{9,13},{10,... | collective-permute-start | bytes 294920 | tf_op jit(solution)/shard_map/ppermute | solution.py:100
  89.4 5.5 %collective-permute-start.15 = (bf16[384,128]{1,0:T(8,128)(2,1)S(1)}, bf16[384,128]{1,0:T(8,128)(2,1)S(1)}, u32[]{:S(2)}, u32[]{:S(2)}) collective-permute-start(bf16[384,128]{1,0:T(8,128)(2,1)S(1)} %get-tuple-element.61), channel_id=1, source_target_pairs={{0,6},{1,7},{2,4},{3,5},{4,2},{5,3},{6,0},{7,1},{8,14},{9,15},{10,... | collective-permute-start | bytes 294920 | tf_op jit(solution)/shard_map/ppermute | solution.py:100
  95.0 6.8 %collective-permute-start.16 = (bf16[384,128]{1,0:T(8,128)(2,1)S(1)}, bf16[384,128]{1,0:T(8,128)(2,1)S(1)}, u32[]{:S(2)}, u32[]{:S(2)}) collective-permute-start(bf16[384,128]{1,0:T(8,128)(2,1)S(1)} %shard_map.124.refs_2_.refs_0_), channel_id=1, source_target_pairs={{0,8},{1,9},{2,10},{3,11},{4,12},{5,13},{6,14},{7,15},{8,0},{9,1},... | collective-permute-start | bytes 294920 | tf_op jit(solution)/shard_map/ppermute | solution.py:100
  98.2 12.0 %collective-permute-start.18 = (bf16[784,128]{1,0:T(8,128)(2,1)S(1)}, bf16[784,128]{1,0:T(8,128)(2,1)S(1)}, u32[]{:S(2)}, u32[]{:S(2)}) collective-permute-start(bf16[784,128]{1,0:T(8,128)(2,1)S(1)} %shard_map.125.refs_2_.refs_0_), channel_id=1, source_target_pairs={{0,2},{1,3},{2,0},{3,1},{4,6},{5,7},{6,4},{7,5},{8,10},{9,11},{10,... | collective-permute-start | bytes 602120 | tf_op jit(solution)/shard_map/ppermute | solution.py:100
  99.6 12.1 %collective-permute-start.19 = (bf16[784,128]{1,0:T(8,128)(2,1)S(1)}, bf16[784,128]{1,0:T(8,128)(2,1)S(1)}, u32[]{:S(2)}, u32[]{:S(2)}) collective-permute-start(bf16[784,128]{1,0:T(8,128)(2,1)S(1)} %shard_map.125.refs_2_.refs_0_), channel_id=1, source_target_pairs={{0,4},{1,5},{2,6},{3,7},{4,0},{5,1},{6,2},{7,3},{8,12},{9,13},{10,... | collective-permute-start | bytes 602120 | tf_op jit(solution)/shard_map/ppermute | solution.py:100
  101.1 10.6 %collective-permute-start.20 = (bf16[784,128]{1,0:T(8,128)(2,1)S(1)}, bf16[784,128]{1,0:T(8,128)(2,1)S(1)}, u32[]{:S(2)}, u32[]{:S(2)}) collective-permute-start(bf16[784,128]{1,0:T(8,128)(2,1)S(1)} %shard_map.125.refs_2_.refs_0_), channel_id=1, source_target_pairs={{0,6},{1,7},{2,4},{3,5},{4,2},{5,3},{6,0},{7,1},{8,14},{9,15},{10,... | collective-permute-start | bytes 602120 | tf_op jit(solution)/shard_map/ppermute | solution.py:100
  101.8 6.2 %collective-permute-start.21 = (bf16[384,128]{1,0:T(8,128)(2,1)S(1)}, bf16[384,128]{1,0:T(8,128)(2,1)S(1)}, u32[]{:S(2)}, u32[]{:S(2)}) collective-permute-start(bf16[384,128]{1,0:T(8,128)(2,1)S(1)} %shard_map.126.refs_6_.refs_0_), channel_id=1, source_target_pairs={{0,16},{1,17},{2,18},{3,19},{4,20},{5,21},{6,22},{7,23},{8,24},{9,... | collective-permute-start | bytes 294920 | tf_op jit(solution)/shard_map/ppermute | solution.py:100
  108.1 5.5 %collective-permute-start.23 = (bf16[384,128]{1,0:T(8,128)(2,1)S(1)}, bf16[384,128]{1,0:T(8,128)(2,1)S(1)}, u32[]{:S(2)}, u32[]{:S(2)}) collective-permute-start(bf16[384,128]{1,0:T(8,128)(2,1)S(1)} %shard_map.128.refs_4_.refs_0_), channel_id=1, source_target_pairs={{0,2},{1,3},{2,0},{3,1},{4,6},{5,7},{6,4},{7,5},{8,10},{9,11},{10,... | collective-permute-start | bytes 294920 | tf_op jit(solution)/shard_map/ppermute | solution.py:100
  108.8 4.8 %collective-permute-start.24 = (bf16[384,128]{1,0:T(8,128)(2,1)S(1)}, bf16[384,128]{1,0:T(8,128)(2,1)S(1)}, u32[]{:S(2)}, u32[]{:S(2)}) collective-permute-start(bf16[384,128]{1,0:T(8,128)(2,1)S(1)} %shard_map.128.refs_4_.refs_0_), channel_id=1, source_target_pairs={{0,4},{1,5},{2,6},{3,7},{4,0},{5,1},{6,2},{7,3},{8,12},{9,13},{10,... | collective-permute-start | bytes 294920 | tf_op jit(solution)/shard_map/ppermute | solution.py:100
  110.3 5.5 %collective-permute-start.25 = (bf16[384,128]{1,0:T(8,128)(2,1)S(1)}, bf16[384,128]{1,0:T(8,128)(2,1)S(1)}, u32[]{:S(2)}, u32[]{:S(2)}) collective-permute-start(bf16[384,128]{1,0:T(8,128)(2,1)S(1)} %shard_map.128.refs_4_.refs_0_), channel_id=1, source_target_pairs={{0,6},{1,7},{2,4},{3,5},{4,2},{5,3},{6,0},{7,1},{8,14},{9,15},{10,... | collective-permute-start | bytes 294920 | tf_op jit(solution)/shard_map/ppermute | solution.py:100
  111.8 4.1 %collective-permute-start.22 = (bf16[4,784,128]{2,1,0:T(8,128)(2,1)S(1)}, bf16[4,784,128]{2,1,0:T(8,128)(2,1)S(1)}, u32[]{:S(2)}, u32[]{:S(2)}) collective-permute-start(bf16[4,784,128]{2,1,0:T(8,128)(2,1)S(1)} %shard_map.129.refs_4_.refs_0_), channel_id=1, source_target_pairs={{0,1},{1,0},{2,3},{3,2},{4,5},{5,4},{6,7},{7,6},{8,9},{9,8},{10,11... | collective-permute-start | bytes 2408456 | tf_op jit(solution)/shard_map/ppermute | solution.py:100
  115.8 2.6 %collective-permute-start.26 = (bf16[4,384,128]{2,1,0:T(8,128)(2,1)S(1)}, bf16[4,384,128]{2,1,0:T(8,128)(2,1)S(1)}, u32[]{:S(2)}, u32[]{:S(2)}) collective-permute-start(bf16[4,384,128]{2,1,0:T(8,128)(2,1)S(1)} %shard_map.130.refs_2_.refs_1_), channel_id=1, source_target_pairs={{0,1},{1,0},{2,3},{3,2},{4,5},{5,4},{6,7},{7,6},{8,9},{9,8},{10,11... | collective-permute-start | bytes 1179656 | tf_op jit(solution)/shard_map/ppermute | solution.py:100

commit v4 on v3

--- a/solution.py
+++ b/solution.py
@@ -36,13 +36,15 @@
     def __init__(self):
         self.last = ()
 
-    def call(self, body, outs, operands, scratch=(), flops=0, blocked=(), key=0, far=(), alias=False):
+    def call(self, body, outs, operands, scratch=(), flops=0, blocked=(), key=0, far=(), alias=False, tap=None):
         count, earlier = len(operands), self.last
 
         def kernel(*refs):
             body(*refs[:count], *refs[count + len(earlier) :])
 
         def spec(shape, at):
+            if tap is not None and at == count - 1:
+                return pl.BlockSpec((1,) + shape[1:], lambda _: (tap, 0, 0))
             if at in far:
                 return pl.BlockSpec(memory_space=pltpu.HBM)
             if not blocked:
@@ -53,7 +55,7 @@
 
         made = pl.pallas_call(
             kernel,
-            grid=(4,) if blocked else (),
+            grid=(4,) if blocked else () if tap is None else (1,),
             out_shape=[jax.ShapeDtypeStruct(shape, dtype) for shape, dtype in outs],
             in_specs=[spec(value.shape, at) for at, value in enumerate(operands)]
             + [pl.BlockSpec(memory_space=pl.ANY)] * len(earlier),
@@ -193,7 +195,8 @@
     mine = sum(group.held_type[0][1] for group in sums)
     outs = [((mine, LANES), F32)] + [((rows, LANES), BF16)] * (blocks - 1)
     own, *sent = chain.call(run, outs, [ref for pair in halves for ref in pair])
-    return [own] + [layout.across(value, 2 * k) for k, value in enumerate(sent, 1)]
+    arrived = {k: layout.across(sent[k - 1], 2 * k) for k in range(blocks - 1, 0, -1)}
+    return [own] + [arrived[k] for k in range(1, blocks)]
 
 
 def plane_sum(chain, layout, sums, parts, flops=0):
@@ -224,7 +227,8 @@
 
 
 def back_plane(layout, sent):
-    return [sent] + [layout.across(sent, 2 * k) for k in range(1, layout.blocks)]
+    arrived = {k: layout.across(sent, 2 * k) for k in range(layout.blocks - 1, 0, -1)}
+    return [sent] + [arrived[k] for k in range(1, layout.blocks)]
 
 
 def back_core(chain, layout, parts, flops=0):
@@ -275,19 +279,21 @@
         cuts = [(0, LANES), (LANES, width)]
         chain = Chain()
 
-        def forward_taps(source, weights, early, late, activated):
-            @blocks_of(rows)
-            def _(block):
-                active = gelu_parts(source[block, :].astype(F32))[0].astype(BF16)
-                activated[block, :] = active
-                early[block, :] = dot(active, weights[0]).astype(BF16)
-                late[block, :] = dot(active, weights[2]).astype(BF16)
-
-        early, late, activated = chain.call(
-            forward_taps,
-            [((rows, width), BF16)] * 2 + [((rows, channels), BF16)],
-            (features, kernel),
-        )
+        def activate(source, activated):
+            @blocks_of(rows)
+            def _(block):
+                activated[block, :] = gelu_parts(source[block, :].astype(F32))[0].astype(BF16)
+
+        (activated,) = chain.call(activate, [((rows, channels), BF16)], (features,))
+
+        def forward_tap(active, weights, out):
+            @blocks_of(rows)
+            def _(block):
+                out[block, :] = dot(active[block, :], weights[0]).astype(BF16)
+
+        outs = [((rows, width), BF16)]
+        (early,) = chain.call(forward_tap, outs, (activated, kernel), tap=0)
+        (late,) = chain.call(forward_tap, outs, (activated, kernel), tap=2, flops=LONG)
         early, late = layout.around(early, 1), layout.around(late, -1)
 
         def local_parts(active, weights, shift, cot, mix, center, hidden_grad):

time: 120 us -> 119 us (level)
  local copies, waits for them, and re-layouts: 4.65 us -> 1.57 us
  waiting for transfers between devices: 59.3 us -> 61 us
  Pallas kernels: 23.6 us -> 24.9 us
    unnamed x16 -> x14, local copies, waits for them, and re-layouts: 3.96 us -> 1.57 us
    pallas_call x24 -> x26, Pallas kernels: 23.6 us -> 24.9 us  [call(): pl.pallas_call(kernel, grid=(4,) if blocked else () if tap is None else (...]
  transfers between devices with their start and end apart: 27 -> 27, of which waited for: 17 -> 16; matrix products, arithmetic and copies ran while one was open for 1% -> 0% of each run, Pallas kernels for 16% -> 18%
where the time goes in v4:
time: 119 us; the launch traced here: 118 us
  waiting for transfers between devices  61 us (51%)
  starting transfers between devices  30.1 us (25%)
  Pallas kernels  24.9 us (21%)
  local copies, waits for them, and re-layouts  1.57 us (1%)
    ppermute x6, waiting for transfers between devices, around(): return lax.ppermute(value, AXES, pairs)  37.6 us
    pallas_call x26, Pallas kernels, call(): pl.pallas_call(kernel, grid=(4,) if blocked else () if tap is None else (...  24.9 us
    ppermute x21, waiting for transfers between devices, across(): return lax.ppermute(value, AXES, [(i, i ^ mask) for i in range(self.count)])  23.3 us
    ppermute x21, starting transfers between devices, across(): return lax.ppermute(value, AXES, [(i, i ^ mask) for i in range(self.count)])  19.2 us
    ppermute x6, starting transfers between devices, around(): return lax.ppermute(value, AXES, pairs)  10.8 us
  transfers between devices with their start and end apart: 27, of which 16 were waited for; matrix products, arithmetic and copies ran while one was open for 0% of the time, Pallas kernels for 18%

profile of v4, /device:TPU:0, one launch (start us, length us, event | category | flops | bytes accessed | tf_op | source)
XLA Modules:
  0.0 118.5 jit_solution(8900351676916123888)
XLA Ops:
  0.7 1.5 %copy-done.2 = bf16[1024,768]{1,0:T(8,128)(2,1)S(1)} copy-done((bf16[1024,768]{1,0:T(8,128)(2,1)S(1)}, bf16[1024,768]{1,0:T(8,128)(2,1)}, u32[]{:S(2)}) %copy-start.2) | copy-done | bytes 1572888
  2.2 0.7 shard_map.109.refs_0_.refs_2_
  2.9 1.5 %shard_map.110.refs_2_ = bf16[1024,384]{1,0:T(8,128)(2,1)S(1)} custom-call(bf16[1024,768]{1,0:T(8,128)(2,1)S(1)} %shard_map.109.refs_0_.refs_2_, bf16[3,768,384]{2,1,0:T(8,128)(2,1)S(1)} %copy-done.1, bf16[1024,768]{1,0:T(8,128)(2,1)S(1)} %shard_map.109.refs_0_.refs_2_), custom_call_target="tpu_custom_call" | custom-call | tf_op jit(solution)/shard_map/pallas_call | solution.py:56
  4.4 3.1 %collective-permute-start = (bf16[1024,384]{1,0:T(8,128)(2,1)S(1)}, bf16[1024,384]{1,0:T(8,128)(2,1)S(1)}, u32[]{:S(2)}, u32[]{:S(2)}) collective-permute-start(bf16[1024,384]{1,0:T(8,128)(2,1)S(1)} %shard_map.110.refs_2_), channel_id=1, source_target_pairs={{0,8},{1,9},{2,10},{3,11},{4,12},{5,13},{6,14},{7,15},{8,16},{9,17... | collective-permute-start | bytes 2359304 | tf_op jit(solution)/shard_map/ppermute | solution.py:99
  7.5 1.5 %shard_map.111.refs_5_ = bf16[1024,384]{1,0:T(8,128)(2,1)S(1)} custom-call(bf16[1024,768]{1,0:T(8,128)(2,1)S(1)} %shard_map.109.refs_0_.refs_2_, bf16[3,768,384]{2,1,0:T(8,128)(2,1)S(1)} %copy-done.1, bf16[1024,384]{1,0:T(8,128)(2,1)S(1)} %shard_map.110.refs_2_), custom_call_target="tpu_custom_call" | custom-call | flops 8000000000 | tf_op jit(solution)/shard_map/pallas_call | solution.py:56
  9.0 2.1 %collective-permute-start.1 = (bf16[1024,384]{1,0:T(8,128)(2,1)S(1)}, bf16[1024,384]{1,0:T(8,128)(2,1)S(1)}, u32[]{:S(2)}, u32[]{:S(2)}) collective-permute-start(bf16[1024,384]{1,0:T(8,128)(2,1)S(1)} %shard_map.111.refs_5_), channel_id=1, source_target_pairs={{0,24},{1,25},{2,26},{3,27},{4,28},{5,29},{6,30},{7,31},{8,0},{9,1... | collective-permute-start | bytes 2359304 | tf_op jit(solution)/shard_map/ppermute | solution.py:99
  11.1 2.2 %shard_map.112 = (f32[1024,384]{1,0:T(8,128)S(1)}, f32[1024,384]{1,0:T(8,128)S(1)}) custom-call(bf16[1024,768]{1,0:T(8,128)(2,1)S(1)} %shard_map.109.refs_0_.refs_2_, bf16[3,768,384]{2,1,0:T(8,128)(2,1)S(1)} %copy-done.1, f32[1,384]{1,0:T(1,128)S(1)} %reshape.19.refs_2_, bf16[1024,768]{1,0:T(8,128)(2,1)S(1)} %copy-done, bf16[384,768]{1,0:T(8,128)(2,1)S(1)} %copy-done.4, ...), custom_call_target="tpu_custom_call" | custom-call | tf_op jit(solution)/shard_map/pallas_call | solution.py:56
  13.4 14.6 %collective-permute-done.refs_2_ = bf16[1024,384]{1,0:T(8,128)(2,1)S(1)} collective-permute-done((bf16[1024,384]{1,0:T(8,128)(2,1)S(1)}, bf16[1024,384]{1,0:T(8,128)(2,1)S(1)}, u32[]{:S(2)}, u32[]{:S(2)}) %collective-permute-start) | collective-permute-done | bytes 786464 | tf_op jit(solution)/shard_map/ppermute | solution.py:99
  27.9 16.0 %collective-permute-done.1.refs_3_ = bf16[1024,384]{1,0:T(8,128)(2,1)S(1)} collective-permute-done((bf16[1024,384]{1,0:T(8,128)(2,1)S(1)}, bf16[1024,384]{1,0:T(8,128)(2,1)S(1)}, u32[]{:S(2)}, u32[]{:S(2)}) %collective-permute-start.1) | collective-permute-done | bytes 786464 | tf_op jit(solution)/shard_map/ppermute | solution.py:99
  43.9 0.3 shard_map.113
  44.3 1.8 %collective-permute-start.2 = (bf16[1024,128]{1,0:T(8,128)(2,1)S(1)}, bf16[1024,128]{1,0:T(8,128)(2,1)S(1)}, u32[]{:S(2)}, u32[]{:S(2)}) collective-permute-start(bf16[1024,128]{1,0:T(8,128)(2,1)S(1)} %get-tuple-element.38.refs_1_.refs_5_.refs_6_), channel_id=1, source_target_pairs={{0,24},{1,25},{2,26},{3,27},{4,28},{5,29},{6,30},{7,31},{8,0},{9,1... | collective-permute-start | bytes 786440 | tf_op jit(solution)/shard_map/ppermute | solution.py:99
  46.1 0.3 collective-permute-start.3
  46.3 0.7 shard_map.114
  47.0 3.6 %collective-permute-start.4 = (bf16[1024,256]{1,0:T(8,128)(2,1)S(1)}, bf16[1024,256]{1,0:T(8,128)(2,1)S(1)}, u32[]{:S(2)}, u32[]{:S(2)}) collective-permute-start(bf16[1024,256]{1,0:T(8,128)(2,1)S(1)} %get-tuple-element.39.refs_2_.refs_6_.refs_7_), channel_id=1, source_target_pairs={{0,24},{1,25},{2,26},{3,27},{4,28},{5,29},{6,30},{7,31},{8,0},{9,1... | collective-permute-start | bytes 1572872 | tf_op jit(solution)/shard_map/ppermute | solution.py:99
  50.6 0.4 shard_map.115.refs_2_.refs_7_
  51.0 2.2 %shard_map.116 = (f32[4,584,128]{2,1,0:T(8,128)S(1)}, bf16[4,592,128]{2,1,0:T(8,128)(2,1)S(1)}) custom-call(bf16[1024,768]{1,0:T(8,128)(2,1)S(1)} %shard_map.109.refs_0_.refs_2_, bf16[1024,768]{1,0:T(8,128)(2,1)S(1)} %copy-done, f32[64,128]{1,0:T(8,128)S(1)} %shard_map.115.refs_2_.refs_7_, bf16[1024,128]{1,0:T(8,128)(2,1)S(1)} %get-tuple-element.36.refs_4_.refs_3_, ...), custom_call_target="tpu_custom_call" | custom-call | tf_op jit(solution)/shard_map/pallas_call | solution.py:56
  53.2 0.1 collective-permute-start.6
  53.3 3.3 %shard_map.117 = (bf16[1024,768]{1,0:T(8,128)(2,1)}, f32[1024,768]{1,0:T(8,128)S(1)}) custom-call(bf16[1024,768]{1,0:T(8,128)(2,1)S(1)} %copy-done.3, bf16[384,768]{1,0:T(8,128)(2,1)S(1)} %copy-done.4, f32[1,768]{1,0:T(1,128)S(1)} %reshape.18.refs_2_, bf16[3,768,384]{2,1,0:T(8,128)(2,1)S(1)} %copy-done.1, ...), custom_call_target="tpu_custom_call" | custom-call | flops 8000000000 | tf_op jit(solution)/shard_map/pallas_call | solution.py:56
  56.5 2.3 %collective-permute-done.2.refs_1_ = bf16[1024,128]{1,0:T(8,128)(2,1)S(1)} collective-permute-done((bf16[1024,128]{1,0:T(8,128)(2,1)S(1)}, bf16[1024,128]{1,0:T(8,128)(2,1)S(1)}, u32[]{:S(2)}, u32[]{:S(2)}) %collective-permute-start.2) | collective-permute-done | bytes 262176 | tf_op jit(solution)/shard_map/ppermute | solution.py:99
  58.8 0.6 collective-permute-done.3.refs_2_
  59.4 1.1 shard_map.118
  60.5 0.1 collective-permute-start.7
  60.5 1.5 %shard_map.119.refs_4_.refs_0_ = f32[1024,768]{1,0:T(8,128)S(1)} custom-call(f32[1024,768]{1,0:T(8,128)S(1)} %get-tuple-element.42.refs_3_.refs_0_, bf16[1024,128]{1,0:T(8,128)(2,1)S(1)} %collective-permute-done.2.refs_1_, bf16[1024,128]{1,0:T(8,128)(2,1)S(1)} %collective-permute-done.3.refs_2_, bf16[3,768,384]{2,1,0:T(8,128)(2,1)S(1)} %copy-done.1, ...), custom_call_target="tpu_custom_call" | custom-call | flops 8000000000 | tf_op jit(solution)/shard_map/pallas_call | solution.py:56
  62.0 0.2 shard_map.120
  62.2 1.6 %collective-permute-start.8 = (bf16[784,128]{1,0:T(8,128)(2,1)S(1)}, bf16[784,128]{1,0:T(8,128)(2,1)S(1)}, u32[]{:S(2)}, u32[]{:S(2)}) collective-permute-start(bf16[784,128]{1,0:T(8,128)(2,1)S(1)} %get-tuple-element.47), channel_id=1, source_target_pairs={{0,2},{1,3},{2,0},{3,1},{4,6},{5,7},{6,4},{7,5},{8,10},{9,11},{10,... | collective-permute-start | bytes 602120 | tf_op jit(solution)/shard_map/ppermute | solution.py:102
  63.8 1.5 %collective-permute-start.9 = (bf16[784,128]{1,0:T(8,128)(2,1)S(1)}, bf16[784,128]{1,0:T(8,128)(2,1)S(1)}, u32[]{:S(2)}, u32[]{:S(2)}) collective-permute-start(bf16[784,128]{1,0:T(8,128)(2,1)S(1)} %get-tuple-element.48), channel_id=1, source_target_pairs={{0,4},{1,5},{2,6},{3,7},{4,0},{5,1},{6,2},{7,3},{8,12},{9,13},{10,... | collective-permute-start | bytes 602120 | tf_op jit(solution)/shard_map/ppermute | solution.py:102
  65.3 0.5 collective-permute-start.10
  65.8 1.2 %shard_map.121.refs_4_.refs_5_ = f32[1024,768]{1,0:T(8,128)S(1)} custom-call(bf16[1024,768]{1,0:T(8,128)(2,1)S(1)} %copy-done.3, f32[776,128]{1,0:T(8,128)S(1)} %get-tuple-element.46.refs_1_.refs_0_), custom_call_target="tpu_custom_call" | custom-call | flops 8000000000 | tf_op jit(solution)/shard_map/pallas_call | solution.py:56
  67.0 2.6 %collective-permute-done.8.refs_1_ = bf16[784,128]{1,0:T(8,128)(2,1)S(1)} collective-permute-done((bf16[784,128]{1,0:T(8,128)(2,1)S(1)}, bf16[784,128]{1,0:T(8,128)(2,1)S(1)}, u32[]{:S(2)}, u32[]{:S(2)}) %collective-permute-start.8) | collective-permute-done | bytes 200736 | tf_op jit(solution)/shard_map/ppermute | solution.py:102
  69.7 2.0 %collective-permute-done.9.refs_2_ = bf16[784,128]{1,0:T(8,128)(2,1)S(1)} collective-permute-done((bf16[784,128]{1,0:T(8,128)(2,1)S(1)}, bf16[784,128]{1,0:T(8,128)(2,1)S(1)}, u32[]{:S(2)}, u32[]{:S(2)}) %collective-permute-start.9) | collective-permute-done | bytes 200736 | tf_op jit(solution)/shard_map/ppermute | solution.py:102
  71.6 3.5 %collective-permute-done.10.refs_3_ = bf16[784,128]{1,0:T(8,128)(2,1)S(1)} collective-permute-done((bf16[784,128]{1,0:T(8,128)(2,1)S(1)}, bf16[784,128]{1,0:T(8,128)(2,1)S(1)}, u32[]{:S(2)}, u32[]{:S(2)}) %collective-permute-start.10) | collective-permute-done | bytes 200736 | tf_op jit(solution)/shard_map/ppermute | solution.py:102
  75.2 0.1 shard_map.122.refs_3_.refs_0_
  75.3 1.6 %collective-permute-start.12 = (bf16[784,128]{1,0:T(8,128)(2,1)S(1)}, bf16[784,128]{1,0:T(8,128)(2,1)S(1)}, u32[]{:S(2)}, u32[]{:S(2)}) collective-permute-start(bf16[784,128]{1,0:T(8,128)(2,1)S(1)} %shard_map.122.refs_3_.refs_0_), channel_id=1, source_target_pairs={{0,8},{1,9},{2,10},{3,11},{4,12},{5,13},{6,14},{7,15},{8,0},{9,1},... | collective-permute-start | bytes 602120 | tf_op jit(solution)/shard_map/ppermute | solution.py:102
  76.9 4.2 %collective-permute-done.4.refs_1_ = bf16[1024,256]{1,0:T(8,128)(2,1)S(1)} collective-permute-done((bf16[1024,256]{1,0:T(8,128)(2,1)S(1)}, bf16[1024,256]{1,0:T(8,128)(2,1)S(1)}, u32[]{:S(2)}, u32[]{:S(2)}) %collective-permute-start.4) | collective-permute-done | bytes 524320 | tf_op jit(solution)/shard_map/ppermute | solution.py:99
  81.1 1.2 %shard_map.123 = (f32[4,384,128]{2,1,0:T(8,128)S(1)}, bf16[4,384,128]{2,1,0:T(8,128)(2,1)S(1)}) custom-call(bf16[1024,768]{1,0:T(8,128)(2,1)S(1)} %shard_map.109.refs_0_.refs_2_, bf16[1024,256]{1,0:T(8,128)(2,1)S(1)} %collective-permute-done.4.refs_1_, bf16[1024,256]{1,0:T(8,128)(2,1)S(1)} %collective-permute-done.5.refs_2_, ...), custom_call_target="tpu_custom_call" | custom-call | flops 8000000000 | tf_op jit(solution)/shard_map/pallas_call | solution.py:56
  82.3 0.1 collective-permute-start.11
  82.3 2.6 %collective-permute-done.12.refs_1_ = bf16[784,128]{1,0:T(8,128)(2,1)S(1)} collective-permute-done((bf16[784,128]{1,0:T(8,128)(2,1)S(1)}, bf16[784,128]{1,0:T(8,128)(2,1)S(1)}, u32[]{:S(2)}, u32[]{:S(2)}) %collective-permute-start.12) | collective-permute-done | bytes 200736 | tf_op jit(solution)/shard_map/ppermute | solution.py:102
  85.0 0.1 collective-permute-start.17
  85.1 0.1 shard_map.125
  85.2 1.6 %collective-permute-start.13 = (bf16[384,128]{1,0:T(8,128)(2,1)S(1)}, bf16[384,128]{1,0:T(8,128)(2,1)S(1)}, u32[]{:S(2)}, u32[]{:S(2)}) collective-permute-start(bf16[384,128]{1,0:T(8,128)(2,1)S(1)} %get-tuple-element.53), channel_id=1, source_target_pairs={{0,2},{1,3},{2,0},{3,1},{4,6},{5,7},{6,4},{7,5},{8,10},{9,11},{10,... | collective-permute-start | bytes 294920 | tf_op jit(solution)/shard_map/ppermute | solution.py:102
  86.8 1.5 %collective-permute-start.14 = (bf16[384,128]{1,0:T(8,128)(2,1)S(1)}, bf16[384,128]{1,0:T(8,128)(2,1)S(1)}, u32[]{:S(2)}, u32[]{:S(2)}) collective-permute-start(bf16[384,128]{1,0:T(8,128)(2,1)S(1)} %get-tuple-element.54), channel_id=1, source_target_pairs={{0,4},{1,5},{2,6},{3,7},{4,0},{5,1},{6,2},{7,3},{8,12},{9,13},{10,... | collective-permute-start | bytes 294920 | tf_op jit(solution)/shard_map/ppermute | solution.py:102
  88.2 0.5 collective-permute-start.15
  88.7 1.1 collective-permute-done.13.refs_1_
  89.8 1.9 %collective-permute-done.14.refs_2_ = bf16[384,128]{1,0:T(8,128)(2,1)S(1)} collective-permute-done((bf16[384,128]{1,0:T(8,128)(2,1)S(1)}, bf16[384,128]{1,0:T(8,128)(2,1)S(1)}, u32[]{:S(2)}, u32[]{:S(2)}) %collective-permute-start.14) | collective-permute-done | bytes 98336 | tf_op jit(solution)/shard_map/ppermute | solution.py:102
  91.8 2.0 %collective-permute-done.15.refs_3_ = bf16[384,128]{1,0:T(8,128)(2,1)S(1)} collective-permute-done((bf16[384,128]{1,0:T(8,128)(2,1)S(1)}, bf16[384,128]{1,0:T(8,128)(2,1)S(1)}, u32[]{:S(2)}, u32[]{:S(2)}) %collective-permute-start.15) | collective-permute-done | bytes 98336 | tf_op jit(solution)/shard_map/ppermute | solution.py:102
  93.8 2.1 %collective-permute-start.16 = (bf16[384,128]{1,0:T(8,128)(2,1)S(1)}, bf16[384,128]{1,0:T(8,128)(2,1)S(1)}, u32[]{:S(2)}, u32[]{:S(2)}) collective-permute-start(bf16[384,128]{1,0:T(8,128)(2,1)S(1)} %shard_map.126.refs_2_.refs_0_), channel_id=1, source_target_pairs={{0,8},{1,9},{2,10},{3,11},{4,12},{5,13},{6,14},{7,15},{8,0},{9,1},... | collective-permute-start | bytes 294920 | tf_op jit(solution)/shard_map/ppermute | solution.py:102
  95.9 1.0 collective-permute-done.17.refs_1_
  96.9 0.1 shard_map.127.refs_2_.refs_0_
  97.0 1.4 %collective-permute-start.18 = (bf16[784,128]{1,0:T(8,128)(2,1)S(1)}, bf16[784,128]{1,0:T(8,128)(2,1)S(1)}, u32[]{:S(2)}, u32[]{:S(2)}) collective-permute-start(bf16[784,128]{1,0:T(8,128)(2,1)S(1)} %shard_map.127.refs_2_.refs_0_), channel_id=1, source_target_pairs={{0,2},{1,3},{2,0},{3,1},{4,6},{5,7},{6,4},{7,5},{8,10},{9,11},{10,... | collective-permute-start | bytes 602120 | tf_op jit(solution)/shard_map/ppermute | solution.py:102
  98.3 1.5 %collective-permute-start.19 = (bf16[784,128]{1,0:T(8,128)(2,1)S(1)}, bf16[784,128]{1,0:T(8,128)(2,1)S(1)}, u32[]{:S(2)}, u32[]{:S(2)}) collective-permute-start(bf16[784,128]{1,0:T(8,128)(2,1)S(1)} %shard_map.127.refs_2_.refs_0_), channel_id=1, source_target_pairs={{0,4},{1,5},{2,6},{3,7},{4,0},{5,1},{6,2},{7,3},{8,12},{9,13},{10,... | collective-permute-start | bytes 602120 | tf_op jit(solution)/shard_map/ppermute | solution.py:102
  99.8 0.7 collective-permute-start.20
  100.5 0.9 collective-permute-start.21
  101.5 2.8 %shard_map.129 = (bf16[1024,768]{1,0:T(8,128)(2,1)}, f32[8,128]{1,0:T(8,128)S(1)}) custom-call(f32[1024,768]{1,0:T(8,128)S(1)} %shard_map.119.refs_4_.refs_0_, bf16[1024,256]{1,0:T(8,128)(2,1)S(1)} %collective-permute-done.4.refs_1_, bf16[1024,256]{1,0:T(8,128)(2,1)S(1)} %collective-permute-done.5.refs_2_, bf16[3,768,384]{2,1,0:T(8,128)(2,1)S(1)} %copy-done.1, ...), custom_call_target="tpu_custom_call" | custom-call | flops 8000000000 | tf_op jit(solution)/shard_map/pallas_call | solution.py:56
  104.3 2.3 %collective-permute-done.21.refs_1_ = bf16[384,128]{1,0:T(8,128)(2,1)S(1)} collective-permute-done((bf16[384,128]{1,0:T(8,128)(2,1)S(1)}, bf16[384,128]{1,0:T(8,128)(2,1)S(1)}, u32[]{:S(2)}, u32[]{:S(2)}) %collective-permute-start.21) | collective-permute-done | bytes 98336 | tf_op jit(solution)/shard_map/ppermute | solution.py:102
  106.6 0.9 collective-permute-start.23
  107.5 1.5 %collective-permute-start.24 = (bf16[384,128]{1,0:T(8,128)(2,1)S(1)}, bf16[384,128]{1,0:T(8,128)(2,1)S(1)}, u32[]{:S(2)}, u32[]{:S(2)}) collective-permute-start(bf16[384,128]{1,0:T(8,128)(2,1)S(1)} %shard_map.130.refs_4_.refs_0_), channel_id=1, source_target_pairs={{0,4},{1,5},{2,6},{3,7},{4,0},{5,1},{6,2},{7,3},{8,12},{9,13},{10,... | collective-permute-start | bytes 294920 | tf_op jit(solution)/shard_map/ppermute | solution.py:102
  109.0 1.1 collective-permute-start.25
  110.2 0.1 shard_map.131.refs_4_.refs_0_
  110.2 0.1 collective-permute-start.22
  110.3 2.2 %collective-permute-done.23.refs_1_ = bf16[384,128]{1,0:T(8,128)(2,1)S(1)} collective-permute-done((bf16[384,128]{1,0:T(8,128)(2,1)S(1)}, bf16[384,128]{1,0:T(8,128)(2,1)S(1)}, u32[]{:S(2)}, u32[]{:S(2)}) %collective-permute-start.23) | collective-permute-done | bytes 98336 | tf_op jit(solution)/shard_map/ppermute | solution.py:102
  112.5 2.1 %collective-permute-done.25.refs_3_ = bf16[384,128]{1,0:T(8,128)(2,1)S(1)} collective-permute-done((bf16[384,128]{1,0:T(8,128)(2,1)S(1)}, bf16[384,128]{1,0:T(8,128)(2,1)S(1)}, u32[]{:S(2)}, u32[]{:S(2)}) %collective-permute-start.25) | collective-permute-done | bytes 98336 | tf_op jit(solution)/shard_map/ppermute | solution.py:102
  114.6 0.1 collective-permute-start.26
  114.7 2.5 %shard_map.133 = (f32[3,768,384]{2,1,0:T(8,128)}, f32[384,768]{1,0:T(8,128)}, f32[768]{0:T(1024)}, f32[384]{0:T(512)}) custom-call(bf16[4,784,128]{2,1,0:T(8,128)(2,1)S(1)} %shard_map.131.refs_4_.refs_0_, bf16[4,784,128]{2,1,0:T(8,128)(2,1)S(1)} %collective-permute-done.22.refs_1_, bf16[4,384,128]{2,1,0:T(8,128)(2,1)S(1)} %shard_map.132.refs_2_.refs_1_), custom_call_target="tpu_custom_call" | custom-call | tf_op jit(solution)/shard_map/pallas_call | solution.py:56
  117.2 1.3 %shard_map.134 = f32[3,768,384]{2,1,0:T(8,128)} custom-call(f32[3,768,384]{2,1,0:T(8,128)} %get-tuple-element.58.refs_0_, bf16[4,384,128]{2,1,0:T(8,128)(2,1)S(1)} %shard_map.132.refs_2_.refs_1_, bf16[4,384,128]{2,1,0:T(8,128)(2,1)S(1)} %collective-permute-done.26.refs_2_), custom_call_target="tpu_custom_call", output_to_operand_aliasing={{}: (0, {})} | custom-call | tf_op jit(solution)/shard_map/pallas_call | solution.py:56
  (32 shorter events, 0.2 us)
Async XLA Ops:
  0.6 2.3 %copy-start.1 = (bf16[3,768,384]{2,1,0:T(8,128)(2,1)S(1)}, bf16[3,768,384]{2,1,0:T(8,128)(2,1)}, u32[]{:S(2)}) copy-start(bf16[3,768,384]{2,1,0:T(8,128)(2,1)} %refs_3_.7) | copy-start | bytes 5308420
  0.6 1.5 %copy-start.2 = (bf16[1024,768]{1,0:T(8,128)(2,1)S(1)}, bf16[1024,768]{1,0:T(8,128)(2,1)}, u32[]{:S(2)}) copy-start(bf16[1024,768]{1,0:T(8,128)(2,1)} %refs_0_.7) | copy-start | bytes 4718596
  4.4 6.7 %copy-start.5 = (f32[768]{0:T(1024)S(1)}, f32[768]{0:T(1024)}, u32[]{:S(2)}) copy-start(f32[768]{0:T(1024)} %param.10) | copy-start | bytes 9220
  4.4 6.7 %copy-start.6 = (f32[384]{0:T(512)S(1)}, f32[384]{0:T(512)}, u32[]{:S(2)}) copy-start(f32[384]{0:T(512)} %param.8) | copy-start | bytes 4612
  4.4 6.7 %copy-start = (bf16[1024,768]{1,0:T(8,128)(2,1)S(1)}, bf16[1024,768]{1,0:T(8,128)(2,1)}, u32[]{:S(2)}) copy-start(bf16[1024,768]{1,0:T(8,128)(2,1)} %refs_4_.3) | copy-start | bytes 4718596
  4.4 6.7 %copy-start.4 = (bf16[384,768]{1,0:T(8,128)(2,1)S(1)}, bf16[384,768]{1,0:T(8,128)(2,1)}, u32[]{:S(2)}) copy-start(bf16[384,768]{1,0:T(8,128)(2,1)} %refs_1_.9) | copy-start | bytes 1769476
  4.4 23.5 %collective-permute-start = (bf16[1024,384]{1,0:T(8,128)(2,1)S(1)}, bf16[1024,384]{1,0:T(8,128)(2,1)S(1)}, u32[]{:S(2)}, u32[]{:S(2)}) collective-permute-start(bf16[1024,384]{1,0:T(8,128)(2,1)S(1)} %shard_map.110.refs_2_), channel_id=1, source_target_pairs={{0,8},{1,9},{2,10},{3,11},{4,12},{5,13},{6,14},{7,15},{8,16},{9,17... | collective-permute-start | bytes 2359304 | tf_op jit(solution)/shard_map/ppermute | solution.py:99
  9.0 34.9 %collective-permute-start.1 = (bf16[1024,384]{1,0:T(8,128)(2,1)S(1)}, bf16[1024,384]{1,0:T(8,128)(2,1)S(1)}, u32[]{:S(2)}, u32[]{:S(2)}) collective-permute-start(bf16[1024,384]{1,0:T(8,128)(2,1)S(1)} %shard_map.111.refs_5_), channel_id=1, source_target_pairs={{0,24},{1,25},{2,26},{3,27},{4,28},{5,29},{6,30},{7,31},{8,0},{9,1... | collective-permute-start | bytes 2359304 | tf_op jit(solution)/shard_map/ppermute | solution.py:99
  44.3 14.5 %collective-permute-start.2 = (bf16[1024,128]{1,0:T(8,128)(2,1)S(1)}, bf16[1024,128]{1,0:T(8,128)(2,1)S(1)}, u32[]{:S(2)}, u32[]{:S(2)}) collective-permute-start(bf16[1024,128]{1,0:T(8,128)(2,1)S(1)} %get-tuple-element.38.refs_1_.refs_5_.refs_6_), channel_id=1, source_target_pairs={{0,24},{1,25},{2,26},{3,27},{4,28},{5,29},{6,30},{7,31},{8,0},{9,1... | collective-permute-start | bytes 786440 | tf_op jit(solution)/shard_map/ppermute | solution.py:99
  46.1 13.3 %collective-permute-start.3 = (bf16[1024,128]{1,0:T(8,128)(2,1)S(1)}, bf16[1024,128]{1,0:T(8,128)(2,1)S(1)}, u32[]{:S(2)}, u32[]{:S(2)}) collective-permute-start(bf16[1024,128]{1,0:T(8,128)(2,1)S(1)} %get-tuple-element.38.refs_1_.refs_5_.refs_6_), channel_id=1, source_target_pairs={{0,8},{1,9},{2,10},{3,11},{4,12},{5,13},{6,14},{7,15},{8,16},{9,17... | collective-permute-start | bytes 786440 | tf_op jit(solution)/shard_map/ppermute | solution.py:99
  47.0 34.1 %collective-permute-start.4 = (bf16[1024,256]{1,0:T(8,128)(2,1)S(1)}, bf16[1024,256]{1,0:T(8,128)(2,1)S(1)}, u32[]{:S(2)}, u32[]{:S(2)}) collective-permute-start(bf16[1024,256]{1,0:T(8,128)(2,1)S(1)} %get-tuple-element.39.refs_2_.refs_6_.refs_7_), channel_id=1, source_target_pairs={{0,24},{1,25},{2,26},{3,27},{4,28},{5,29},{6,30},{7,31},{8,0},{9,1... | collective-permute-start | bytes 1572872 | tf_op jit(solution)/shard_map/ppermute | solution.py:99
  50.6 30.5 %collective-permute-start.5 = (bf16[1024,256]{1,0:T(8,128)(2,1)S(1)}, bf16[1024,256]{1,0:T(8,128)(2,1)S(1)}, u32[]{:S(2)}, u32[]{:S(2)}) collective-permute-start(bf16[1024,256]{1,0:T(8,128)(2,1)S(1)} %get-tuple-element.39.refs_2_.refs_6_.refs_7_), channel_id=1, source_target_pairs={{0,8},{1,9},{2,10},{3,11},{4,12},{5,13},{6,14},{7,15},{8,16},{9,17... | collective-permute-start | bytes 1572872 | tf_op jit(solution)/shard_map/ppermute | solution.py:99
  51.0 2.2 %copy-start.3 = (bf16[1024,768]{1,0:T(8,128)(2,1)S(1)}, bf16[1024,768]{1,0:T(8,128)(2,1)}, u32[]{:S(2)}) copy-start(bf16[1024,768]{1,0:T(8,128)(2,1)} %refs_0_.7) | copy-start | bytes 4718596
  53.2 8.9 %collective-permute-start.6 = (bf16[4,592,128]{2,1,0:T(8,128)(2,1)S(1)}, bf16[4,592,128]{2,1,0:T(8,128)(2,1)S(1)}, u32[]{:S(2)}, u32[]{:S(2)}) collective-permute-start(bf16[4,592,128]{2,1,0:T(8,128)(2,1)S(1)} %get-tuple-element.44), channel_id=1, source_target_pairs={{0,1},{1,0},{2,3},{3,2},{4,5},{5,4},{6,7},{7,6},{8,9},{9,8},{10,11... | collective-permute-start | bytes 1818632 | tf_op jit(solution)/shard_map/ppermute | solution.py:102
  60.5 1.6 %collective-permute-start.7 = (bf16[4,192,128]{2,1,0:T(8,128)(2,1)S(1)}, bf16[4,192,128]{2,1,0:T(8,128)(2,1)S(1)}, u32[]{:S(2)}, u32[]{:S(2)}) collective-permute-start(bf16[4,192,128]{2,1,0:T(8,128)(2,1)S(1)} %get-tuple-element.45), channel_id=1, source_target_pairs={{0,1},{1,0},{2,3},{3,2},{4,5},{5,4},{6,7},{7,6},{8,9},{9,8},{10,11... | collective-permute-start | bytes 589832 | tf_op jit(solution)/shard_map/ppermute | solution.py:102
  62.2 7.5 %collective-permute-start.8 = (bf16[784,128]{1,0:T(8,128)(2,1)S(1)}, bf16[784,128]{1,0:T(8,128)(2,1)S(1)}, u32[]{:S(2)}, u32[]{:S(2)}) collective-permute-start(bf16[784,128]{1,0:T(8,128)(2,1)S(1)} %get-tuple-element.47), channel_id=1, source_target_pairs={{0,2},{1,3},{2,0},{3,1},{4,6},{5,7},{6,4},{7,5},{8,10},{9,11},{10,... | collective-permute-start | bytes 602120 | tf_op jit(solution)/shard_map/ppermute | solution.py:102
  63.8 7.8 %collective-permute-start.9 = (bf16[784,128]{1,0:T(8,128)(2,1)S(1)}, bf16[784,128]{1,0:T(8,128)(2,1)S(1)}, u32[]{:S(2)}, u32[]{:S(2)}) collective-permute-start(bf16[784,128]{1,0:T(8,128)(2,1)S(1)} %get-tuple-element.48), channel_id=1, source_target_pairs={{0,4},{1,5},{2,6},{3,7},{4,0},{5,1},{6,2},{7,3},{8,12},{9,13},{10,... | collective-permute-start | bytes 602120 | tf_op jit(solution)/shard_map/ppermute | solution.py:102
  65.3 9.9 %collective-permute-start.10 = (bf16[784,128]{1,0:T(8,128)(2,1)S(1)}, bf16[784,128]{1,0:T(8,128)(2,1)S(1)}, u32[]{:S(2)}, u32[]{:S(2)}) collective-permute-start(bf16[784,128]{1,0:T(8,128)(2,1)S(1)} %get-tuple-element.49), channel_id=1, source_target_pairs={{0,6},{1,7},{2,4},{3,5},{4,2},{5,3},{6,0},{7,1},{8,14},{9,15},{10,... | collective-permute-start | bytes 602120 | tf_op jit(solution)/shard_map/ppermute | solution.py:102
  75.3 9.7 %collective-permute-start.12 = (bf16[784,128]{1,0:T(8,128)(2,1)S(1)}, bf16[784,128]{1,0:T(8,128)(2,1)S(1)}, u32[]{:S(2)}, u32[]{:S(2)}) collective-permute-start(bf16[784,128]{1,0:T(8,128)(2,1)S(1)} %shard_map.122.refs_3_.refs_0_), channel_id=1, source_target_pairs={{0,8},{1,9},{2,10},{3,11},{4,12},{5,13},{6,14},{7,15},{8,0},{9,1},... | collective-permute-start | bytes 602120 | tf_op jit(solution)/shard_map/ppermute | solution.py:102
  82.3 2.8 %collective-permute-start.11 = (bf16[4,384,128]{2,1,0:T(8,128)(2,1)S(1)}, bf16[4,384,128]{2,1,0:T(8,128)(2,1)S(1)}, u32[]{:S(2)}, u32[]{:S(2)}) collective-permute-start(bf16[4,384,128]{2,1,0:T(8,128)(2,1)S(1)} %get-tuple-element.51), channel_id=1, source_target_pairs={{0,1},{1,0},{2,3},{3,2},{4,5},{5,4},{6,7},{7,6},{8,9},{9,8},{10,11... | collective-permute-start | bytes 1179656 | tf_op jit(solution)/shard_map/ppermute | solution.py:102
  85.0 11.9 %collective-permute-start.17 = (bf16[784,128]{1,0:T(8,128)(2,1)S(1)}, bf16[784,128]{1,0:T(8,128)(2,1)S(1)}, u32[]{:S(2)}, u32[]{:S(2)}) collective-permute-start(bf16[784,128]{1,0:T(8,128)(2,1)S(1)} %shard_map.124.refs_2_.refs_0_), channel_id=1, source_target_pairs={{0,16},{1,17},{2,18},{3,19},{4,20},{5,21},{6,22},{7,23},{8,24},{9,... | collective-permute-start | bytes 602120 | tf_op jit(solution)/shard_map/ppermute | solution.py:102
  85.2 4.7 %collective-permute-start.13 = (bf16[384,128]{1,0:T(8,128)(2,1)S(1)}, bf16[384,128]{1,0:T(8,128)(2,1)S(1)}, u32[]{:S(2)}, u32[]{:S(2)}) collective-permute-start(bf16[384,128]{1,0:T(8,128)(2,1)S(1)} %get-tuple-element.53), channel_id=1, source_target_pairs={{0,2},{1,3},{2,0},{3,1},{4,6},{5,7},{6,4},{7,5},{8,10},{9,11},{10,... | collective-permute-start | bytes 294920 | tf_op jit(solution)/shard_map/ppermute | solution.py:102
  86.8 5.0 %collective-permute-start.14 = (bf16[384,128]{1,0:T(8,128)(2,1)S(1)}, bf16[384,128]{1,0:T(8,128)(2,1)S(1)}, u32[]{:S(2)}, u32[]{:S(2)}) collective-permute-start(bf16[384,128]{1,0:T(8,128)(2,1)S(1)} %get-tuple-element.54), channel_id=1, source_target_pairs={{0,4},{1,5},{2,6},{3,7},{4,0},{5,1},{6,2},{7,3},{8,12},{9,13},{10,... | collective-permute-start | bytes 294920 | tf_op jit(solution)/shard_map/ppermute | solution.py:102
  88.2 5.5 %collective-permute-start.15 = (bf16[384,128]{1,0:T(8,128)(2,1)S(1)}, bf16[384,128]{1,0:T(8,128)(2,1)S(1)}, u32[]{:S(2)}, u32[]{:S(2)}) collective-permute-start(bf16[384,128]{1,0:T(8,128)(2,1)S(1)} %get-tuple-element.55), channel_id=1, source_target_pairs={{0,6},{1,7},{2,4},{3,5},{4,2},{5,3},{6,0},{7,1},{8,14},{9,15},{10,... | collective-permute-start | bytes 294920 | tf_op jit(solution)/shard_map/ppermute | solution.py:102
  93.8 6.7 %collective-permute-start.16 = (bf16[384,128]{1,0:T(8,128)(2,1)S(1)}, bf16[384,128]{1,0:T(8,128)(2,1)S(1)}, u32[]{:S(2)}, u32[]{:S(2)}) collective-permute-start(bf16[384,128]{1,0:T(8,128)(2,1)S(1)} %shard_map.126.refs_2_.refs_0_), channel_id=1, source_target_pairs={{0,8},{1,9},{2,10},{3,11},{4,12},{5,13},{6,14},{7,15},{8,0},{9,1},... | collective-permute-start | bytes 294920 | tf_op jit(solution)/shard_map/ppermute | solution.py:102
  97.0 12.1 %collective-permute-start.18 = (bf16[784,128]{1,0:T(8,128)(2,1)S(1)}, bf16[784,128]{1,0:T(8,128)(2,1)S(1)}, u32[]{:S(2)}, u32[]{:S(2)}) collective-permute-start(bf16[784,128]{1,0:T(8,128)(2,1)S(1)} %shard_map.127.refs_2_.refs_0_), channel_id=1, source_target_pairs={{0,2},{1,3},{2,0},{3,1},{4,6},{5,7},{6,4},{7,5},{8,10},{9,11},{10,... | collective-permute-start | bytes 602120 | tf_op jit(solution)/shard_map/ppermute | solution.py:102
  98.3 11.8 %collective-permute-start.19 = (bf16[784,128]{1,0:T(8,128)(2,1)S(1)}, bf16[784,128]{1,0:T(8,128)(2,1)S(1)}, u32[]{:S(2)}, u32[]{:S(2)}) collective-permute-start(bf16[784,128]{1,0:T(8,128)(2,1)S(1)} %shard_map.127.refs_2_.refs_0_), channel_id=1, source_target_pairs={{0,4},{1,5},{2,6},{3,7},{4,0},{5,1},{6,2},{7,3},{8,12},{9,13},{10,... | collective-permute-start | bytes 602120 | tf_op jit(solution)/shard_map/ppermute | solution.py:102
  99.8 10.4 %collective-permute-start.20 = (bf16[784,128]{1,0:T(8,128)(2,1)S(1)}, bf16[784,128]{1,0:T(8,128)(2,1)S(1)}, u32[]{:S(2)}, u32[]{:S(2)}) collective-permute-start(bf16[784,128]{1,0:T(8,128)(2,1)S(1)} %shard_map.127.refs_2_.refs_0_), channel_id=1, source_target_pairs={{0,6},{1,7},{2,4},{3,5},{4,2},{5,3},{6,0},{7,1},{8,14},{9,15},{10,... | collective-permute-start | bytes 602120 | tf_op jit(solution)/shard_map/ppermute | solution.py:102
  100.5 6.0 %collective-permute-start.21 = (bf16[384,128]{1,0:T(8,128)(2,1)S(1)}, bf16[384,128]{1,0:T(8,128)(2,1)S(1)}, u32[]{:S(2)}, u32[]{:S(2)}) collective-permute-start(bf16[384,128]{1,0:T(8,128)(2,1)S(1)} %shard_map.128.refs_6_.refs_0_), channel_id=1, source_target_pairs={{0,16},{1,17},{2,18},{3,19},{4,20},{5,21},{6,22},{7,23},{8,24},{9,... | collective-permute-start | bytes 294920 | tf_op jit(solution)/shard_map/ppermute | solution.py:102
  106.6 5.9 %collective-permute-start.23 = (bf16[384,128]{1,0:T(8,128)(2,1)S(1)}, bf16[384,128]{1,0:T(8,128)(2,1)S(1)}, u32[]{:S(2)}, u32[]{:S(2)}) collective-permute-start(bf16[384,128]{1,0:T(8,128)(2,1)S(1)} %shard_map.130.refs_4_.refs_0_), channel_id=1, source_target_pairs={{0,2},{1,3},{2,0},{3,1},{4,6},{5,7},{6,4},{7,5},{8,10},{9,11},{10,... | collective-permute-start | bytes 294920 | tf_op jit(solution)/shard_map/ppermute | solution.py:102
  107.5 4.9 %collective-permute-start.24 = (bf16[384,128]{1,0:T(8,128)(2,1)S(1)}, bf16[384,128]{1,0:T(8,128)(2,1)S(1)}, u32[]{:S(2)}, u32[]{:S(2)}) collective-permute-start(bf16[384,128]{1,0:T(8,128)(2,1)S(1)} %shard_map.130.refs_4_.refs_0_), channel_id=1, source_target_pairs={{0,4},{1,5},{2,6},{3,7},{4,0},{5,1},{6,2},{7,3},{8,12},{9,13},{10,... | collective-permute-start | bytes 294920 | tf_op jit(solution)/shard_map/ppermute | solution.py:102
  109.0 5.5 %collective-permute-start.25 = (bf16[384,128]{1,0:T(8,128)(2,1)S(1)}, bf16[384,128]{1,0:T(8,128)(2,1)S(1)}, u32[]{:S(2)}, u32[]{:S(2)}) collective-permute-start(bf16[384,128]{1,0:T(8,128)(2,1)S(1)} %shard_map.130.refs_4_.refs_0_), channel_id=1, source_target_pairs={{0,6},{1,7},{2,4},{3,5},{4,2},{5,3},{6,0},{7,1},{8,14},{9,15},{10,... | collective-permute-start | bytes 294920 | tf_op jit(solution)/shard_map/ppermute | solution.py:102
  110.2 4.4 %collective-permute-start.22 = (bf16[4,784,128]{2,1,0:T(8,128)(2,1)S(1)}, bf16[4,784,128]{2,1,0:T(8,128)(2,1)S(1)}, u32[]{:S(2)}, u32[]{:S(2)}) collective-permute-start(bf16[4,784,128]{2,1,0:T(8,128)(2,1)S(1)} %shard_map.131.refs_4_.refs_0_), channel_id=1, source_target_pairs={{0,1},{1,0},{2,3},{3,2},{4,5},{5,4},{6,7},{7,6},{8,9},{9,8},{10,11... | collective-permute-start | bytes 2408456 | tf_op jit(solution)/shard_map/ppermute | solution.py:102
  114.6 2.6 %collective-permute-start.26 = (bf16[4,384,128]{2,1,0:T(8,128)(2,1)S(1)}, bf16[4,384,128]{2,1,0:T(8,128)(2,1)S(1)}, u32[]{:S(2)}, u32[]{:S(2)}) collective-permute-start(bf16[4,384,128]{2,1,0:T(8,128)(2,1)S(1)} %shard_map.132.refs_2_.refs_1_), channel_id=1, source_target_pairs={{0,1},{1,0},{2,3},{3,2},{4,5},{5,4},{6,7},{7,6},{8,9},{9,8},{10,11... | collective-permute-start | bytes 1179656 | tf_op jit(solution)/shard_map/ppermute | solution.py:102

commit v5 on v4

--- a/solution.py
+++ b/solution.py
@@ -279,12 +279,18 @@
         cuts = [(0, LANES), (LANES, width)]
         chain = Chain()
 
-        def activate(source, activated):
-            @blocks_of(rows)
-            def _(block):
-                activated[block, :] = gelu_parts(source[block, :].astype(F32))[0].astype(BF16)
-
-        (activated,) = chain.call(activate, [((rows, channels), BF16)], (features,))
+        def activate_and_tap(source, weights, out, activated):
+            active = gelu_parts(source[...].astype(F32))[0].astype(BF16)
+            activated[...] = active
+            out[...] = dot(active, weights[0]).astype(BF16)
+
+        early, activated = chain.call(
+            activate_and_tap,
+            [((rows, width), BF16), ((rows, channels), BF16)],
+            (features, kernel),
+            blocked=(1, 0, 1, 1),
+            tap=0,
+        )
 
         def forward_tap(active, weights, out):
             @blocks_of(rows)
@@ -292,7 +298,6 @@
                 out[block, :] = dot(active[block, :], weights[0]).astype(BF16)
 
         outs = [((rows, width), BF16)]
-        (early,) = chain.call(forward_tap, outs, (activated, kernel), tap=0)
         (late,) = chain.call(forward_tap, outs, (activated, kernel), tap=2, flops=LONG)
         early, late = layout.around(early, 1), layout.around(late, -1)
 

time: 119 us -> 119 us (level)
  local copies, waits for them, and re-layouts: 1.57 us -> 2.91 us
    unnamed x14 -> x16, local copies, waits for them, and re-layouts: 1.57 us -> 2.9 us
    pallas_call x26 -> x25, Pallas kernels: 24.9 us -> 24.3 us  [call(): pl.pallas_call(kernel, grid=(4,) if blocked else () if tap is None else (...]
where the time goes in v5:
time: 119 us
  waiting for transfers between devices  60.9 us (51%)
  starting transfers between devices  30.1 us (25%)
  Pallas kernels  24.3 us (20%)
  local copies, waits for them, and re-layouts  2.91 us (2%)
    ppermute x6, waiting for transfers between devices, around(): return lax.ppermute(value, AXES, pairs)  37.5 us
    pallas_call x25, Pallas kernels, call(): pl.pallas_call(kernel, grid=(4,) if blocked else () if tap is None else (...  24.3 us
    ppermute x21, waiting for transfers between devices, across(): return lax.ppermute(value, AXES, [(i, i ^ mask) for i in range(self.count)])  23.4 us
    ppermute x21, starting transfers between devices, across(): return lax.ppermute(value, AXES, [(i, i ^ mask) for i in range(self.count)])  19.2 us
    ppermute x6, starting transfers between devices, around(): return lax.ppermute(value, AXES, pairs)  10.9 us
    unnamed x16, local copies, waits for them, and re-layouts  2.9 us
  transfers between devices with their start and end apart: 27, of which 16 were waited for; matrix products, arithmetic and copies ran while one was open for 0% of the time, Pallas kernels for 18%

profile of v5, /device:TPU:0, one launch (start us, length us, event | category | flops | bytes accessed | tf_op | source)
XLA Modules:
  0.0 119.1 jit_solution(12352370231133495076)
XLA Ops:
  0.6 1.5 %copy-done.1 = bf16[3,768,384]{2,1,0:T(8,128)(2,1)S(1)} copy-done((bf16[3,768,384]{2,1,0:T(8,128)(2,1)S(1)}, bf16[3,768,384]{2,1,0:T(8,128)(2,1)}, u32[]{:S(2)}) %copy-start.1) | copy-done | bytes 1769496
  2.1 1.4 %copy-done.3 = bf16[1024,768]{1,0:T(8,128)(2,1)S(1)} copy-done((bf16[1024,768]{1,0:T(8,128)(2,1)S(1)}, bf16[1024,768]{1,0:T(8,128)(2,1)}, u32[]{:S(2)}) %copy-start.3) | copy-done | bytes 1572888
  3.5 1.5 %shard_map.109 = (bf16[1024,384]{1,0:T(8,128)(2,1)S(1)}, bf16[1024,768]{1,0:T(8,128)(2,1)S(1)}) custom-call(bf16[1024,768]{1,0:T(8,128)(2,1)S(1)} %copy-done.3, bf16[3,768,384]{2,1,0:T(8,128)(2,1)S(1)} %copy-done.1), custom_call_target="tpu_custom_call" | custom-call | tf_op jit(solution)/shard_map/pallas_call | solution.py:56
  5.0 3.1 %collective-permute-start = (bf16[1024,384]{1,0:T(8,128)(2,1)S(1)}, bf16[1024,384]{1,0:T(8,128)(2,1)S(1)}, u32[]{:S(2)}, u32[]{:S(2)}) collective-permute-start(bf16[1024,384]{1,0:T(8,128)(2,1)S(1)} %get-tuple-element.37.refs_2_), channel_id=1, source_target_pairs={{0,8},{1,9},{2,10},{3,11},{4,12},{5,13},{6,14},{7,15},{8,16},{9,17... | collective-permute-start | bytes 2359304 | tf_op jit(solution)/shard_map/ppermute | solution.py:99
  8.1 1.5 %shard_map.110.refs_5_ = bf16[1024,384]{1,0:T(8,128)(2,1)S(1)} custom-call(bf16[1024,768]{1,0:T(8,128)(2,1)S(1)} %get-tuple-element.36.refs_0_, bf16[3,768,384]{2,1,0:T(8,128)(2,1)S(1)} %copy-done.2, bf16[1024,384]{1,0:T(8,128)(2,1)S(1)} %get-tuple-element.37.refs_2_), custom_call_target="tpu_custom_call" | custom-call | flops 8000000000 | tf_op jit(solution)/shard_map/pallas_call | solution.py:56
  9.6 2.1 %collective-permute-start.1 = (bf16[1024,384]{1,0:T(8,128)(2,1)S(1)}, bf16[1024,384]{1,0:T(8,128)(2,1)S(1)}, u32[]{:S(2)}, u32[]{:S(2)}) collective-permute-start(bf16[1024,384]{1,0:T(8,128)(2,1)S(1)} %shard_map.110.refs_5_), channel_id=1, source_target_pairs={{0,24},{1,25},{2,26},{3,27},{4,28},{5,29},{6,30},{7,31},{8,0},{9,1... | collective-permute-start | bytes 2359304 | tf_op jit(solution)/shard_map/ppermute | solution.py:99
  11.8 2.3 %shard_map.111 = (f32[1024,384]{1,0:T(8,128)S(1)}, f32[1024,384]{1,0:T(8,128)S(1)}) custom-call(bf16[1024,768]{1,0:T(8,128)(2,1)S(1)} %get-tuple-element.36.refs_0_, bf16[3,768,384]{2,1,0:T(8,128)(2,1)S(1)} %copy-done.2, f32[1,384]{1,0:T(1,128)S(1)} %reshape.19.refs_2_, bf16[1024,768]{1,0:T(8,128)(2,1)S(1)} %copy-done, bf16[384,768]{1,0:T(8,128)(2,1)S(1)} %copy-done.5, ...), custom_call_target="tpu_custom_call" | custom-call | tf_op jit(solution)/shard_map/pallas_call | solution.py:56
  14.0 14.5 %collective-permute-done.refs_2_ = bf16[1024,384]{1,0:T(8,128)(2,1)S(1)} collective-permute-done((bf16[1024,384]{1,0:T(8,128)(2,1)S(1)}, bf16[1024,384]{1,0:T(8,128)(2,1)S(1)}, u32[]{:S(2)}, u32[]{:S(2)}) %collective-permute-start) | collective-permute-done | bytes 786464 | tf_op jit(solution)/shard_map/ppermute | solution.py:99
  28.6 16.0 %collective-permute-done.1.refs_3_ = bf16[1024,384]{1,0:T(8,128)(2,1)S(1)} collective-permute-done((bf16[1024,384]{1,0:T(8,128)(2,1)S(1)}, bf16[1024,384]{1,0:T(8,128)(2,1)S(1)}, u32[]{:S(2)}, u32[]{:S(2)}) %collective-permute-start.1) | collective-permute-done | bytes 786464 | tf_op jit(solution)/shard_map/ppermute | solution.py:99
  44.5 0.3 shard_map.112
  44.9 1.8 %collective-permute-start.2 = (bf16[1024,128]{1,0:T(8,128)(2,1)S(1)}, bf16[1024,128]{1,0:T(8,128)(2,1)S(1)}, u32[]{:S(2)}, u32[]{:S(2)}) collective-permute-start(bf16[1024,128]{1,0:T(8,128)(2,1)S(1)} %get-tuple-element.42.refs_1_.refs_5_.refs_6_), channel_id=1, source_target_pairs={{0,24},{1,25},{2,26},{3,27},{4,28},{5,29},{6,30},{7,31},{8,0},{9,1... | collective-permute-start | bytes 786440 | tf_op jit(solution)/shard_map/ppermute | solution.py:99
  46.7 0.3 collective-permute-start.3
  47.0 0.7 shard_map.113
  47.6 3.6 %collective-permute-start.4 = (bf16[1024,256]{1,0:T(8,128)(2,1)S(1)}, bf16[1024,256]{1,0:T(8,128)(2,1)S(1)}, u32[]{:S(2)}, u32[]{:S(2)}) collective-permute-start(bf16[1024,256]{1,0:T(8,128)(2,1)S(1)} %get-tuple-element.43.refs_2_.refs_6_.refs_7_), channel_id=1, source_target_pairs={{0,24},{1,25},{2,26},{3,27},{4,28},{5,29},{6,30},{7,31},{8,0},{9,1... | collective-permute-start | bytes 1572872 | tf_op jit(solution)/shard_map/ppermute | solution.py:99
  51.2 0.4 shard_map.114.refs_2_.refs_7_
  51.6 2.2 %shard_map.115 = (f32[4,584,128]{2,1,0:T(8,128)S(1)}, bf16[4,592,128]{2,1,0:T(8,128)(2,1)S(1)}) custom-call(bf16[1024,768]{1,0:T(8,128)(2,1)S(1)} %get-tuple-element.36.refs_0_, bf16[1024,768]{1,0:T(8,128)(2,1)S(1)} %copy-done, f32[64,128]{1,0:T(8,128)S(1)} %shard_map.114.refs_2_.refs_7_, bf16[1024,128]{1,0:T(8,128)(2,1)S(1)} %get-tuple-element.40.refs_4_.refs_3_, ...), custom_call_target="tpu_custom_call" | custom-call | tf_op jit(solution)/shard_map/pallas_call | solution.py:56
  53.8 0.1 collective-permute-start.6
  53.9 3.3 %shard_map.116 = (bf16[1024,768]{1,0:T(8,128)(2,1)}, f32[1024,768]{1,0:T(8,128)S(1)}) custom-call(bf16[1024,768]{1,0:T(8,128)(2,1)S(1)} %copy-done.4, bf16[384,768]{1,0:T(8,128)(2,1)S(1)} %copy-done.5, f32[1,768]{1,0:T(1,128)S(1)} %reshape.18.refs_2_, bf16[3,768,384]{2,1,0:T(8,128)(2,1)S(1)} %copy-done.2, ...), custom_call_target="tpu_custom_call" | custom-call | flops 8000000000 | tf_op jit(solution)/shard_map/pallas_call | solution.py:56
  57.1 2.3 %collective-permute-done.2.refs_1_ = bf16[1024,128]{1,0:T(8,128)(2,1)S(1)} collective-permute-done((bf16[1024,128]{1,0:T(8,128)(2,1)S(1)}, bf16[1024,128]{1,0:T(8,128)(2,1)S(1)}, u32[]{:S(2)}, u32[]{:S(2)}) %collective-permute-start.2) | collective-permute-done | bytes 262176 | tf_op jit(solution)/shard_map/ppermute | solution.py:99
  59.4 0.6 collective-permute-done.3.refs_2_
  60.0 1.1 shard_map.117
  61.1 0.1 collective-permute-start.7
  61.2 1.5 %shard_map.118.refs_4_.refs_0_ = f32[1024,768]{1,0:T(8,128)S(1)} custom-call(f32[1024,768]{1,0:T(8,128)S(1)} %get-tuple-element.46.refs_3_.refs_0_, bf16[1024,128]{1,0:T(8,128)(2,1)S(1)} %collective-permute-done.2.refs_1_, bf16[1024,128]{1,0:T(8,128)(2,1)S(1)} %collective-permute-done.3.refs_2_, bf16[3,768,384]{2,1,0:T(8,128)(2,1)S(1)} %copy-done.2, ...), custom_call_target="tpu_custom_call" | custom-call | flops 8000000000 | tf_op jit(solution)/shard_map/pallas_call | solution.py:56
  62.7 0.2 shard_map.119
  62.9 1.6 %collective-permute-start.8 = (bf16[784,128]{1,0:T(8,128)(2,1)S(1)}, bf16[784,128]{1,0:T(8,128)(2,1)S(1)}, u32[]{:S(2)}, u32[]{:S(2)}) collective-permute-start(bf16[784,128]{1,0:T(8,128)(2,1)S(1)} %get-tuple-element.51), channel_id=1, source_target_pairs={{0,2},{1,3},{2,0},{3,1},{4,6},{5,7},{6,4},{7,5},{8,10},{9,11},{10,... | collective-permute-start | bytes 602120 | tf_op jit(solution)/shard_map/ppermute | solution.py:102
  64.5 1.5 %collective-permute-start.9 = (bf16[784,128]{1,0:T(8,128)(2,1)S(1)}, bf16[784,128]{1,0:T(8,128)(2,1)S(1)}, u32[]{:S(2)}, u32[]{:S(2)}) collective-permute-start(bf16[784,128]{1,0:T(8,128)(2,1)S(1)} %get-tuple-element.52), channel_id=1, source_target_pairs={{0,4},{1,5},{2,6},{3,7},{4,0},{5,1},{6,2},{7,3},{8,12},{9,13},{10,... | collective-permute-start | bytes 602120 | tf_op jit(solution)/shard_map/ppermute | solution.py:102
  66.0 0.5 collective-permute-start.10
  66.4 1.2 %shard_map.120.refs_4_.refs_5_ = f32[1024,768]{1,0:T(8,128)S(1)} custom-call(bf16[1024,768]{1,0:T(8,128)(2,1)S(1)} %copy-done.4, f32[776,128]{1,0:T(8,128)S(1)} %get-tuple-element.50.refs_1_.refs_0_), custom_call_target="tpu_custom_call" | custom-call | flops 8000000000 | tf_op jit(solution)/shard_map/pallas_call | solution.py:56
  67.7 2.6 %collective-permute-done.8.refs_1_ = bf16[784,128]{1,0:T(8,128)(2,1)S(1)} collective-permute-done((bf16[784,128]{1,0:T(8,128)(2,1)S(1)}, bf16[784,128]{1,0:T(8,128)(2,1)S(1)}, u32[]{:S(2)}, u32[]{:S(2)}) %collective-permute-start.8) | collective-permute-done | bytes 200736 | tf_op jit(solution)/shard_map/ppermute | solution.py:102
  70.3 2.0 %collective-permute-done.9.refs_2_ = bf16[784,128]{1,0:T(8,128)(2,1)S(1)} collective-permute-done((bf16[784,128]{1,0:T(8,128)(2,1)S(1)}, bf16[784,128]{1,0:T(8,128)(2,1)S(1)}, u32[]{:S(2)}, u32[]{:S(2)}) %collective-permute-start.9) | collective-permute-done | bytes 200736 | tf_op jit(solution)/shard_map/ppermute | solution.py:102
  72.3 3.5 %collective-permute-done.10.refs_3_ = bf16[784,128]{1,0:T(8,128)(2,1)S(1)} collective-permute-done((bf16[784,128]{1,0:T(8,128)(2,1)S(1)}, bf16[784,128]{1,0:T(8,128)(2,1)S(1)}, u32[]{:S(2)}, u32[]{:S(2)}) %collective-permute-start.10) | collective-permute-done | bytes 200736 | tf_op jit(solution)/shard_map/ppermute | solution.py:102
  75.8 0.1 shard_map.121.refs_3_.refs_0_
  75.9 1.6 %collective-permute-start.12 = (bf16[784,128]{1,0:T(8,128)(2,1)S(1)}, bf16[784,128]{1,0:T(8,128)(2,1)S(1)}, u32[]{:S(2)}, u32[]{:S(2)}) collective-permute-start(bf16[784,128]{1,0:T(8,128)(2,1)S(1)} %shard_map.121.refs_3_.refs_0_), channel_id=1, source_target_pairs={{0,8},{1,9},{2,10},{3,11},{4,12},{5,13},{6,14},{7,15},{8,0},{9,1},... | collective-permute-start | bytes 602120 | tf_op jit(solution)/shard_map/ppermute | solution.py:102
  77.5 4.2 %collective-permute-done.4.refs_1_ = bf16[1024,256]{1,0:T(8,128)(2,1)S(1)} collective-permute-done((bf16[1024,256]{1,0:T(8,128)(2,1)S(1)}, bf16[1024,256]{1,0:T(8,128)(2,1)S(1)}, u32[]{:S(2)}, u32[]{:S(2)}) %collective-permute-start.4) | collective-permute-done | bytes 524320 | tf_op jit(solution)/shard_map/ppermute | solution.py:99
  81.7 1.2 %shard_map.122 = (f32[4,384,128]{2,1,0:T(8,128)S(1)}, bf16[4,384,128]{2,1,0:T(8,128)(2,1)S(1)}) custom-call(bf16[1024,768]{1,0:T(8,128)(2,1)S(1)} %get-tuple-element.36.refs_0_, bf16[1024,256]{1,0:T(8,128)(2,1)S(1)} %collective-permute-done.4.refs_1_, bf16[1024,256]{1,0:T(8,128)(2,1)S(1)} %collective-permute-done.5.refs_2_, ...), custom_call_target="tpu_custom_call" | custom-call | flops 8000000000 | tf_op jit(solution)/shard_map/pallas_call | solution.py:56
  82.9 0.1 collective-permute-start.11
  83.0 2.6 %collective-permute-done.12.refs_1_ = bf16[784,128]{1,0:T(8,128)(2,1)S(1)} collective-permute-done((bf16[784,128]{1,0:T(8,128)(2,1)S(1)}, bf16[784,128]{1,0:T(8,128)(2,1)S(1)}, u32[]{:S(2)}, u32[]{:S(2)}) %collective-permute-start.12) | collective-permute-done | bytes 200736 | tf_op jit(solution)/shard_map/ppermute | solution.py:102
  85.6 0.1 shard_map.123.refs_2_.refs_0_
  85.6 0.1 collective-permute-start.17
  85.7 0.1 shard_map.124
  85.8 1.6 %collective-permute-start.13 = (bf16[384,128]{1,0:T(8,128)(2,1)S(1)}, bf16[384,128]{1,0:T(8,128)(2,1)S(1)}, u32[]{:S(2)}, u32[]{:S(2)}) collective-permute-start(bf16[384,128]{1,0:T(8,128)(2,1)S(1)} %get-tuple-element.57), channel_id=1, source_target_pairs={{0,2},{1,3},{2,0},{3,1},{4,6},{5,7},{6,4},{7,5},{8,10},{9,11},{10,... | collective-permute-start | bytes 294920 | tf_op jit(solution)/shard_map/ppermute | solution.py:102
  87.4 1.5 %collective-permute-start.14 = (bf16[384,128]{1,0:T(8,128)(2,1)S(1)}, bf16[384,128]{1,0:T(8,128)(2,1)S(1)}, u32[]{:S(2)}, u32[]{:S(2)}) collective-permute-start(bf16[384,128]{1,0:T(8,128)(2,1)S(1)} %get-tuple-element.58), channel_id=1, source_target_pairs={{0,4},{1,5},{2,6},{3,7},{4,0},{5,1},{6,2},{7,3},{8,12},{9,13},{10,... | collective-permute-start | bytes 294920 | tf_op jit(solution)/shard_map/ppermute | solution.py:102
  88.9 0.5 collective-permute-start.15
  89.4 1.1 collective-permute-done.13.refs_1_
  90.5 1.9 %collective-permute-done.14.refs_2_ = bf16[384,128]{1,0:T(8,128)(2,1)S(1)} collective-permute-done((bf16[384,128]{1,0:T(8,128)(2,1)S(1)}, bf16[384,128]{1,0:T(8,128)(2,1)S(1)}, u32[]{:S(2)}, u32[]{:S(2)}) %collective-permute-start.14) | collective-permute-done | bytes 98336 | tf_op jit(solution)/shard_map/ppermute | solution.py:102
  92.4 2.0 %collective-permute-done.15.refs_3_ = bf16[384,128]{1,0:T(8,128)(2,1)S(1)} collective-permute-done((bf16[384,128]{1,0:T(8,128)(2,1)S(1)}, bf16[384,128]{1,0:T(8,128)(2,1)S(1)}, u32[]{:S(2)}, u32[]{:S(2)}) %collective-permute-start.15) | collective-permute-done | bytes 98336 | tf_op jit(solution)/shard_map/ppermute | solution.py:102
  94.4 2.1 %collective-permute-start.16 = (bf16[384,128]{1,0:T(8,128)(2,1)S(1)}, bf16[384,128]{1,0:T(8,128)(2,1)S(1)}, u32[]{:S(2)}, u32[]{:S(2)}) collective-permute-start(bf16[384,128]{1,0:T(8,128)(2,1)S(1)} %shard_map.125.refs_2_.refs_0_), channel_id=1, source_target_pairs={{0,8},{1,9},{2,10},{3,11},{4,12},{5,13},{6,14},{7,15},{8,0},{9,1},... | collective-permute-start | bytes 294920 | tf_op jit(solution)/shard_map/ppermute | solution.py:102
  96.5 1.0 collective-permute-done.17.refs_1_
  97.6 1.4 %collective-permute-start.18 = (bf16[784,128]{1,0:T(8,128)(2,1)S(1)}, bf16[784,128]{1,0:T(8,128)(2,1)S(1)}, u32[]{:S(2)}, u32[]{:S(2)}) collective-permute-start(bf16[784,128]{1,0:T(8,128)(2,1)S(1)} %shard_map.126.refs_2_.refs_0_), channel_id=1, source_target_pairs={{0,2},{1,3},{2,0},{3,1},{4,6},{5,7},{6,4},{7,5},{8,10},{9,11},{10,... | collective-permute-start | bytes 602120 | tf_op jit(solution)/shard_map/ppermute | solution.py:102
  99.0 1.5 %collective-permute-start.19 = (bf16[784,128]{1,0:T(8,128)(2,1)S(1)}, bf16[784,128]{1,0:T(8,128)(2,1)S(1)}, u32[]{:S(2)}, u32[]{:S(2)}) collective-permute-start(bf16[784,128]{1,0:T(8,128)(2,1)S(1)} %shard_map.126.refs_2_.refs_0_), channel_id=1, source_target_pairs={{0,4},{1,5},{2,6},{3,7},{4,0},{5,1},{6,2},{7,3},{8,12},{9,13},{10,... | collective-permute-start | bytes 602120 | tf_op jit(solution)/shard_map/ppermute | solution.py:102
  100.4 0.7 collective-permute-start.20
  101.2 0.9 collective-permute-start.21
  102.1 2.8 %shard_map.128 = (bf16[1024,768]{1,0:T(8,128)(2,1)}, f32[8,128]{1,0:T(8,128)S(1)}) custom-call(f32[1024,768]{1,0:T(8,128)S(1)} %shard_map.118.refs_4_.refs_0_, bf16[1024,256]{1,0:T(8,128)(2,1)S(1)} %collective-permute-done.4.refs_1_, bf16[1024,256]{1,0:T(8,128)(2,1)S(1)} %collective-permute-done.5.refs_2_, bf16[3,768,384]{2,1,0:T(8,128)(2,1)S(1)} %copy-done.2, ...), custom_call_target="tpu_custom_call" | custom-call | flops 8000000000 | tf_op jit(solution)/shard_map/pallas_call | solution.py:56
  104.9 2.3 %collective-permute-done.21.refs_1_ = bf16[384,128]{1,0:T(8,128)(2,1)S(1)} collective-permute-done((bf16[384,128]{1,0:T(8,128)(2,1)S(1)}, bf16[384,128]{1,0:T(8,128)(2,1)S(1)}, u32[]{:S(2)}, u32[]{:S(2)}) %collective-permute-start.21) | collective-permute-done | bytes 98336 | tf_op jit(solution)/shard_map/ppermute | solution.py:102
  107.2 0.9 collective-permute-start.23
  108.2 1.5 %collective-permute-start.24 = (bf16[384,128]{1,0:T(8,128)(2,1)S(1)}, bf16[384,128]{1,0:T(8,128)(2,1)S(1)}, u32[]{:S(2)}, u32[]{:S(2)}) collective-permute-start(bf16[384,128]{1,0:T(8,128)(2,1)S(1)} %shard_map.129.refs_4_.refs_0_), channel_id=1, source_target_pairs={{0,4},{1,5},{2,6},{3,7},{4,0},{5,1},{6,2},{7,3},{8,12},{9,13},{10,... | collective-permute-start | bytes 294920 | tf_op jit(solution)/shard_map/ppermute | solution.py:102
  109.7 1.1 collective-permute-start.25
  110.8 0.1 shard_map.130.refs_4_.refs_0_
  110.9 0.1 collective-permute-start.22
  110.9 2.2 %collective-permute-done.23.refs_1_ = bf16[384,128]{1,0:T(8,128)(2,1)S(1)} collective-permute-done((bf16[384,128]{1,0:T(8,128)(2,1)S(1)}, bf16[384,128]{1,0:T(8,128)(2,1)S(1)}, u32[]{:S(2)}, u32[]{:S(2)}) %collective-permute-start.23) | collective-permute-done | bytes 98336 | tf_op jit(solution)/shard_map/ppermute | solution.py:102
  113.1 2.1 %collective-permute-done.25.refs_3_ = bf16[384,128]{1,0:T(8,128)(2,1)S(1)} collective-permute-done((bf16[384,128]{1,0:T(8,128)(2,1)S(1)}, bf16[384,128]{1,0:T(8,128)(2,1)S(1)}, u32[]{:S(2)}, u32[]{:S(2)}) %collective-permute-start.25) | collective-permute-done | bytes 98336 | tf_op jit(solution)/shard_map/ppermute | solution.py:102
  115.2 0.1 collective-permute-start.26
  115.3 2.5 %shard_map.132 = (f32[3,768,384]{2,1,0:T(8,128)}, f32[384,768]{1,0:T(8,128)}, f32[768]{0:T(1024)}, f32[384]{0:T(512)}) custom-call(bf16[4,784,128]{2,1,0:T(8,128)(2,1)S(1)} %shard_map.130.refs_4_.refs_0_, bf16[4,784,128]{2,1,0:T(8,128)(2,1)S(1)} %collective-permute-done.22.refs_1_, bf16[4,384,128]{2,1,0:T(8,128)(2,1)S(1)} %shard_map.131.refs_2_.refs_1_), custom_call_target="tpu_custom_call" | custom-call | tf_op jit(solution)/shard_map/pallas_call | solution.py:56
  117.8 1.3 %shard_map.133 = f32[3,768,384]{2,1,0:T(8,128)} custom-call(f32[3,768,384]{2,1,0:T(8,128)} %get-tuple-element.62.refs_0_, bf16[4,384,128]{2,1,0:T(8,128)(2,1)S(1)} %shard_map.131.refs_2_.refs_1_, bf16[4,384,128]{2,1,0:T(8,128)(2,1)S(1)} %collective-permute-done.26.refs_2_), custom_call_target="tpu_custom_call", output_to_operand_aliasing={{}: (0, {})} | custom-call | tf_op jit(solution)/shard_map/pallas_call | solution.py:56
  (33 shorter events, 0.2 us)
Async XLA Ops:
  0.6 1.5 %copy-start.1 = (bf16[3,768,384]{2,1,0:T(8,128)(2,1)S(1)}, bf16[3,768,384]{2,1,0:T(8,128)(2,1)}, u32[]{:S(2)}) copy-start(bf16[3,768,384]{2,1,0:T(8,128)(2,1)} %refs_3_.7) | copy-start | bytes 5308420
  2.1 1.4 %copy-start.3 = (bf16[1024,768]{1,0:T(8,128)(2,1)S(1)}, bf16[1024,768]{1,0:T(8,128)(2,1)}, u32[]{:S(2)}) copy-start(bf16[1024,768]{1,0:T(8,128)(2,1)} %refs_0_.7) | copy-start | bytes 4718596
  3.5 4.6 %copy-start.2 = (bf16[3,768,384]{2,1,0:T(8,128)(2,1)S(1)}, bf16[3,768,384]{2,1,0:T(8,128)(2,1)}, u32[]{:S(2)}) copy-start(bf16[3,768,384]{2,1,0:T(8,128)(2,1)} %refs_3_.7) | copy-start | bytes 5308420
  5.0 23.5 %collective-permute-start = (bf16[1024,384]{1,0:T(8,128)(2,1)S(1)}, bf16[1024,384]{1,0:T(8,128)(2,1)S(1)}, u32[]{:S(2)}, u32[]{:S(2)}) collective-permute-start(bf16[1024,384]{1,0:T(8,128)(2,1)S(1)} %get-tuple-element.37.refs_2_), channel_id=1, source_target_pairs={{0,8},{1,9},{2,10},{3,11},{4,12},{5,13},{6,14},{7,15},{8,16},{9,17... | collective-permute-start | bytes 2359304 | tf_op jit(solution)/shard_map/ppermute | solution.py:99
  8.1 3.6 %copy-start.6 = (f32[768]{0:T(1024)S(1)}, f32[768]{0:T(1024)}, u32[]{:S(2)}) copy-start(f32[768]{0:T(1024)} %param.10) | copy-start | bytes 9220
  8.1 3.6 %copy-start.7 = (f32[384]{0:T(512)S(1)}, f32[384]{0:T(512)}, u32[]{:S(2)}) copy-start(f32[384]{0:T(512)} %param.8) | copy-start | bytes 4612
  8.1 3.6 %copy-start = (bf16[1024,768]{1,0:T(8,128)(2,1)S(1)}, bf16[1024,768]{1,0:T(8,128)(2,1)}, u32[]{:S(2)}) copy-start(bf16[1024,768]{1,0:T(8,128)(2,1)} %refs_4_.3) | copy-start | bytes 4718596
  8.1 3.6 %copy-start.5 = (bf16[384,768]{1,0:T(8,128)(2,1)S(1)}, bf16[384,768]{1,0:T(8,128)(2,1)}, u32[]{:S(2)}) copy-start(bf16[384,768]{1,0:T(8,128)(2,1)} %refs_1_.9) | copy-start | bytes 1769476
  9.6 34.9 %collective-permute-start.1 = (bf16[1024,384]{1,0:T(8,128)(2,1)S(1)}, bf16[1024,384]{1,0:T(8,128)(2,1)S(1)}, u32[]{:S(2)}, u32[]{:S(2)}) collective-permute-start(bf16[1024,384]{1,0:T(8,128)(2,1)S(1)} %shard_map.110.refs_5_), channel_id=1, source_target_pairs={{0,24},{1,25},{2,26},{3,27},{4,28},{5,29},{6,30},{7,31},{8,0},{9,1... | collective-permute-start | bytes 2359304 | tf_op jit(solution)/shard_map/ppermute | solution.py:99
  44.9 14.5 %collective-permute-start.2 = (bf16[1024,128]{1,0:T(8,128)(2,1)S(1)}, bf16[1024,128]{1,0:T(8,128)(2,1)S(1)}, u32[]{:S(2)}, u32[]{:S(2)}) collective-permute-start(bf16[1024,128]{1,0:T(8,128)(2,1)S(1)} %get-tuple-element.42.refs_1_.refs_5_.refs_6_), channel_id=1, source_target_pairs={{0,24},{1,25},{2,26},{3,27},{4,28},{5,29},{6,30},{7,31},{8,0},{9,1... | collective-permute-start | bytes 786440 | tf_op jit(solution)/shard_map/ppermute | solution.py:99
  46.7 13.3 %collective-permute-start.3 = (bf16[1024,128]{1,0:T(8,128)(2,1)S(1)}, bf16[1024,128]{1,0:T(8,128)(2,1)S(1)}, u32[]{:S(2)}, u32[]{:S(2)}) collective-permute-start(bf16[1024,128]{1,0:T(8,128)(2,1)S(1)} %get-tuple-element.42.refs_1_.refs_5_.refs_6_), channel_id=1, source_target_pairs={{0,8},{1,9},{2,10},{3,11},{4,12},{5,13},{6,14},{7,15},{8,16},{9,17... | collective-permute-start | bytes 786440 | tf_op jit(solution)/shard_map/ppermute | solution.py:99
  47.6 34.1 %collective-permute-start.4 = (bf16[1024,256]{1,0:T(8,128)(2,1)S(1)}, bf16[1024,256]{1,0:T(8,128)(2,1)S(1)}, u32[]{:S(2)}, u32[]{:S(2)}) collective-permute-start(bf16[1024,256]{1,0:T(8,128)(2,1)S(1)} %get-tuple-element.43.refs_2_.refs_6_.refs_7_), channel_id=1, source_target_pairs={{0,24},{1,25},{2,26},{3,27},{4,28},{5,29},{6,30},{7,31},{8,0},{9,1... | collective-permute-start | bytes 1572872 | tf_op jit(solution)/shard_map/ppermute | solution.py:99
  51.2 30.5 %collective-permute-start.5 = (bf16[1024,256]{1,0:T(8,128)(2,1)S(1)}, bf16[1024,256]{1,0:T(8,128)(2,1)S(1)}, u32[]{:S(2)}, u32[]{:S(2)}) collective-permute-start(bf16[1024,256]{1,0:T(8,128)(2,1)S(1)} %get-tuple-element.43.refs_2_.refs_6_.refs_7_), channel_id=1, source_target_pairs={{0,8},{1,9},{2,10},{3,11},{4,12},{5,13},{6,14},{7,15},{8,16},{9,17... | collective-permute-start | bytes 1572872 | tf_op jit(solution)/shard_map/ppermute | solution.py:99
  51.6 2.3 %copy-start.4 = (bf16[1024,768]{1,0:T(8,128)(2,1)S(1)}, bf16[1024,768]{1,0:T(8,128)(2,1)}, u32[]{:S(2)}) copy-start(bf16[1024,768]{1,0:T(8,128)(2,1)} %refs_0_.7) | copy-start | bytes 4718596
  53.8 8.9 %collective-permute-start.6 = (bf16[4,592,128]{2,1,0:T(8,128)(2,1)S(1)}, bf16[4,592,128]{2,1,0:T(8,128)(2,1)S(1)}, u32[]{:S(2)}, u32[]{:S(2)}) collective-permute-start(bf16[4,592,128]{2,1,0:T(8,128)(2,1)S(1)} %get-tuple-element.48), channel_id=1, source_target_pairs={{0,1},{1,0},{2,3},{3,2},{4,5},{5,4},{6,7},{7,6},{8,9},{9,8},{10,11... | collective-permute-start | bytes 1818632 | tf_op jit(solution)/shard_map/ppermute | solution.py:102
  61.1 1.6 %collective-permute-start.7 = (bf16[4,192,128]{2,1,0:T(8,128)(2,1)S(1)}, bf16[4,192,128]{2,1,0:T(8,128)(2,1)S(1)}, u32[]{:S(2)}, u32[]{:S(2)}) collective-permute-start(bf16[4,192,128]{2,1,0:T(8,128)(2,1)S(1)} %get-tuple-element.49), channel_id=1, source_target_pairs={{0,1},{1,0},{2,3},{3,2},{4,5},{5,4},{6,7},{7,6},{8,9},{9,8},{10,11... | collective-permute-start | bytes 589832 | tf_op jit(solution)/shard_map/ppermute | solution.py:102
  62.9 7.5 %collective-permute-start.8 = (bf16[784,128]{1,0:T(8,128)(2,1)S(1)}, bf16[784,128]{1,0:T(8,128)(2,1)S(1)}, u32[]{:S(2)}, u32[]{:S(2)}) collective-permute-start(bf16[784,128]{1,0:T(8,128)(2,1)S(1)} %get-tuple-element.51), channel_id=1, source_target_pairs={{0,2},{1,3},{2,0},{3,1},{4,6},{5,7},{6,4},{7,5},{8,10},{9,11},{10,... | collective-permute-start | bytes 602120 | tf_op jit(solution)/shard_map/ppermute | solution.py:102
  64.5 7.8 %collective-permute-start.9 = (bf16[784,128]{1,0:T(8,128)(2,1)S(1)}, bf16[784,128]{1,0:T(8,128)(2,1)S(1)}, u32[]{:S(2)}, u32[]{:S(2)}) collective-permute-start(bf16[784,128]{1,0:T(8,128)(2,1)S(1)} %get-tuple-element.52), channel_id=1, source_target_pairs={{0,4},{1,5},{2,6},{3,7},{4,0},{5,1},{6,2},{7,3},{8,12},{9,13},{10,... | collective-permute-start | bytes 602120 | tf_op jit(solution)/shard_map/ppermute | solution.py:102
  66.0 9.9 %collective-permute-start.10 = (bf16[784,128]{1,0:T(8,128)(2,1)S(1)}, bf16[784,128]{1,0:T(8,128)(2,1)S(1)}, u32[]{:S(2)}, u32[]{:S(2)}) collective-permute-start(bf16[784,128]{1,0:T(8,128)(2,1)S(1)} %get-tuple-element.53), channel_id=1, source_target_pairs={{0,6},{1,7},{2,4},{3,5},{4,2},{5,3},{6,0},{7,1},{8,14},{9,15},{10,... | collective-permute-start | bytes 602120 | tf_op jit(solution)/shard_map/ppermute | solution.py:102
  75.9 9.6 %collective-permute-start.12 = (bf16[784,128]{1,0:T(8,128)(2,1)S(1)}, bf16[784,128]{1,0:T(8,128)(2,1)S(1)}, u32[]{:S(2)}, u32[]{:S(2)}) collective-permute-start(bf16[784,128]{1,0:T(8,128)(2,1)S(1)} %shard_map.121.refs_3_.refs_0_), channel_id=1, source_target_pairs={{0,8},{1,9},{2,10},{3,11},{4,12},{5,13},{6,14},{7,15},{8,0},{9,1},... | collective-permute-start | bytes 602120 | tf_op jit(solution)/shard_map/ppermute | solution.py:102
  82.9 2.8 %collective-permute-start.11 = (bf16[4,384,128]{2,1,0:T(8,128)(2,1)S(1)}, bf16[4,384,128]{2,1,0:T(8,128)(2,1)S(1)}, u32[]{:S(2)}, u32[]{:S(2)}) collective-permute-start(bf16[4,384,128]{2,1,0:T(8,128)(2,1)S(1)} %get-tuple-element.55), channel_id=1, source_target_pairs={{0,1},{1,0},{2,3},{3,2},{4,5},{5,4},{6,7},{7,6},{8,9},{9,8},{10,11... | collective-permute-start | bytes 1179656 | tf_op jit(solution)/shard_map/ppermute | solution.py:102
  85.6 11.9 %collective-permute-start.17 = (bf16[784,128]{1,0:T(8,128)(2,1)S(1)}, bf16[784,128]{1,0:T(8,128)(2,1)S(1)}, u32[]{:S(2)}, u32[]{:S(2)}) collective-permute-start(bf16[784,128]{1,0:T(8,128)(2,1)S(1)} %shard_map.123.refs_2_.refs_0_), channel_id=1, source_target_pairs={{0,16},{1,17},{2,18},{3,19},{4,20},{5,21},{6,22},{7,23},{8,24},{9,... | collective-permute-start | bytes 602120 | tf_op jit(solution)/shard_map/ppermute | solution.py:102
  85.8 4.7 %collective-permute-start.13 = (bf16[384,128]{1,0:T(8,128)(2,1)S(1)}, bf16[384,128]{1,0:T(8,128)(2,1)S(1)}, u32[]{:S(2)}, u32[]{:S(2)}) collective-permute-start(bf16[384,128]{1,0:T(8,128)(2,1)S(1)} %get-tuple-element.57), channel_id=1, source_target_pairs={{0,2},{1,3},{2,0},{3,1},{4,6},{5,7},{6,4},{7,5},{8,10},{9,11},{10,... | collective-permute-start | bytes 294920 | tf_op jit(solution)/shard_map/ppermute | solution.py:102
  87.4 5.0 %collective-permute-start.14 = (bf16[384,128]{1,0:T(8,128)(2,1)S(1)}, bf16[384,128]{1,0:T(8,128)(2,1)S(1)}, u32[]{:S(2)}, u32[]{:S(2)}) collective-permute-start(bf16[384,128]{1,0:T(8,128)(2,1)S(1)} %get-tuple-element.58), channel_id=1, source_target_pairs={{0,4},{1,5},{2,6},{3,7},{4,0},{5,1},{6,2},{7,3},{8,12},{9,13},{10,... | collective-permute-start | bytes 294920 | tf_op jit(solution)/shard_map/ppermute | solution.py:102
  88.9 5.5 %collective-permute-start.15 = (bf16[384,128]{1,0:T(8,128)(2,1)S(1)}, bf16[384,128]{1,0:T(8,128)(2,1)S(1)}, u32[]{:S(2)}, u32[]{:S(2)}) collective-permute-start(bf16[384,128]{1,0:T(8,128)(2,1)S(1)} %get-tuple-element.59), channel_id=1, source_target_pairs={{0,6},{1,7},{2,4},{3,5},{4,2},{5,3},{6,0},{7,1},{8,14},{9,15},{10,... | collective-permute-start | bytes 294920 | tf_op jit(solution)/shard_map/ppermute | solution.py:102
  94.4 6.7 %collective-permute-start.16 = (bf16[384,128]{1,0:T(8,128)(2,1)S(1)}, bf16[384,128]{1,0:T(8,128)(2,1)S(1)}, u32[]{:S(2)}, u32[]{:S(2)}) collective-permute-start(bf16[384,128]{1,0:T(8,128)(2,1)S(1)} %shard_map.125.refs_2_.refs_0_), channel_id=1, source_target_pairs={{0,8},{1,9},{2,10},{3,11},{4,12},{5,13},{6,14},{7,15},{8,0},{9,1},... | collective-permute-start | bytes 294920 | tf_op jit(solution)/shard_map/ppermute | solution.py:102
  97.6 12.1 %collective-permute-start.18 = (bf16[784,128]{1,0:T(8,128)(2,1)S(1)}, bf16[784,128]{1,0:T(8,128)(2,1)S(1)}, u32[]{:S(2)}, u32[]{:S(2)}) collective-permute-start(bf16[784,128]{1,0:T(8,128)(2,1)S(1)} %shard_map.126.refs_2_.refs_0_), channel_id=1, source_target_pairs={{0,2},{1,3},{2,0},{3,1},{4,6},{5,7},{6,4},{7,5},{8,10},{9,11},{10,... | collective-permute-start | bytes 602120 | tf_op jit(solution)/shard_map/ppermute | solution.py:102
  99.0 11.8 %collective-permute-start.19 = (bf16[784,128]{1,0:T(8,128)(2,1)S(1)}, bf16[784,128]{1,0:T(8,128)(2,1)S(1)}, u32[]{:S(2)}, u32[]{:S(2)}) collective-permute-start(bf16[784,128]{1,0:T(8,128)(2,1)S(1)} %shard_map.126.refs_2_.refs_0_), channel_id=1, source_target_pairs={{0,4},{1,5},{2,6},{3,7},{4,0},{5,1},{6,2},{7,3},{8,12},{9,13},{10,... | collective-permute-start | bytes 602120 | tf_op jit(solution)/shard_map/ppermute | solution.py:102
  100.4 10.4 %collective-permute-start.20 = (bf16[784,128]{1,0:T(8,128)(2,1)S(1)}, bf16[784,128]{1,0:T(8,128)(2,1)S(1)}, u32[]{:S(2)}, u32[]{:S(2)}) collective-permute-start(bf16[784,128]{1,0:T(8,128)(2,1)S(1)} %shard_map.126.refs_2_.refs_0_), channel_id=1, source_target_pairs={{0,6},{1,7},{2,4},{3,5},{4,2},{5,3},{6,0},{7,1},{8,14},{9,15},{10,... | collective-permute-start | bytes 602120 | tf_op jit(solution)/shard_map/ppermute | solution.py:102
  101.2 6.0 %collective-permute-start.21 = (bf16[384,128]{1,0:T(8,128)(2,1)S(1)}, bf16[384,128]{1,0:T(8,128)(2,1)S(1)}, u32[]{:S(2)}, u32[]{:S(2)}) collective-permute-start(bf16[384,128]{1,0:T(8,128)(2,1)S(1)} %shard_map.127.refs_6_.refs_0_), channel_id=1, source_target_pairs={{0,16},{1,17},{2,18},{3,19},{4,20},{5,21},{6,22},{7,23},{8,24},{9,... | collective-permute-start | bytes 294920 | tf_op jit(solution)/shard_map/ppermute | solution.py:102
  107.2 5.9 %collective-permute-start.23 = (bf16[384,128]{1,0:T(8,128)(2,1)S(1)}, bf16[384,128]{1,0:T(8,128)(2,1)S(1)}, u32[]{:S(2)}, u32[]{:S(2)}) collective-permute-start(bf16[384,128]{1,0:T(8,128)(2,1)S(1)} %shard_map.129.refs_4_.refs_0_), channel_id=1, source_target_pairs={{0,2},{1,3},{2,0},{3,1},{4,6},{5,7},{6,4},{7,5},{8,10},{9,11},{10,... | collective-permute-start | bytes 294920 | tf_op jit(solution)/shard_map/ppermute | solution.py:102
  108.2 4.9 %collective-permute-start.24 = (bf16[384,128]{1,0:T(8,128)(2,1)S(1)}, bf16[384,128]{1,0:T(8,128)(2,1)S(1)}, u32[]{:S(2)}, u32[]{:S(2)}) collective-permute-start(bf16[384,128]{1,0:T(8,128)(2,1)S(1)} %shard_map.129.refs_4_.refs_0_), channel_id=1, source_target_pairs={{0,4},{1,5},{2,6},{3,7},{4,0},{5,1},{6,2},{7,3},{8,12},{9,13},{10,... | collective-permute-start | bytes 294920 | tf_op jit(solution)/shard_map/ppermute | solution.py:102
  109.7 5.5 %collective-permute-start.25 = (bf16[384,128]{1,0:T(8,128)(2,1)S(1)}, bf16[384,128]{1,0:T(8,128)(2,1)S(1)}, u32[]{:S(2)}, u32[]{:S(2)}) collective-permute-start(bf16[384,128]{1,0:T(8,128)(2,1)S(1)} %shard_map.129.refs_4_.refs_0_), channel_id=1, source_target_pairs={{0,6},{1,7},{2,4},{3,5},{4,2},{5,3},{6,0},{7,1},{8,14},{9,15},{10,... | collective-permute-start | bytes 294920 | tf_op jit(solution)/shard_map/ppermute | solution.py:102
  110.9 4.4 %collective-permute-start.22 = (bf16[4,784,128]{2,1,0:T(8,128)(2,1)S(1)}, bf16[4,784,128]{2,1,0:T(8,128)(2,1)S(1)}, u32[]{:S(2)}, u32[]{:S(2)}) collective-permute-start(bf16[4,784,128]{2,1,0:T(8,128)(2,1)S(1)} %shard_map.130.refs_4_.refs_0_), channel_id=1, source_target_pairs={{0,1},{1,0},{2,3},{3,2},{4,5},{5,4},{6,7},{7,6},{8,9},{9,8},{10,11... | collective-permute-start | bytes 2408456 | tf_op jit(solution)/shard_map/ppermute | solution.py:102
  115.2 2.6 %collective-permute-start.26 = (bf16[4,384,128]{2,1,0:T(8,128)(2,1)S(1)}, bf16[4,384,128]{2,1,0:T(8,128)(2,1)S(1)}, u32[]{:S(2)}, u32[]{:S(2)}) collective-permute-start(bf16[4,384,128]{2,1,0:T(8,128)(2,1)S(1)} %shard_map.131.refs_2_.refs_1_), channel_id=1, source_target_pairs={{0,1},{1,0},{2,3},{3,2},{4,5},{5,4},{6,7},{7,6},{8,9},{9,8},{10,11... | collective-permute-start | bytes 1179656 | tf_op jit(solution)/shard_map/ppermute | solution.py:102
